TPU v7x, 256 devices: a whole 4x4x8 slice. The times are simulated.
256 devices in a mesh: dp: 64 (over z, y, core), mp: 4 (over x).
Axes of the slice: x: 4, y: 4, z: 8, core: 2. Of those that a mesh axis runs over, the one named last changes fastest.
Arguments:
- gradient: bfloat16 [2048, 16384], P('dp', 'mp')
- block_owner: int32 [4, 32], replicated, may hold values from 0 to 63, as said below
- prev_left: float32 [4, 64, 2, 512, 512], P('mp', 'dp'), as said below
- prev_right: float32 [4, 64, 2, 512, 512], P('mp', 'dp'), as said below
Outputs:
- update_out: bfloat16 [2048, 16384], P('dp', 'mp')
- new_left: float32 [4, 64, 2, 512, 512], P('mp', 'dp')
- new_right: float32 [4, 64, 2, 512, 512], P('mp', 'dp')
Inputs may be any that keep to these rules, and one draw needn't show every extreme that they name: `block_owner`: within each column shard of 8 column blocks, each owner holds at most 2 blocks, and some owner holds exactly 2; no owner holds two blocks of the same row block of one column shard. `prev_left`: each slot is symmetric positive definite. `prev_right`: each slot is symmetric positive definite.
All inputs are finite; a program needn't handle non-finite values.
Results may differ from a plain program's by a relative error of at most 0.001.
Values may be sent and summed in bfloat16 or wider, within the bound.
No kernel may reach another device: no remote copies, remote signals or barrier semaphores. Data moves between devices by JAX's collectives and lax.ppermute only.
A program may use at most 128 MiB of HBM per device.

v0:
```python
import jax
import jax.numpy as jnp
from jax import lax
from jax.experimental import pallas as pl
from jax.experimental.pallas import tpu as pltpu
from jax.sharding import PartitionSpec as P

EPS_DAMP = 1.0
BETA = 0.95
BLOCK = 512
GROUPS = 4
MEMBERS = 16
PER_SHARD = 8
OWNERS = 64
SLOTS = 2
ROWS_DEV = 32
PIECE = 128
CELLS = 2048 * 16384

WHOLE = pl.BlockSpec(memory_space=pltpu.VMEM)
SMEM = pl.BlockSpec(memory_space=pltpu.SMEM)


def rank_table(owner_ref, where_ref, count_ref, place_ref):
    base = where_ref[0] * PER_SHARD

    def clear(o, _):
        count_ref[o] = 0
        return 0

    lax.fori_loop(0, OWNERS, clear, 0)

    def step(b, _):
        owner = owner_ref[b // PER_SHARD, base + b % PER_SHARD]
        slot = count_ref[owner]
        count_ref[owner] = slot + 1
        place_ref[b] = owner * SLOTS + slot
        return 0

    lax.fori_loop(0, GROUPS * PER_SHARD, step, 0)


def spread_kernel(where_ref, grad_ref, *out_refs):
    group = where_ref[1]
    for shift in range(GROUPS):
        chunk = lax.rem(group + shift, GROUPS)
        for j in range(PER_SHARD):
            columns = pl.ds(pl.multiple_of(j * BLOCK + chunk * PIECE, PIECE), PIECE)
            out_refs[shift][j] = grad_ref[:, columns]


def route_kernel(where_ref, owner_ref, *refs):
    in_refs, (out_ref, count_ref, place_ref) = refs[:GROUPS], refs[GROUPS:]
    rank_table(owner_ref, where_ref, count_ref, place_ref)
    group = where_ref[1]
    for shift in range(GROUPS):
        row = lax.rem(group + GROUPS - shift, GROUPS)
        for j in range(PER_SHARD):
            out_ref[place_ref[row * PER_SHARD + j]] = in_refs[shift][j]


def collect_kernel(where_ref, owner_ref, in_ref, *refs):
    out_refs, (count_ref, place_ref) = refs[:GROUPS], refs[GROUPS:]
    rank_table(owner_ref, where_ref, count_ref, place_ref)
    group = where_ref[1]
    for shift in range(GROUPS):
        row = lax.rem(group + shift, GROUPS)
        for j in range(PER_SHARD):
            out_refs[shift][j] = in_ref[place_ref[row * PER_SHARD + j]]


def place_kernel(where_ref, *refs):
    in_refs, out_ref = refs[:GROUPS], refs[GROUPS]
    group = where_ref[1]
    for shift in range(GROUPS):
        chunk = lax.rem(group + GROUPS - shift, GROUPS)
        for j in range(PER_SHARD):
            columns = pl.ds(pl.multiple_of(j * BLOCK + chunk * PIECE, PIECE), PIECE)
            out_ref[:, columns] = in_refs[shift][j]


def dot(a, b):
    return jnp.dot(a, b, preferred_element_type=jnp.float32)


def split(x):
    high = x.astype(jnp.bfloat16)
    return high, (x - high.astype(jnp.float32)).astype(jnp.bfloat16)


def dot3(a, b):
    return dot(a[0], b[0]) + (dot(a[0], b[1]) + dot(a[1], b[0]))


def root(stat, eye):
    damped = stat + EPS_DAMP * eye
    total = jnp.sum(damped * damped, keepdims=True)
    norm = jnp.sqrt(total)
    n = damped * (1.0 / norm)
    n_split = split(n)
    n2 = dot3(n_split, n_split)
    q = split(1.5625 * eye - 2.5 * n + n2)
    h = split(1.25 * n - n2)
    r = split(dot3(q, q))
    product = 1.5625 * eye - 1.25 * n - dot3(h, r)
    return product * lax.rsqrt(jnp.sqrt(0.25 * norm))


def owner_kernel(where_ref, owner_ref, got_ref, left_ref, right_ref, new_left_ref, new_right_ref,
                 raw_ref, sums_ref, block_ref):
    slot = pl.program_id(0)
    base = where_ref[0] * PER_SHARD
    me = where_ref[2]

    def step(b, held):
        return held + jnp.where(owner_ref[b // PER_SHARD, base + b % PER_SHARD] == me, 1, 0)

    held = lax.fori_loop(0, GROUPS * PER_SHARD, step, jnp.int32(0))
    used = held > slot
    for chunk in range(GROUPS):
        for member in range(MEMBERS):
            piece = got_ref[chunk * MEMBERS + member, 0]
            block_ref[pl.ds(member * ROWS_DEV, ROWS_DEV), pl.ds(chunk * PIECE, PIECE)] = jnp.where(
                used, piece, jnp.zeros_like(piece)
            )
    block = block_ref[...]
    turned = block.T
    rows = lax.broadcasted_iota(jnp.int32, (BLOCK, BLOCK), 0)
    columns = lax.broadcasted_iota(jnp.int32, (BLOCK, BLOCK), 1)
    eye = jnp.where(rows == columns, 1.0, 0.0).astype(jnp.float32)
    left = BETA * left_ref[0] + dot(block, turned)
    new_left_ref[0] = left
    right = BETA * right_ref[0] + dot(turned, block)
    new_right_ref[0] = right
    left_root = split(root(left, eye))
    half = split(dot(left_root[0], block) + dot(left_root[1], block))
    raw = dot3(half, split(root(right, eye)))
    raw_ref[0] = raw
    wide = block.astype(jnp.float32)
    grad_sq = jnp.sum(wide * wide, keepdims=True)
    update_sq = jnp.sum(raw * raw, keepdims=True)
    line = lax.broadcasted_iota(jnp.int32, (8, 128), 0)
    sums = jnp.where(line == 0, grad_sq, update_sq)

    @pl.when(slot == 0)
    def _():
        sums_ref[...] = sums

    @pl.when(slot > 0)
    def _():
        sums_ref[...] += sums


def scale_kernel(sums_ref, raw_ref, out_ref):
    grad_total = sums_ref[0:1, 0:1]
    update_total = sums_ref[1:2, 0:1]
    graft = jnp.sqrt(grad_total / CELLS) * lax.rsqrt(update_total / CELLS + 1e-06)
    for chunk in range(GROUPS):
        for member in range(MEMBERS):
            for slot in range(SLOTS):
                piece = raw_ref[slot, pl.ds(member * ROWS_DEV, ROWS_DEV), pl.ds(chunk * PIECE, PIECE)]
                out_ref[(chunk * MEMBERS + member) * SLOTS + slot] = (piece * graft).astype(jnp.bfloat16)


def between_groups(arrays):
    moved = [arrays[0]]
    for shift in range(1, GROUPS):
        pairs = [(d, (d + shift * MEMBERS) % OWNERS) for d in range(OWNERS)]
        moved.append(lax.ppermute(arrays[shift], "dp", pairs))
    return moved


def sum_everywhere(x):
    stages = [
        ("mp", [[(d, (d + s) % 4) for d in range(4)] for s in (1, 2, 3)]),
        ("dp", [[(d, d // 8 * 8 + (d + s) % 8) for d in range(OWNERS)] for s in (2, 4, 6)]),
        ("dp", [[(d, d ^ s) for d in range(OWNERS)] for s in (8, 16, 24)]),
        ("dp", [[(d, d ^ s) for d in range(OWNERS)] for s in (1, 32, 33)]),
    ]
    for axis, perms in stages:
        got = [lax.ppermute(x, axis, perm) for perm in perms]
        x = (x + got[0]) + (got[1] + got[2])
    return x


def shards(gradient, block_owner, prev_left, prev_right):
    my_index = lax.axis_index("dp")
    where = jnp.stack([lax.axis_index("mp"), my_index // MEMBERS, my_index]).astype(jnp.int32)
    piece_set = jax.ShapeDtypeStruct((PER_SHARD, ROWS_DEV, PIECE), jnp.bfloat16)
    rank_scratch = [pltpu.SMEM((OWNERS,), jnp.int32), pltpu.SMEM((GROUPS * PER_SHARD,), jnp.int32)]
    routed_shape = (OWNERS * SLOTS, ROWS_DEV, PIECE)

    pieces = pl.pallas_call(
        spread_kernel,
        out_shape=[piece_set] * GROUPS,
        in_specs=[SMEM, WHOLE],
        out_specs=[WHOLE] * GROUPS,
        name="spread",
    )(where, gradient)
    pieces = between_groups(pieces)
    routed = pl.pallas_call(
        route_kernel,
        out_shape=jax.ShapeDtypeStruct(routed_shape, jnp.bfloat16),
        in_specs=[SMEM, SMEM] + [WHOLE] * GROUPS,
        out_specs=WHOLE,
        scratch_shapes=rank_scratch,
        name="route",
    )(where, block_owner, *pieces)
    got = lax.all_to_all(
        routed.reshape(OWNERS, SLOTS, ROWS_DEV, PIECE), "dp", split_axis=0, concat_axis=0, tiled=True
    )

    stat_spec = pl.BlockSpec((1, BLOCK, BLOCK), lambda k: (k, 0, 0))
    stat_shape = jax.ShapeDtypeStruct((SLOTS, BLOCK, BLOCK), jnp.float32)
    new_left, new_right, raw, sums = pl.pallas_call(
        owner_kernel,
        grid=(SLOTS,),
        out_shape=[stat_shape, stat_shape, stat_shape, jax.ShapeDtypeStruct((8, 128), jnp.float32)],
        in_specs=[
            SMEM,
            SMEM,
            pl.BlockSpec((OWNERS, 1, ROWS_DEV, PIECE), lambda k: (0, k, 0, 0)),
            stat_spec,
            stat_spec,
        ],
        out_specs=[stat_spec, stat_spec, stat_spec, pl.BlockSpec((8, 128), lambda k: (0, 0))],
        scratch_shapes=[pltpu.VMEM((BLOCK, BLOCK), jnp.bfloat16)],
        compiler_params=pltpu.CompilerParams(vmem_limit_bytes=48 * 1024 * 1024),
        cost_estimate=pl.CostEstimate(
            flops=50 * 2 * BLOCK**3, bytes_accessed=12 * 1024 * 1024, transcendentals=0
        ),
        name="owner",
    )(where, block_owner, got, prev_left[0, 0], prev_right[0, 0])

    totals = sum_everywhere(sums)
    sending = pl.pallas_call(
        scale_kernel,
        out_shape=jax.ShapeDtypeStruct(routed_shape, jnp.bfloat16),
        in_specs=[WHOLE, WHOLE],
        out_specs=WHOLE,
        name="scale",
    )(totals, raw)
    returned = lax.all_to_all(
        sending.reshape(OWNERS, SLOTS, ROWS_DEV, PIECE), "dp", split_axis=0, concat_axis=0, tiled=True
    )
    back = pl.pallas_call(
        collect_kernel,
        out_shape=[piece_set] * GROUPS,
        in_specs=[SMEM, SMEM, WHOLE],
        out_specs=[WHOLE] * GROUPS,
        scratch_shapes=rank_scratch,
        name="collect",
    )(where, block_owner, returned.reshape(routed_shape))
    back = between_groups(back)
    update_out = pl.pallas_call(
        place_kernel,
        out_shape=jax.ShapeDtypeStruct(gradient.shape, jnp.bfloat16),
        in_specs=[SMEM] + [WHOLE] * GROUPS,
        out_specs=WHOLE,
        name="place",
    )(where, *back)
    return (update_out, new_left[None, None], new_right[None, None])


def solution(mesh):
    in_specs = (
        P("dp", "mp"),
        P(),
        P("mp", "dp", None, None, None),
        P("mp", "dp", None, None, None),
    )
    out_specs = (P("dp", "mp"), P("mp", "dp", None, None, None), P("mp", "dp", None, None, None))
    return jax.shard_map(shards, mesh=mesh, in_specs=in_specs, out_specs=out_specs, check_vma=False)
```

profile of v0, /device:TPU:8, one launch (start us, length us, event | category | flops | bytes accessed | tf_op | source)
XLA Modules:
  0.0 169.2 jit_solution(9211606020801420465)
XLA Ops:
  0.6 0.0 copy-start.2
  0.7 0.7 pad_add_fusion.where_ref
  1.3 1.7 %spread.1 = (bf16[8,32,128]{2,1,0:T(8,128)(2,1)}, bf16[8,32,128]{2,1,0:T(8,128)(2,1)}, bf16[8,32,128]{2,1,0:T(8,128)(2,1)}, bf16[8,32,128]{2,1,0:T(8,128)(2,1)}) custom-call(s32[3]{0:T(128)} %pad_add_fusion.where_ref, bf16[32,4096]{1,0:T(8,128)(2,1)} %grad_ref.1), custom_call_target="tpu_custom_call" | custom-call | tf_op jit(solution)/shard_map/spread/pallas_call | solution.py:193
  3.0 3.3 %collective-permute-start = (bf16[8,32,128]{2,1,0:T(8,128)(2,1)}, bf16[8,32,128]{2,1,0:T(8,128)(2,1)S(1)}, u32[]{:S(2)}, u32[]{:S(2)}) collective-permute-start(bf16[8,32,128]{2,1,0:T(8,128)(2,1)} %get-tuple-element.16), channel_id=1, source_target_pairs={{0,64},{4,68},{8,72},{12,76},{16,80},{20,84},{24,88},{28,92},{32,9... | collective-permute-start | bytes 196616 | tf_op jit(solution)/shard_map/ppermute | solution.py:169
  6.3 5.4 %collective-permute-start.1 = (bf16[8,32,128]{2,1,0:T(8,128)(2,1)}, bf16[8,32,128]{2,1,0:T(8,128)(2,1)S(1)}, u32[]{:S(2)}, u32[]{:S(2)}) collective-permute-start(bf16[8,32,128]{2,1,0:T(8,128)(2,1)} %get-tuple-element.17), channel_id=1, source_target_pairs={{0,128},{4,132},{8,136},{12,140},{16,144},{20,148},{24,152},{28,15... | collective-permute-start | bytes 196616 | tf_op jit(solution)/shard_map/ppermute | solution.py:169
  11.7 2.7 %collective-permute-start.2 = (bf16[8,32,128]{2,1,0:T(8,128)(2,1)}, bf16[8,32,128]{2,1,0:T(8,128)(2,1)S(1)}, u32[]{:S(2)}, u32[]{:S(2)}) collective-permute-start(bf16[8,32,128]{2,1,0:T(8,128)(2,1)} %get-tuple-element.18), channel_id=1, source_target_pairs={{0,192},{4,196},{8,200},{12,204},{16,208},{20,212},{24,216},{28,22... | collective-permute-start | bytes 196616 | tf_op jit(solution)/shard_map/ppermute | solution.py:169
  14.4 0.0 collective-permute-done.refs_1_
  14.4 1.7 collective-permute-done.1.refs_2_
  16.0 2.8 %collective-permute-done.2.refs_3_ = bf16[8,32,128]{2,1,0:T(8,128)(2,1)S(1)} collective-permute-done((bf16[8,32,128]{2,1,0:T(8,128)(2,1)}, bf16[8,32,128]{2,1,0:T(8,128)(2,1)S(1)}, u32[]{:S(2)}, u32[]{:S(2)}) %collective-permute-start.2) | collective-permute-done | bytes 65568 | tf_op jit(solution)/shard_map/ppermute | solution.py:169
  18.8 0.6 copy-done.9
  19.4 2.9 %route.1 = bf16[128,32,128]{2,1,0:T(8,128)(2,1)} custom-call(s32[3]{0:T(128)} %pad_add_fusion.where_ref, s32[4,32]{1,0:T(4,128)} %owner_ref.5, bf16[8,32,128]{2,1,0:T(8,128)(2,1)} %get-tuple-element.15.refs_0_, bf16[8,32,128]{2,1,0:T(8,128)(2,1)} %copy-done.5, bf16[8,32,128]{2,1,0:T(8,128)(2,1)} %copy-done.7, bf16[8,32,128]{2,1,0:T(8,128)(2,1)} %copy-done.9), custom_call_target="tpu_custom_call" | custom-call | tf_op jit(solution)/shard_map/route/pallas_call | solution.py:201
  22.3 37.6 %all_to_all.10.got_ref = bf16[64,2,32,128]{3,2,1,0:T(8,128)(2,1)S(1)} all-to-all(bf16[64,2,32,128]{3,2,1,0:T(8,128)(2,1)} %bitcast.12), channel_id=1, replica_groups=mesh['dp'=64,'mp'=4] {'dp'}, dimensions={0} | all-to-all | bytes 2097152 | tf_op jit(solution)/shard_map/all_to_all | solution.py:209
  59.9 20.1 %owner.1 = (f32[2,512,512]{2,1,0:T(8,128)}, f32[2,512,512]{2,1,0:T(8,128)}, f32[2,512,512]{2,1,0:T(8,128)S(1)}, f32[8,128]{1,0:T(8,128)S(1)}) custom-call(s32[3]{0:T(128)S(1)} %copy-done.1, s32[4,32]{1,0:T(4,128)S(1)} %copy-done.2, bf16[64,2,32,128]{3,2,1,0:T(8,128)(2,1)S(1)} %all_to_all.10.got_ref, f32[2,512,512]{2,1,0:T(8,128)S(1)} %bitcast.10, ...), custom_call_target="tpu_custom_call" | custom-call | flops 13421772800 | bytes 12582912 | tf_op jit(solution)/shard_map/owner/pallas_call | solution.py:215
  80.0 1.4 copy-done
  81.4 2.8 %collective-permute-start.5 = (f32[8,128]{1,0:T(8,128)S(1)}, f32[8,128]{1,0:T(8,128)S(1)}, u32[]{:S(2)}, u32[]{:S(2)}) collective-permute-start(f32[8,128]{1,0:T(8,128)S(1)} %get-tuple-element.19), channel_id=1, source_target_pairs={{0,3},{1,0},{2,1},{3,2},{4,7},{5,4},{6,5},{7,6},{8,11},{9,8},{10,9... | collective-permute-start | bytes 12296 | tf_op jit(solution)/shard_map/ppermute | solution.py:181
  84.1 0.8 collective-permute-start.4
  84.9 0.9 collective-permute-start.3
  85.8 0.0 collective-permute-done.5
  85.8 3.4 %collective-permute-done.4 = f32[8,128]{1,0:T(8,128)S(1)} collective-permute-done((f32[8,128]{1,0:T(8,128)S(1)}, f32[8,128]{1,0:T(8,128)S(1)}, u32[]{:S(2)}, u32[]{:S(2)}) %collective-permute-start.4) | collective-permute-done | bytes 4128 | tf_op jit(solution)/shard_map/ppermute | solution.py:181
  89.3 0.5 collective-permute-done.3
  89.8 0.6 collective-permute-start.8
  90.3 2.4 %collective-permute-start.7 = (f32[8,128]{1,0:T(8,128)S(1)}, f32[8,128]{1,0:T(8,128)S(1)}, u32[]{:S(2)}, u32[]{:S(2)}) collective-permute-start(f32[8,128]{1,0:T(8,128)S(1)} %add_add_fusion.3), channel_id=1, source_target_pairs={{0,16},{4,20},{8,24},{12,28},{16,0},{20,4},{24,8},{28,12},{32,48},... | collective-permute-start | bytes 12296 | tf_op jit(solution)/shard_map/ppermute | solution.py:181
  92.7 1.8 %collective-permute-start.6 = (f32[8,128]{1,0:T(8,128)S(1)}, f32[8,128]{1,0:T(8,128)S(1)}, u32[]{:S(2)}, u32[]{:S(2)}) collective-permute-start(f32[8,128]{1,0:T(8,128)S(1)} %add_add_fusion.3), channel_id=1, source_target_pairs={{0,8},{4,12},{8,16},{12,20},{16,24},{20,28},{24,0},{28,4},{32,40},... | collective-permute-start | bytes 12296 | tf_op jit(solution)/shard_map/ppermute | solution.py:181
  94.5 0.9 collective-permute-done.7
  95.4 0.9 collective-permute-done.6
  96.3 1.9 %collective-permute-start.11 = (f32[8,128]{1,0:T(8,128)S(1)}, f32[8,128]{1,0:T(8,128)S(1)}, u32[]{:S(2)}, u32[]{:S(2)}) collective-permute-start(f32[8,128]{1,0:T(8,128)S(1)} %add_add_fusion.2), channel_id=1, source_target_pairs={{0,96},{4,100},{8,104},{12,108},{16,112},{20,116},{24,120},{28,124... | collective-permute-start | bytes 12296 | tf_op jit(solution)/shard_map/ppermute | solution.py:181
  98.2 0.2 collective-permute-start.10
  98.4 2.3 %collective-permute-start.9 = (f32[8,128]{1,0:T(8,128)S(1)}, f32[8,128]{1,0:T(8,128)S(1)}, u32[]{:S(2)}, u32[]{:S(2)}) collective-permute-start(f32[8,128]{1,0:T(8,128)S(1)} %add_add_fusion.2), channel_id=1, source_target_pairs={{0,32},{4,36},{8,40},{12,44},{16,48},{20,52},{24,56},{28,60},{32,0... | collective-permute-start | bytes 12296 | tf_op jit(solution)/shard_map/ppermute | solution.py:181
  100.7 1.0 collective-permute-done.11
  101.7 1.0 collective-permute-done.10
  102.7 0.1 collective-permute-start.14
  102.8 1.8 %collective-permute-start.13 = (f32[8,128]{1,0:T(8,128)S(1)}, f32[8,128]{1,0:T(8,128)S(1)}, u32[]{:S(2)}, u32[]{:S(2)}) collective-permute-start(f32[8,128]{1,0:T(8,128)S(1)} %add_add_fusion.1), channel_id=1, source_target_pairs={{0,128},{4,132},{8,136},{12,140},{16,144},{20,148},{24,152},{28,15... | collective-permute-start | bytes 12296 | tf_op jit(solution)/shard_map/ppermute | solution.py:181
  104.7 3.9 %collective-permute-start.12 = (f32[8,128]{1,0:T(8,128)S(1)}, f32[8,128]{1,0:T(8,128)S(1)}, u32[]{:S(2)}, u32[]{:S(2)}) collective-permute-start(f32[8,128]{1,0:T(8,128)S(1)} %add_add_fusion.1), channel_id=1, source_target_pairs={{0,4},{4,0},{8,12},{12,8},{16,20},{20,16},{24,28},{28,24},{32,36},... | collective-permute-start | bytes 12296 | tf_op jit(solution)/shard_map/ppermute | solution.py:181
  108.6 1.2 collective-permute-done.14
  109.8 0.7 collective-permute-done.13
  110.4 0.0 collective-permute-done.12
  110.4 0.6 add_add_fusion.sums_ref
  111.0 2.8 %scale.1 = bf16[128,32,128]{2,1,0:T(8,128)(2,1)} custom-call(f32[8,128]{1,0:T(8,128)} %add_add_fusion.sums_ref, f32[2,512,512]{2,1,0:T(8,128)} %copy-done), custom_call_target="tpu_custom_call" | custom-call | tf_op jit(solution)/shard_map/scale/pallas_call | solution.py:236
  113.9 38.5 %all_to_all.11 = bf16[64,2,32,128]{3,2,1,0:T(8,128)(2,1)} all-to-all(bf16[64,2,32,128]{3,2,1,0:T(8,128)(2,1)} %bitcast.13), channel_id=1, replica_groups=mesh['dp'=64,'mp'=4] {'dp'}, dimensions={0} | all-to-all | bytes 2097152 | tf_op jit(solution)/shard_map/all_to_all | solution.py:243
  152.3 2.9 %collect.1 = (bf16[8,32,128]{2,1,0:T(8,128)(2,1)}, bf16[8,32,128]{2,1,0:T(8,128)(2,1)}, bf16[8,32,128]{2,1,0:T(8,128)(2,1)}, bf16[8,32,128]{2,1,0:T(8,128)(2,1)}) custom-call(s32[3]{0:T(128)} %pad_add_fusion.where_ref, s32[4,32]{1,0:T(4,128)} %owner_ref.5, bf16[128,32,128]{2,1,0:T(8,128)(2,1)} %bitcast.11), custom_call_target="tpu_custom_call" | custom-call | tf_op jit(solution)/shard_map/collect/pallas_call | solution.py:246
  155.2 1.0 collective-permute-start.15
  156.2 2.2 %collective-permute-start.16 = (bf16[8,32,128]{2,1,0:T(8,128)(2,1)}, bf16[8,32,128]{2,1,0:T(8,128)(2,1)S(1)}, u32[]{:S(2)}, u32[]{:S(2)}) collective-permute-start(bf16[8,32,128]{2,1,0:T(8,128)(2,1)} %get-tuple-element.23), channel_id=1, source_target_pairs={{0,128},{4,132},{8,136},{12,140},{16,144},{20,148},{24,152},{28,15... | collective-permute-start | bytes 196616 | tf_op jit(solution)/shard_map/ppermute | solution.py:169
  158.5 2.0 %collective-permute-start.17 = (bf16[8,32,128]{2,1,0:T(8,128)(2,1)}, bf16[8,32,128]{2,1,0:T(8,128)(2,1)S(1)}, u32[]{:S(2)}, u32[]{:S(2)}) collective-permute-start(bf16[8,32,128]{2,1,0:T(8,128)(2,1)} %get-tuple-element.24), channel_id=1, source_target_pairs={{0,192},{4,196},{8,200},{12,204},{16,208},{20,212},{24,216},{28,22... | collective-permute-start | bytes 196616 | tf_op jit(solution)/shard_map/ppermute | solution.py:169
  160.5 1.7 %collective-permute-done.15.refs_1_ = bf16[8,32,128]{2,1,0:T(8,128)(2,1)S(1)} collective-permute-done((bf16[8,32,128]{2,1,0:T(8,128)(2,1)}, bf16[8,32,128]{2,1,0:T(8,128)(2,1)S(1)}, u32[]{:S(2)}, u32[]{:S(2)}) %collective-permute-start.15) | collective-permute-done | bytes 65568 | tf_op jit(solution)/shard_map/ppermute | solution.py:169
  162.2 2.7 %collective-permute-done.16.refs_2_ = bf16[8,32,128]{2,1,0:T(8,128)(2,1)S(1)} collective-permute-done((bf16[8,32,128]{2,1,0:T(8,128)(2,1)}, bf16[8,32,128]{2,1,0:T(8,128)(2,1)S(1)}, u32[]{:S(2)}, u32[]{:S(2)}) %collective-permute-start.16) | collective-permute-done | bytes 65568 | tf_op jit(solution)/shard_map/ppermute | solution.py:169
  164.9 2.0 %collective-permute-done.17.refs_3_ = bf16[8,32,128]{2,1,0:T(8,128)(2,1)S(1)} collective-permute-done((bf16[8,32,128]{2,1,0:T(8,128)(2,1)}, bf16[8,32,128]{2,1,0:T(8,128)(2,1)S(1)}, u32[]{:S(2)}, u32[]{:S(2)}) %collective-permute-start.17) | collective-permute-done | bytes 65568 | tf_op jit(solution)/shard_map/ppermute | solution.py:169
  166.9 0.6 copy-done.8
  167.5 1.7 %place.1 = bf16[32,4096]{1,0:T(8,128)(2,1)} custom-call(s32[3]{0:T(128)} %pad_add_fusion.where_ref, bf16[8,32,128]{2,1,0:T(8,128)(2,1)} %get-tuple-element.21.refs_0_, bf16[8,32,128]{2,1,0:T(8,128)(2,1)} %copy-done.4, bf16[8,32,128]{2,1,0:T(8,128)(2,1)} %copy-done.6, bf16[8,32,128]{2,1,0:T(8,128)(2,1)} %copy-done.8), custom_call_target="tpu_custom_call" | custom-call | tf_op jit(solution)/shard_map/place/pallas_call | solution.py:255
  (21 shorter events, 0.1 us)
Async XLA Ops:
  0.6 59.3 %copy-start.2 = (s32[4,32]{1,0:T(4,128)S(1)}, s32[4,32]{1,0:T(4,128)}, u32[]{:S(2)}) copy-start(s32[4,32]{1,0:T(4,128)} %owner_ref.5) | copy-start | bytes 1540
  0.6 59.3 %copy-start.3 = (f32[1,1,2,512,512]{4,3,2,1,0:T(8,128)S(1)}, f32[1,1,2,512,512]{4,3,2,1,0:T(8,128)}, u32[]{:S(2)}) copy-start(f32[1,1,2,512,512]{4,3,2,1,0:T(8,128)} %param.6) | copy-start | bytes 6291460
  1.3 58.6 %copy-start.1 = (s32[3]{0:T(128)S(1)}, s32[3]{0:T(128)}, u32[]{:S(2)}) copy-start(s32[3]{0:T(128)} %pad_add_fusion.where_ref) | copy-start | bytes 40
  3.0 11.3 %collective-permute-start = (bf16[8,32,128]{2,1,0:T(8,128)(2,1)}, bf16[8,32,128]{2,1,0:T(8,128)(2,1)S(1)}, u32[]{:S(2)}, u32[]{:S(2)}) collective-permute-start(bf16[8,32,128]{2,1,0:T(8,128)(2,1)} %get-tuple-element.16), channel_id=1, source_target_pairs={{0,64},{4,68},{8,72},{12,76},{16,80},{20,84},{24,88},{28,92},{32,9... | collective-permute-start | bytes 196616 | tf_op jit(solution)/shard_map/ppermute | solution.py:169
  6.3 9.7 %collective-permute-start.1 = (bf16[8,32,128]{2,1,0:T(8,128)(2,1)}, bf16[8,32,128]{2,1,0:T(8,128)(2,1)S(1)}, u32[]{:S(2)}, u32[]{:S(2)}) collective-permute-start(bf16[8,32,128]{2,1,0:T(8,128)(2,1)} %get-tuple-element.17), channel_id=1, source_target_pairs={{0,128},{4,132},{8,136},{12,140},{16,144},{20,148},{24,152},{28,15... | collective-permute-start | bytes 196616 | tf_op jit(solution)/shard_map/ppermute | solution.py:169
  11.7 7.1 %collective-permute-start.2 = (bf16[8,32,128]{2,1,0:T(8,128)(2,1)}, bf16[8,32,128]{2,1,0:T(8,128)(2,1)S(1)}, u32[]{:S(2)}, u32[]{:S(2)}) collective-permute-start(bf16[8,32,128]{2,1,0:T(8,128)(2,1)} %get-tuple-element.18), channel_id=1, source_target_pairs={{0,192},{4,196},{8,200},{12,204},{16,208},{20,212},{24,216},{28,22... | collective-permute-start | bytes 196616 | tf_op jit(solution)/shard_map/ppermute | solution.py:169
  14.4 4.5 %copy-start.5 = (bf16[8,32,128]{2,1,0:T(8,128)(2,1)}, bf16[8,32,128]{2,1,0:T(8,128)(2,1)S(1)}, u32[]{:S(2)}) copy-start(bf16[8,32,128]{2,1,0:T(8,128)(2,1)S(1)} %collective-permute-done.refs_1_) | copy-start | bytes 196612
  16.0 2.8 %copy-start.7 = (bf16[8,32,128]{2,1,0:T(8,128)(2,1)}, bf16[8,32,128]{2,1,0:T(8,128)(2,1)S(1)}, u32[]{:S(2)}) copy-start(bf16[8,32,128]{2,1,0:T(8,128)(2,1)S(1)} %collective-permute-done.1.refs_2_) | copy-start | bytes 196612
  18.8 0.6 copy-start.9
  80.0 1.4 copy-start
  81.4 4.4 %collective-permute-start.5 = (f32[8,128]{1,0:T(8,128)S(1)}, f32[8,128]{1,0:T(8,128)S(1)}, u32[]{:S(2)}, u32[]{:S(2)}) collective-permute-start(f32[8,128]{1,0:T(8,128)S(1)} %get-tuple-element.19), channel_id=1, source_target_pairs={{0,3},{1,0},{2,1},{3,2},{4,7},{5,4},{6,5},{7,6},{8,11},{9,8},{10,9... | collective-permute-start | bytes 12296 | tf_op jit(solution)/shard_map/ppermute | solution.py:181
  84.1 5.1 %collective-permute-start.4 = (f32[8,128]{1,0:T(8,128)S(1)}, f32[8,128]{1,0:T(8,128)S(1)}, u32[]{:S(2)}, u32[]{:S(2)}) collective-permute-start(f32[8,128]{1,0:T(8,128)S(1)} %get-tuple-element.19), channel_id=1, source_target_pairs={{0,2},{1,3},{2,0},{3,1},{4,6},{5,7},{6,4},{7,5},{8,10},{9,11},{10,... | collective-permute-start | bytes 12296 | tf_op jit(solution)/shard_map/ppermute | solution.py:181
  84.9 4.8 %collective-permute-start.3 = (f32[8,128]{1,0:T(8,128)S(1)}, f32[8,128]{1,0:T(8,128)S(1)}, u32[]{:S(2)}, u32[]{:S(2)}) collective-permute-start(f32[8,128]{1,0:T(8,128)S(1)} %get-tuple-element.19), channel_id=1, source_target_pairs={{0,1},{1,2},{2,3},{3,0},{4,5},{5,6},{6,7},{7,4},{8,9},{9,10},{10,1... | collective-permute-start | bytes 12296 | tf_op jit(solution)/shard_map/ppermute | solution.py:181
  89.8 4.7 %collective-permute-start.8 = (f32[8,128]{1,0:T(8,128)S(1)}, f32[8,128]{1,0:T(8,128)S(1)}, u32[]{:S(2)}, u32[]{:S(2)}) collective-permute-start(f32[8,128]{1,0:T(8,128)S(1)} %add_add_fusion.3), channel_id=1, source_target_pairs={{0,24},{4,28},{8,0},{12,4},{16,8},{20,12},{24,16},{28,20},{32,56},... | collective-permute-start | bytes 12296 | tf_op jit(solution)/shard_map/ppermute | solution.py:181
  90.3 5.1 %collective-permute-start.7 = (f32[8,128]{1,0:T(8,128)S(1)}, f32[8,128]{1,0:T(8,128)S(1)}, u32[]{:S(2)}, u32[]{:S(2)}) collective-permute-start(f32[8,128]{1,0:T(8,128)S(1)} %add_add_fusion.3), channel_id=1, source_target_pairs={{0,16},{4,20},{8,24},{12,28},{16,0},{20,4},{24,8},{28,12},{32,48},... | collective-permute-start | bytes 12296 | tf_op jit(solution)/shard_map/ppermute | solution.py:181
  92.7 3.6 %collective-permute-start.6 = (f32[8,128]{1,0:T(8,128)S(1)}, f32[8,128]{1,0:T(8,128)S(1)}, u32[]{:S(2)}, u32[]{:S(2)}) collective-permute-start(f32[8,128]{1,0:T(8,128)S(1)} %add_add_fusion.3), channel_id=1, source_target_pairs={{0,8},{4,12},{8,16},{12,20},{16,24},{20,28},{24,0},{28,4},{32,40},... | collective-permute-start | bytes 12296 | tf_op jit(solution)/shard_map/ppermute | solution.py:181
  96.3 5.4 %collective-permute-start.11 = (f32[8,128]{1,0:T(8,128)S(1)}, f32[8,128]{1,0:T(8,128)S(1)}, u32[]{:S(2)}, u32[]{:S(2)}) collective-permute-start(f32[8,128]{1,0:T(8,128)S(1)} %add_add_fusion.2), channel_id=1, source_target_pairs={{0,96},{4,100},{8,104},{12,108},{16,112},{20,116},{24,120},{28,124... | collective-permute-start | bytes 12296 | tf_op jit(solution)/shard_map/ppermute | solution.py:181
  98.2 4.5 %collective-permute-start.10 = (f32[8,128]{1,0:T(8,128)S(1)}, f32[8,128]{1,0:T(8,128)S(1)}, u32[]{:S(2)}, u32[]{:S(2)}) collective-permute-start(f32[8,128]{1,0:T(8,128)S(1)} %add_add_fusion.2), channel_id=1, source_target_pairs={{0,64},{4,68},{8,72},{12,76},{16,80},{20,84},{24,88},{28,92},{32,9... | collective-permute-start | bytes 12296 | tf_op jit(solution)/shard_map/ppermute | solution.py:181
  98.4 4.3 %collective-permute-start.9 = (f32[8,128]{1,0:T(8,128)S(1)}, f32[8,128]{1,0:T(8,128)S(1)}, u32[]{:S(2)}, u32[]{:S(2)}) collective-permute-start(f32[8,128]{1,0:T(8,128)S(1)} %add_add_fusion.2), channel_id=1, source_target_pairs={{0,32},{4,36},{8,40},{12,44},{16,48},{20,52},{24,56},{28,60},{32,0... | collective-permute-start | bytes 12296 | tf_op jit(solution)/shard_map/ppermute | solution.py:181
  102.7 7.0 %collective-permute-start.14 = (f32[8,128]{1,0:T(8,128)S(1)}, f32[8,128]{1,0:T(8,128)S(1)}, u32[]{:S(2)}, u32[]{:S(2)}) collective-permute-start(f32[8,128]{1,0:T(8,128)S(1)} %add_add_fusion.1), channel_id=1, source_target_pairs={{0,132},{4,128},{8,140},{12,136},{16,148},{20,144},{24,156},{28,15... | collective-permute-start | bytes 12296 | tf_op jit(solution)/shard_map/ppermute | solution.py:181
  102.8 7.6 %collective-permute-start.13 = (f32[8,128]{1,0:T(8,128)S(1)}, f32[8,128]{1,0:T(8,128)S(1)}, u32[]{:S(2)}, u32[]{:S(2)}) collective-permute-start(f32[8,128]{1,0:T(8,128)S(1)} %add_add_fusion.1), channel_id=1, source_target_pairs={{0,128},{4,132},{8,136},{12,140},{16,144},{20,148},{24,152},{28,15... | collective-permute-start | bytes 12296 | tf_op jit(solution)/shard_map/ppermute | solution.py:181
  104.7 5.8 %collective-permute-start.12 = (f32[8,128]{1,0:T(8,128)S(1)}, f32[8,128]{1,0:T(8,128)S(1)}, u32[]{:S(2)}, u32[]{:S(2)}) collective-permute-start(f32[8,128]{1,0:T(8,128)S(1)} %add_add_fusion.1), channel_id=1, source_target_pairs={{0,4},{4,0},{8,12},{12,8},{16,20},{20,16},{24,28},{28,24},{32,36},... | collective-permute-start | bytes 12296 | tf_op jit(solution)/shard_map/ppermute | solution.py:181
  155.2 7.0 %collective-permute-start.15 = (bf16[8,32,128]{2,1,0:T(8,128)(2,1)}, bf16[8,32,128]{2,1,0:T(8,128)(2,1)S(1)}, u32[]{:S(2)}, u32[]{:S(2)}) collective-permute-start(bf16[8,32,128]{2,1,0:T(8,128)(2,1)} %get-tuple-element.22), channel_id=1, source_target_pairs={{0,64},{4,68},{8,72},{12,76},{16,80},{20,84},{24,88},{28,92},{32,9... | collective-permute-start | bytes 196616 | tf_op jit(solution)/shard_map/ppermute | solution.py:169
  156.2 8.6 %collective-permute-start.16 = (bf16[8,32,128]{2,1,0:T(8,128)(2,1)}, bf16[8,32,128]{2,1,0:T(8,128)(2,1)S(1)}, u32[]{:S(2)}, u32[]{:S(2)}) collective-permute-start(bf16[8,32,128]{2,1,0:T(8,128)(2,1)} %get-tuple-element.23), channel_id=1, source_target_pairs={{0,128},{4,132},{8,136},{12,140},{16,144},{20,148},{24,152},{28,15... | collective-permute-start | bytes 196616 | tf_op jit(solution)/shard_map/ppermute | solution.py:169
  158.5 8.4 %collective-permute-start.17 = (bf16[8,32,128]{2,1,0:T(8,128)(2,1)}, bf16[8,32,128]{2,1,0:T(8,128)(2,1)S(1)}, u32[]{:S(2)}, u32[]{:S(2)}) collective-permute-start(bf16[8,32,128]{2,1,0:T(8,128)(2,1)} %get-tuple-element.24), channel_id=1, source_target_pairs={{0,192},{4,196},{8,200},{12,204},{16,208},{20,212},{24,216},{28,22... | collective-permute-start | bytes 196616 | tf_op jit(solution)/shard_map/ppermute | solution.py:169
  162.2 4.7 %copy-start.4 = (bf16[8,32,128]{2,1,0:T(8,128)(2,1)}, bf16[8,32,128]{2,1,0:T(8,128)(2,1)S(1)}, u32[]{:S(2)}) copy-start(bf16[8,32,128]{2,1,0:T(8,128)(2,1)S(1)} %collective-permute-done.15.refs_1_) | copy-start | bytes 196612
  164.9 2.0 %copy-start.6 = (bf16[8,32,128]{2,1,0:T(8,128)(2,1)}, bf16[8,32,128]{2,1,0:T(8,128)(2,1)S(1)}, u32[]{:S(2)}) copy-start(bf16[8,32,128]{2,1,0:T(8,128)(2,1)S(1)} %collective-permute-done.16.refs_2_) | copy-start | bytes 196612
  166.9 0.6 copy-start.8
where the time goes:
time: 172 us; the launch traced here: 169 us
  blocking collectives  76.1 us (44%)
  starting transfers between devices  36 us (21%)
  Pallas kernels  32.1 us (19%)
  waiting for transfers between devices  20.5 us (12%)
  local copies, waits for them, and re-layouts  2.62 us (2%)
    all_to_all x1, blocking collectives, shards(): lax.all_to_all(sending.reshape(OWNERS, SLOTS, ROWS_DEV, PIECE), 'dp', spl...  38.5 us
    all_to_all x1, blocking collectives, shards(): lax.all_to_all(routed.reshape(OWNERS, SLOTS, ROWS_DEV, PIECE), 'dp', spli...  37.6 us
    pallas_call x1, Pallas kernels, shards(): pl.pallas_call(owner_kernel, grid=(SLOTS,), out_shape=[stat_shape, stat_s...  20.1 us
    ppermute x12, starting transfers between devices, sum_everywhere(): got = [lax.ppermute(x, axis, perm) for perm in perms]  19.4 us
    ppermute x6, starting transfers between devices, between_groups(): moved.append(lax.ppermute(arrays[shift], 'dp', pairs))  16.6 us
    ppermute x6, waiting for transfers between devices, between_groups(): moved.append(lax.ppermute(arrays[shift], 'dp', pairs))  10.8 us
    ppermute x12, waiting for transfers between devices, sum_everywhere(): got = [lax.ppermute(x, axis, perm) for perm in perms]  9.62 us
  transfers between devices with their start and end apart: 18, of which 13 were waited for; matrix products, arithmetic and copies ran while one was open for 0% of the time, Pallas kernels for 0%

commit v1 on v0

v1 whole, which is shorter than its diff:
```python
import jax
import jax.numpy as jnp
from jax import lax
from jax.experimental import pallas as pl
from jax.experimental.pallas import tpu as pltpu
from jax.sharding import Mesh
from jax.sharding import PartitionSpec as P

EPS_DAMP = 1.0
BETA = 0.95
BLOCK = 512
SHARDS = 4
GROUPS = 4
MEMBERS = 16
PER_SHARD = 8
OWNERS = 64
SLOTS = 2
ROWS_DEV = 32
PIECE = 128
CELLS = 2048 * 16384

WHOLE = pl.BlockSpec(memory_space=pltpu.VMEM)
SMEM = pl.BlockSpec(memory_space=pltpu.SMEM)


def place_table_kernel(shard_ref, owner_ref, place_ref, count_ref):
    base = shard_ref[0] * PER_SHARD

    def clear(o, _):
        count_ref[o] = 0
        return 0

    lax.fori_loop(0, OWNERS, clear, 0, unroll=8)
    for b in range(GROUPS * PER_SHARD):
        owner = owner_ref[b // PER_SHARD, base + b % PER_SHARD]
        slot = count_ref[owner]
        count_ref[owner] = slot + 1
        place_ref[b] = owner * SLOTS + slot


def spread_kernel(grad_ref, out_ref):
    for chunk in range(GROUPS):
        for j in range(PER_SHARD):
            out_ref[chunk, j] = grad_ref[:, pl.ds(j * BLOCK + chunk * PIECE, PIECE)]


def route_kernel(place_ref, in_ref, out_ref):
    for row in range(GROUPS):
        for j in range(PER_SHARD):
            out_ref[place_ref[row * PER_SHARD + j]] = in_ref[row, j]


def collect_kernel(place_ref, in_ref, out_ref):
    for row in range(GROUPS):
        for j in range(PER_SHARD):
            out_ref[row, j] = in_ref[place_ref[row * PER_SHARD + j]]


def place_kernel(in_ref, out_ref):
    for chunk in range(GROUPS):
        for j in range(PER_SHARD):
            out_ref[:, pl.ds(j * BLOCK + chunk * PIECE, PIECE)] = in_ref[chunk, j]


def dot(a, b):
    return jnp.dot(a, b, preferred_element_type=jnp.float32)


def split(x):
    high = x.astype(jnp.bfloat16)
    return high, (x - high.astype(jnp.float32)).astype(jnp.bfloat16)


def dot3(a, b):
    return dot(a[0], b[0]) + (dot(a[0], b[1]) + dot(a[1], b[0]))


def root(stat, eye):
    damped = stat + EPS_DAMP * eye
    total = jnp.sum(damped * damped, keepdims=True)
    norm = jnp.sqrt(total)
    n = damped * (1.0 / norm)
    n_split = split(n)
    n2 = dot3(n_split, n_split)
    q = split(1.5625 * eye - 2.5 * n + n2)
    h = split(1.25 * n - n2)
    r = split(dot3(q, q))
    product = 1.5625 * eye - 1.25 * n - dot3(h, r)
    return product * lax.rsqrt(jnp.sqrt(0.25 * norm))


def owner_kernel(me_ref, place_ref, got_ref, left_ref, right_ref, new_left_ref, new_right_ref,
                 raw_ref, sums_ref, block_ref):
    slot = pl.program_id(0)
    wanted = me_ref[0] * SLOTS + slot
    used = place_ref[0] == wanted
    for b in range(1, GROUPS * PER_SHARD):
        used = used | (place_ref[b] == wanted)
    for chunk in range(GROUPS):
        for member in range(MEMBERS):
            piece = got_ref[chunk * MEMBERS + member, 0]
            block_ref[pl.ds(member * ROWS_DEV, ROWS_DEV), pl.ds(chunk * PIECE, PIECE)] = jnp.where(
                used, piece, jnp.zeros_like(piece)
            )
    block = block_ref[...]
    turned = block.T
    rows = lax.broadcasted_iota(jnp.int32, (BLOCK, BLOCK), 0)
    columns = lax.broadcasted_iota(jnp.int32, (BLOCK, BLOCK), 1)
    eye = jnp.where(rows == columns, 1.0, 0.0).astype(jnp.float32)
    left = BETA * left_ref[0] + dot(block, turned)
    new_left_ref[0] = left
    right = BETA * right_ref[0] + dot(turned, block)
    new_right_ref[0] = right
    left_root = split(root(left, eye))
    half = split(dot(left_root[0], block) + dot(left_root[1], block))
    raw = dot3(half, split(root(right, eye)))
    raw_ref[0] = raw
    wide = block.astype(jnp.float32)
    grad_sq = jnp.sum(wide * wide, keepdims=True)
    update_sq = jnp.sum(raw * raw, keepdims=True)
    line = lax.broadcasted_iota(jnp.int32, (GROUPS * SHARDS, 8, 128), 1)
    sums = jnp.where(line == 0, grad_sq[None], update_sq[None])

    @pl.when(slot == 0)
    def _():
        sums_ref[...] = sums

    @pl.when(slot > 0)
    def _():
        sums_ref[...] += sums


def scale_kernel(sums_ref, raw_ref, out_ref):
    totals = jnp.sum(sums_ref[...], axis=0)
    grad_total = totals[0:1, 0:1]
    update_total = totals[1:2, 0:1]
    graft = jnp.sqrt(grad_total / CELLS) * lax.rsqrt(update_total / CELLS + 1e-06)
    for chunk in range(GROUPS):
        for member in range(MEMBERS):
            for slot in range(SLOTS):
                piece = raw_ref[slot, pl.ds(member * ROWS_DEV, ROWS_DEV), pl.ds(chunk * PIECE, PIECE)]
                out_ref[(chunk * MEMBERS + member) * SLOTS + slot] = (piece * graft).astype(jnp.bfloat16)


def exchange(x, axes):
    return lax.all_to_all(x, axes, split_axis=0, concat_axis=0, tiled=True)


def shards(gradient, block_owner, prev_left, prev_right):
    shard = jnp.reshape(lax.axis_index("mp"), (1,)).astype(jnp.int32)
    me = jnp.reshape(lax.axis_index(("g", "r")), (1,)).astype(jnp.int32)
    spread_shape = jax.ShapeDtypeStruct((GROUPS, PER_SHARD, ROWS_DEV, PIECE), jnp.bfloat16)
    routed_shape = jax.ShapeDtypeStruct((OWNERS * SLOTS, ROWS_DEV, PIECE), jnp.bfloat16)
    sums_shape = (GROUPS * SHARDS, 8, 128)

    places = pl.pallas_call(
        place_table_kernel,
        out_shape=jax.ShapeDtypeStruct((GROUPS * PER_SHARD,), jnp.int32),
        in_specs=[SMEM, SMEM],
        out_specs=SMEM,
        scratch_shapes=[pltpu.SMEM((OWNERS,), jnp.int32)],
        cost_estimate=pl.CostEstimate(flops=1000, bytes_accessed=1000, transcendentals=0),
        name="places",
    )(shard, block_owner)
    pieces = pl.pallas_call(
        spread_kernel, out_shape=spread_shape, in_specs=[WHOLE], out_specs=WHOLE, name="spread"
    )(gradient)
    pieces = exchange(pieces, "g")
    routed = pl.pallas_call(
        route_kernel, out_shape=routed_shape, in_specs=[SMEM, WHOLE], out_specs=WHOLE, name="route"
    )(places, pieces)
    got = exchange(routed, ("g", "r")).reshape(OWNERS, SLOTS, ROWS_DEV, PIECE)

    stat_spec = pl.BlockSpec((1, BLOCK, BLOCK), lambda k: (k, 0, 0))
    stat_shape = jax.ShapeDtypeStruct((SLOTS, BLOCK, BLOCK), jnp.float32)
    new_left, new_right, raw, sums = pl.pallas_call(
        owner_kernel,
        grid=(SLOTS,),
        out_shape=[stat_shape, stat_shape, stat_shape, jax.ShapeDtypeStruct(sums_shape, jnp.float32)],
        in_specs=[
            SMEM,
            SMEM,
            pl.BlockSpec((OWNERS, 1, ROWS_DEV, PIECE), lambda k: (0, k, 0, 0)),
            stat_spec,
            stat_spec,
        ],
        out_specs=[stat_spec, stat_spec, stat_spec, pl.BlockSpec(sums_shape, lambda k: (0, 0, 0))],
        scratch_shapes=[pltpu.VMEM((BLOCK, BLOCK), jnp.bfloat16)],
        compiler_params=pltpu.CompilerParams(vmem_limit_bytes=48 * 1024 * 1024),
        cost_estimate=pl.CostEstimate(
            flops=50 * 2 * BLOCK**3, bytes_accessed=12 * 1024 * 1024, transcendentals=0
        ),
        name="owner",
    )(me, places, got, prev_left[0, 0], prev_right[0, 0])

    sums = jnp.sum(exchange(sums, ("g", "mp")), axis=0, keepdims=True)
    sums = exchange(jnp.broadcast_to(sums, (MEMBERS, 8, 128)), "r")
    sending = pl.pallas_call(
        scale_kernel, out_shape=routed_shape, in_specs=[WHOLE, WHOLE], out_specs=WHOLE, name="scale"
    )(sums, raw)
    returned = exchange(sending, ("g", "r"))
    back = pl.pallas_call(
        collect_kernel, out_shape=spread_shape, in_specs=[SMEM, WHOLE], out_specs=WHOLE, name="collect"
    )(places, returned)
    back = exchange(back, "g")
    update_out = pl.pallas_call(
        place_kernel,
        out_shape=jax.ShapeDtypeStruct(gradient.shape, jnp.bfloat16),
        in_specs=[WHOLE],
        out_specs=WHOLE,
        name="place",
    )(back)
    return (update_out, new_left[None, None], new_right[None, None])


def solution(mesh):
    fine = Mesh(mesh.devices.reshape(GROUPS, MEMBERS, SHARDS), ("g", "r", "mp"))
    grad_spec = P(("g", "r"), "mp")
    stat_spec = P("mp", ("g", "r"), None, None, None)
    return jax.shard_map(
        shards,
        mesh=fine,
        in_specs=(grad_spec, P(), stat_spec, stat_spec),
        out_specs=(grad_spec, stat_spec, stat_spec),
        check_vma=False,
    )
```

time: 172 us -> 162 us (0.942); the launches traced: 169 us -> 161 us
  starting transfers between devices: 36 us -> 15.2 us
  waiting for transfers between devices: 20.5 us -> 38.1 us
    all_to_all x0 -> x2, waiting for transfers between devices: none -> 38.1 us  [exchange(): return lax.all_to_all(x, axes, split_axis=0, concat_axis=0, tiled=True)]
    ppermute x18 -> x0, starting transfers between devices: 36 us -> none  [the longest x12 19.4 us: sum_everywhere(): got = [lax.ppermute(x, axis, perm) for perm in perms]]
    ppermute x18 -> x0, waiting for transfers between devices: 20.5 us -> none  [the longest x6 10.8 us: between_groups(): moved.append(lax.ppermute(arrays[shift], 'dp', pairs))]
    all_to_all x0 -> x2, starting transfers between devices: none -> 15.2 us  [exchange(): return lax.all_to_all(x, axes, split_axis=0, concat_axis=0, tiled=True)]
    all_to_all x2 -> x4, blocking collectives: 76.1 us -> 74.4 us  [exchange(): return lax.all_to_all(x, axes, split_axis=0, concat_axis=0, tiled=True)]
    pallas_call x4 -> x5, Pallas kernels: 10.3 us -> 9.95 us  [the longest x1 2.9 us: shards(): pl.pallas_call(scale_kernel, out_shape=routed_shape, in_specs=[WHOLE, WHO...]
  transfers between devices with their start and end apart: 18 -> 2, of which waited for: 13 -> 2; matrix products, arithmetic and copies ran while one was open for 0% -> 0% of each run, Pallas kernels for 0% -> 1%
where the time goes in v1:
time: 162 us; the launch traced here: 161 us
  blocking collectives  74.4 us (46%)
  waiting for transfers between devices  38.1 us (24%)
  Pallas kernels  30.8 us (19%)
  starting transfers between devices  15.2 us (9%)
  local copies, waits for them, and re-layouts  2.07 us (1%)
    all_to_all x4, blocking collectives, exchange(): return lax.all_to_all(x, axes, split_axis=0, concat_axis=0, tiled=True)  74.4 us
    all_to_all x2, waiting for transfers between devices, exchange(): return lax.all_to_all(x, axes, split_axis=0, concat_axis=0, tiled=True)  38.1 us
    pallas_call x1, Pallas kernels, shards(): pl.pallas_call(owner_kernel, grid=(SLOTS,), out_shape=[stat_shape, stat_s...  19.1 us
    all_to_all x2, starting transfers between devices, exchange(): return lax.all_to_all(x, axes, split_axis=0, concat_axis=0, tiled=True)  15.2 us
  transfers between devices with their start and end apart: 2, of which 2 were waited for; matrix products, arithmetic and copies ran while one was open for 0% of the time, Pallas kernels for 1%

profile of v1, /device:TPU:8, one launch (start us, length us, event | category | flops | bytes accessed | tf_op | source)
XLA Modules:
  0.0 161.2 jit_solution(7936254530575827551)
XLA Ops:
  0.6 1.7 %spread.1 = bf16[4,8,32,128]{3,2,1,0:T(8,128)(2,1)} custom-call(bf16[32,4096]{1,0:T(8,128)(2,1)} %grad_ref.1), custom_call_target="tpu_custom_call" | custom-call | tf_op jit(solution)/shard_map/spread/pallas_call | solution.py:165
  2.3 0.0 copy-start.2
  2.3 8.6 %all-to-all-start = ((bf16[4,8,32,128]{3,2,1,0:T(8,128)(2,1)}), bf16[4,8,32,128]{3,2,1,0:T(8,128)(2,1)S(1)}, u32[]{:S(2)}, u32[]{:S(2)}) async-start(bf16[4,8,32,128]{3,2,1,0:T(8,128)(2,1)} %spread.1), calls=%async_computation | async-start | bytes 524288 | tf_op jit(solution)/shard_map/all_to_all | solution.py:146
  10.9 1.4 places.1.place_ref
  12.4 0.0 copy-start.1
  12.4 9.3 %all-to-all-done.in_ref = bf16[4,8,32,128]{3,2,1,0:T(8,128)(2,1)S(1)} async-done(((bf16[4,8,32,128]{3,2,1,0:T(8,128)(2,1)}), bf16[4,8,32,128]{3,2,1,0:T(8,128)(2,1)S(1)}, u32[]{:S(2)}, u32[]{:S(2)}) %all-to-all-start) | async-done | bytes 262176 | tf_op jit(solution)/shard_map/all_to_all | solution.py:146
  21.7 0.0 copy-start.3
  21.7 0.7 copy-done.3
  22.4 2.0 %route.1 = bf16[128,32,128]{2,1,0:T(8,128)(2,1)} custom-call(s32[32]{0:T(128)} %places.1.place_ref, bf16[4,8,32,128]{3,2,1,0:T(8,128)(2,1)} %copy-done.3), custom_call_target="tpu_custom_call" | custom-call | tf_op jit(solution)/shard_map/route/pallas_call | solution.py:169
  24.3 6.6 %all-to-all-start.1 = ((bf16[128,32,128]{2,1,0:T(8,128)(2,1)}), bf16[128,32,128]{2,1,0:T(8,128)(2,1)S(1)}, u32[]{:S(2)}, u32[]{:S(2)}) async-start(bf16[128,32,128]{2,1,0:T(8,128)(2,1)} %route.1), calls=%async_computation.1 | async-start | bytes 2097152 | tf_op jit(solution)/shard_map/all_to_all | solution.py:146
  30.9 28.8 %all-to-all-done.1 = bf16[128,32,128]{2,1,0:T(8,128)(2,1)S(1)} async-done(((bf16[128,32,128]{2,1,0:T(8,128)(2,1)}), bf16[128,32,128]{2,1,0:T(8,128)(2,1)S(1)}, u32[]{:S(2)}, u32[]{:S(2)}) %all-to-all-start.1) | async-done | bytes 1048608 | tf_op jit(solution)/shard_map/all_to_all | solution.py:146
  59.7 0.0 copy-done.2
  59.7 0.0 copy-done.1
  59.7 19.1 %owner.1 = (f32[2,512,512]{2,1,0:T(8,128)}, f32[2,512,512]{2,1,0:T(8,128)}, f32[2,512,512]{2,1,0:T(8,128)S(1)}, f32[16,8,128]{2,1,0:T(8,128)S(1)}) custom-call(s32[1]{0:T(128)} %bitcast.1.me_ref, s32[32]{0:T(128)S(1)} %copy-done.1, bf16[64,2,32,128]{3,2,1,0:T(8,128)(2,1)S(1)} %bitcast.7, f32[2,512,512]{2,1,0:T(8,128)S(1)} %bitcast.8, f32[2,512,512]{2,1,0:T(8,128)} %bitcast.9), custom_call_target="tpu_custom_call" | custom-call | flops 13421772800 | bytes 12582912 | tf_op jit(solution)/shard_map/owner/pallas_call | solution.py:176
  78.9 0.0 copy-start
  78.9 1.4 copy-done
  80.2 14.8 %all_to_all.30 = f32[16,8,128]{2,1,0:T(8,128)S(1)} all-to-all(f32[16,8,128]{2,1,0:T(8,128)S(1)} %get-tuple-element.7), channel_id=1, replica_groups=mesh['g'=4,'r'=16,'mp'=4] {'g','mp'}, dimensions={0} | all-to-all | bytes 131072 | tf_op jit(solution)/shard_map/all_to_all | solution.py:146
  95.1 9.6 %all_to_all.31.sums_ref = f32[16,8,128]{2,1,0:T(8,128)} all-to-all(f32[16,8,128]{2,1,0:T(8,128)S(1)} %broadcast_in_dim.12), channel_id=1, replica_groups=mesh['g'=4,'r'=16,'mp'=4] {'r'}, dimensions={0} | all-to-all | bytes 131072 | tf_op jit(solution)/shard_map/all_to_all | solution.py:146
  104.7 2.9 %scale.1 = bf16[128,32,128]{2,1,0:T(8,128)(2,1)} custom-call(f32[16,8,128]{2,1,0:T(8,128)} %all_to_all.31.sums_ref, f32[2,512,512]{2,1,0:T(8,128)} %copy-done), custom_call_target="tpu_custom_call" | custom-call | tf_op jit(solution)/shard_map/scale/pallas_call | solution.py:198
  107.6 35.3 %all_to_all.32.in_ref = bf16[128,32,128]{2,1,0:T(8,128)(2,1)} all-to-all(bf16[128,32,128]{2,1,0:T(8,128)(2,1)} %scale.1), channel_id=1, replica_groups=mesh['g'=4,'r'=16,'mp'=4] {'g','r'}, dimensions={0} | all-to-all | bytes 2097152 | tf_op jit(solution)/shard_map/all_to_all | solution.py:146
  142.8 2.0 %collect.1 = bf16[4,8,32,128]{3,2,1,0:T(8,128)(2,1)} custom-call(s32[32]{0:T(128)} %places.1.place_ref, bf16[128,32,128]{2,1,0:T(8,128)(2,1)} %all_to_all.32.in_ref), custom_call_target="tpu_custom_call" | custom-call | tf_op jit(solution)/shard_map/collect/pallas_call | solution.py:202
  144.8 14.7 %all_to_all.33.in_ref = bf16[4,8,32,128]{3,2,1,0:T(8,128)(2,1)} all-to-all(bf16[4,8,32,128]{3,2,1,0:T(8,128)(2,1)} %collect.1), channel_id=1, replica_groups=mesh['g'=4,'r'=16,'mp'=4] {'g'}, dimensions={0} | all-to-all | bytes 524288 | tf_op jit(solution)/shard_map/all_to_all | solution.py:146
  159.5 1.7 %place.1 = bf16[32,4096]{1,0:T(8,128)(2,1)} custom-call(bf16[4,8,32,128]{3,2,1,0:T(8,128)(2,1)} %all_to_all.33.in_ref), custom_call_target="tpu_custom_call" | custom-call | tf_op jit(solution)/shard_map/place/pallas_call | solution.py:206
  (2 shorter events, 0.0 us)
Async XLA Ops:
  2.3 57.4 %copy-start.2 = (f32[1,1,2,512,512]{4,3,2,1,0:T(8,128)S(1)}, f32[1,1,2,512,512]{4,3,2,1,0:T(8,128)}, u32[]{:S(2)}) copy-start(f32[1,1,2,512,512]{4,3,2,1,0:T(8,128)} %param.6) | copy-start | bytes 6291460
  2.3 19.3 %all-to-all-start = ((bf16[4,8,32,128]{3,2,1,0:T(8,128)(2,1)}), bf16[4,8,32,128]{3,2,1,0:T(8,128)(2,1)S(1)}, u32[]{:S(2)}, u32[]{:S(2)}) async-start(bf16[4,8,32,128]{3,2,1,0:T(8,128)(2,1)} %spread.1), calls=%async_computation | async-start | bytes 524288 | tf_op jit(solution)/shard_map/all_to_all | solution.py:146
  12.4 47.4 %copy-start.1 = (s32[32]{0:T(128)S(1)}, s32[32]{0:T(128)}, u32[]{:S(2)}) copy-start(s32[32]{0:T(128)} %places.1.place_ref) | copy-start | bytes 388
  21.7 0.7 copy-start.3
  24.3 35.4 %all-to-all-start.1 = ((bf16[128,32,128]{2,1,0:T(8,128)(2,1)}), bf16[128,32,128]{2,1,0:T(8,128)(2,1)S(1)}, u32[]{:S(2)}, u32[]{:S(2)}) async-start(bf16[128,32,128]{2,1,0:T(8,128)(2,1)} %route.1), calls=%async_computation.1 | async-start | bytes 2097152 | tf_op jit(solution)/shard_map/all_to_all | solution.py:146
  78.9 1.4 copy-start

commit v2 on v1

v2 whole, which is shorter than its diff:
```python
import jax
import jax.numpy as jnp
from jax import lax
from jax.experimental import pallas as pl
from jax.experimental.pallas import tpu as pltpu
from jax.sharding import Mesh
from jax.sharding import PartitionSpec as P

EPS_DAMP = 1.0
BETA = 0.95
BLOCK = 512
SHARDS = 4
GROUPS = 4
MEMBERS = 16
PER_SHARD = 8
BLOCKS = GROUPS * PER_SHARD
OWNERS = 64
SLOTS = 2
LINES = 8
CELLS = 2048 * 16384
MIB = 1024 * 1024

WHOLE = pl.BlockSpec(memory_space=pltpu.VMEM)
SMEM = pl.BlockSpec(memory_space=pltpu.SMEM)


def params(mib):
    return pltpu.CompilerParams(vmem_limit_bytes=mib * MIB)


def place_table_kernel(shard_ref, owner_ref, place_ref, count_ref):
    base = shard_ref[0] * PER_SHARD

    def clear(o, _):
        count_ref[o] = 0
        return 0

    lax.fori_loop(0, OWNERS, clear, 0, unroll=8)
    for b in range(BLOCKS):
        owner = owner_ref[b // PER_SHARD, base + b % PER_SHARD]
        slot = count_ref[owner]
        count_ref[owner] = slot + 1
        place_ref[b] = (lax.rem(owner, MEMBERS) * GROUPS + owner // MEMBERS) * SLOTS + slot


def route_kernel(place_ref, in_ref, out_ref):
    for row in range(GROUPS):
        for j in range(PER_SHARD):
            place = place_ref[row * PER_SHARD + j]
            columns = pl.ds(pl.multiple_of(lax.rem(place, SLOTS) * BLOCK, BLOCK), BLOCK)
            out_ref[place // SLOTS, :, columns] = in_ref[row, :, pl.ds(j * BLOCK, BLOCK)]


def collect_kernel(place_ref, sums_ref, in_ref, out_ref):
    grad_total = sums_ref[0:1, 0:1]
    update_total = sums_ref[1:2, 0:1]
    graft = jnp.sqrt(grad_total / CELLS) * lax.rsqrt(update_total / CELLS + 1e-06)
    for row in range(GROUPS):
        for j in range(PER_SHARD):
            place = place_ref[row * PER_SHARD + j]
            slot = lax.rem(place, SLOTS)
            columns = pl.ds(pl.multiple_of(slot * BLOCK, BLOCK), BLOCK)
            coded = in_ref[place // SLOTS, :, columns].astype(jnp.int32).astype(jnp.float32)
            steps = jnp.exp2(
                in_ref[place // SLOTS, :, pl.ds(SLOTS * BLOCK, 128)].astype(jnp.int32).astype(jnp.float32)
            )
            step = jnp.where(slot == 0, steps[:, 0:1], steps[:, 64:65])
            out_ref[row, :, pl.ds(j * BLOCK, BLOCK)] = (coded * (step * graft)).astype(jnp.bfloat16)


def dot(a, b):
    return jnp.dot(a, b, preferred_element_type=jnp.float32)


def split(x):
    high = x.astype(jnp.bfloat16)
    return high, (x - high.astype(jnp.float32)).astype(jnp.bfloat16)


def dot3(a, b):
    return dot(a[0], b[0]) + (dot(a[0], b[1]) + dot(a[1], b[0]))


def root(stat, eye):
    damped = stat + EPS_DAMP * eye
    total = jnp.sum(damped * damped, keepdims=True)
    norm = jnp.sqrt(total)
    n = damped * (1.0 / norm)
    n_split = split(n)
    n2 = dot3(n_split, n_split)
    q = split(1.5625 * eye - 2.5 * n + n2)
    h = split(1.25 * n - n2)
    r = split(dot3(q, q))
    product = 1.5625 * eye - 1.25 * n - dot3(h, r)
    return product * lax.rsqrt(jnp.sqrt(0.25 * norm))


def owner_kernel(me_ref, place_ref, got_ref, left_ref, right_ref, new_left_ref, new_right_ref, coded_ref,
                 sums_ref, power_ref):
    slot = pl.program_id(0)
    wanted = me_ref[0] * SLOTS + slot
    used = place_ref[0] == wanted
    for b in range(1, BLOCKS):
        used = used | (place_ref[b] == wanted)
    block = got_ref[...]
    block = jnp.where(used, block, jnp.zeros_like(block))
    turned = block.T
    rows = lax.broadcasted_iota(jnp.int32, (BLOCK, BLOCK), 0)
    columns = lax.broadcasted_iota(jnp.int32, (BLOCK, BLOCK), 1)
    eye = jnp.where(rows == columns, 1.0, 0.0).astype(jnp.float32)
    left = BETA * left_ref[0] + dot(block, turned)
    new_left_ref[0] = left
    right = BETA * right_ref[0] + dot(turned, block)
    new_right_ref[0] = right
    left_root = split(root(left, eye))
    half = split(dot(left_root[0], block) + dot(left_root[1], block))
    raw = dot3(half, split(root(right, eye)))
    wide = block.astype(jnp.float32)
    grad_sq = jnp.sum(wide * wide, keepdims=True)
    update_sq = jnp.sum(raw * raw, keepdims=True)
    line = lax.broadcasted_iota(jnp.int32, sums_ref.shape, 0)
    sums = jnp.where(line == 0, grad_sq, update_sq)
    largest = jnp.max(jnp.abs(raw), axis=1, keepdims=True)
    power = jnp.ceil(jnp.log2(jnp.maximum(largest, 1e-30)) + 0.001) - 15.0
    coded = jnp.round(raw * jnp.exp2(-power)).astype(jnp.int32)
    place = pl.ds(pl.multiple_of(slot * BLOCK, BLOCK), BLOCK)
    for p in range(OWNERS):
        coded_ref[p, :, place] = coded[p * LINES : (p + 1) * LINES].astype(jnp.int16)

    @pl.when(slot == 0)
    def _():
        sums_ref[...] = sums
        power_ref[...] = jnp.broadcast_to(power, power_ref.shape)

    @pl.when(slot > 0)
    def _():
        sums_ref[...] += sums
        lane = lax.broadcasted_iota(jnp.int32, power_ref.shape, 1)
        powers = jnp.where(lane < 64, power_ref[...], power).astype(jnp.int32)
        for p in range(OWNERS):
            coded_ref[p, :, pl.ds(SLOTS * BLOCK, 128)] = powers[p * LINES : (p + 1) * LINES].astype(jnp.int16)


def exchange(x, axes):
    return lax.all_to_all(x, axes, split_axis=0, concat_axis=0, tiled=True)


def sum_everywhere(x):
    stages = [
        ("mp", [[(d, (d + s) % SHARDS) for d in range(SHARDS)] for s in (1, 2, 3)]),
        ("r", [[(d, d // 8 * 8 + (d + s) % 8) for d in range(MEMBERS)] for s in (2, 4, 6)]),
        ("r", [[(d, d ^ s) for d in range(MEMBERS)] for s in (1, 8, 9)]),
        ("g", [[(d, (d + s) % GROUPS) for d in range(GROUPS)] for s in (1, 2, 3)]),
    ]
    for axis, perms in stages:
        got = [lax.ppermute(x, axis, perm) for perm in perms]
        x = (x + got[0]) + (got[1] + got[2])
    return x


def shards(gradient, block_owner, prev_left, prev_right):
    shard = jnp.reshape(lax.axis_index("mp"), (1,)).astype(jnp.int32)
    me = jnp.reshape(lax.axis_index(("r", "g")), (1,)).astype(jnp.int32)
    spread_shape = (GROUPS, LINES, PER_SHARD * BLOCK)

    places = pl.pallas_call(
        place_table_kernel,
        out_shape=jax.ShapeDtypeStruct((BLOCKS,), jnp.int32),
        in_specs=[SMEM, SMEM],
        out_specs=SMEM,
        scratch_shapes=[pltpu.SMEM((OWNERS,), jnp.int32)],
        compiler_params=params(4),
        cost_estimate=pl.CostEstimate(flops=1000, bytes_accessed=1000, transcendentals=0),
        name="places",
    )(shard, block_owner)
    pieces = exchange(gradient.reshape(spread_shape), "g")
    routed = pl.pallas_call(
        route_kernel,
        out_shape=jax.ShapeDtypeStruct((OWNERS, LINES, SLOTS * BLOCK), jnp.bfloat16),
        in_specs=[SMEM, WHOLE],
        out_specs=WHOLE,
        compiler_params=params(4),
        name="route",
    )(places, pieces)
    got = exchange(routed, ("r", "g")).reshape(BLOCK, SLOTS * BLOCK)

    stat_spec = pl.BlockSpec((1, BLOCK, BLOCK), lambda k: (k, 0, 0))
    stat_shape = jax.ShapeDtypeStruct((SLOTS, BLOCK, BLOCK), jnp.float32)
    coded_shape = (OWNERS, LINES, SLOTS * BLOCK + 128)
    new_left, new_right, coded, sums = pl.pallas_call(
        owner_kernel,
        grid=(SLOTS,),
        out_shape=[
            stat_shape,
            stat_shape,
            jax.ShapeDtypeStruct(coded_shape, jnp.int16),
            jax.ShapeDtypeStruct((8, 128), jnp.float32),
        ],
        in_specs=[SMEM, SMEM, pl.BlockSpec((BLOCK, BLOCK), lambda k: (0, k)), stat_spec, stat_spec],
        out_specs=[
            stat_spec,
            stat_spec,
            pl.BlockSpec(coded_shape, lambda k: (0, 0, 0)),
            pl.BlockSpec((8, 128), lambda k: (0, 0)),
        ],
        scratch_shapes=[pltpu.VMEM((BLOCK, 128), jnp.float32)],
        compiler_params=params(40),
        cost_estimate=pl.CostEstimate(
            flops=50 * 2 * BLOCK**3, bytes_accessed=12 * MIB, transcendentals=0
        ),
        name="owner",
    )(me, places, got, prev_left[0, 0], prev_right[0, 0])

    returned = exchange(coded, ("r", "g"))
    sums = sum_everywhere(sums)
    back = pl.pallas_call(
        collect_kernel,
        out_shape=jax.ShapeDtypeStruct(spread_shape, jnp.bfloat16),
        in_specs=[SMEM, WHOLE, WHOLE],
        out_specs=WHOLE,
        compiler_params=params(8),
        name="collect",
    )(places, sums, returned)
    update_out = exchange(back, "g").reshape(gradient.shape)
    return (update_out, new_left[None, None], new_right[None, None])


def solution(mesh):
    fine = Mesh(mesh.devices.reshape(GROUPS, MEMBERS, SHARDS), ("g", "r", "mp"))
    grad_spec = P(("g", "r"), "mp")
    stat_spec = P("mp", ("g", "r"), None, None, None)
    return jax.shard_map(
        shards,
        mesh=fine,
        in_specs=(grad_spec, P(), stat_spec, stat_spec),
        out_specs=(grad_spec, stat_spec, stat_spec),
        check_vma=False,
    )
```

time: 162 us -> 139 us (0.86)
  blocking collectives: 74.4 us -> 15.4 us
  starting transfers between devices: 15.2 us -> 41.2 us
  waiting for transfers between devices: 38.1 us -> 55.5 us
  Pallas kernels: 30.8 us -> 23 us
    all_to_all x4 -> x1, blocking collectives: 74.4 us -> 15.4 us  [exchange(): return lax.all_to_all(x, axes, split_axis=0, concat_axis=0, tiled=True)]
    ppermute x0 -> x12, waiting for transfers between devices: none -> 19.9 us  [sum_everywhere(): got = [lax.ppermute(x, axis, perm) for perm in perms]]
    ppermute x0 -> x12, starting transfers between devices: none -> 18.5 us  [sum_everywhere(): got = [lax.ppermute(x, axis, perm) for perm in perms]]
    pallas_call x6 -> x3, Pallas kernels: 11.7 us -> 4.06 us  [the longest x1 1.71 us: shards(): pl.pallas_call(route_kernel, out_shape=jax.ShapeDtypeStruct((OWNERS, LINE...]
    all_to_all x2 -> x3, starting transfers between devices: 15.2 us -> 22.8 us  [exchange(): return lax.all_to_all(x, axes, split_axis=0, concat_axis=0, tiled=True)]
    all_to_all x2 -> x3, waiting for transfers between devices: 38.1 us -> 35.6 us  [exchange(): return lax.all_to_all(x, axes, split_axis=0, concat_axis=0, tiled=True)]
  transfers between devices with their start and end apart: 2 -> 15, of which waited for: 2 -> 10; matrix products, arithmetic and copies ran while one was open for 0% -> 0% of each run, Pallas kernels for 1% -> 1%
where the time goes in v2:
time: 139 us
  waiting for transfers between devices  55.5 us (40%)
  starting transfers between devices  41.2 us (30%)
  Pallas kernels  23 us (17%)
  blocking collectives  15.4 us (11%)
  local copies, waits for them, and re-layouts  2.98 us (2%)
    all_to_all x3, waiting for transfers between devices, exchange(): return lax.all_to_all(x, axes, split_axis=0, concat_axis=0, tiled=True)  35.6 us
    all_to_all x3, starting transfers between devices, exchange(): return lax.all_to_all(x, axes, split_axis=0, concat_axis=0, tiled=True)  22.8 us
    ppermute x12, waiting for transfers between devices, sum_everywhere(): got = [lax.ppermute(x, axis, perm) for perm in perms]  19.9 us
    pallas_call x1, Pallas kernels, shards(): pl.pallas_call(owner_kernel, grid=(SLOTS,), out_shape=[stat_shape, stat_s...  18.9 us
    ppermute x12, starting transfers between devices, sum_everywhere(): got = [lax.ppermute(x, axis, perm) for perm in perms]  18.5 us
    all_to_all x1, blocking collectives, exchange(): return lax.all_to_all(x, axes, split_axis=0, concat_axis=0, tiled=True)  15.4 us
    unnamed x7, local copies, waits for them, and re-layouts  2.98 us
  transfers between devices with their start and end apart: 15, of which 10 were waited for; matrix products, arithmetic and copies ran while one was open for 0% of the time, Pallas kernels for 1%

profile of v2, /device:TPU:8, one launch (start us, length us, event | category | flops | bytes accessed | tf_op | source)
XLA Modules:
  0.0 138.8 jit_solution(12271594830545787911)
XLA Ops:
  0.6 8.5 %all-to-all-start = ((bf16[4,8,4096]{2,1,0:T(8,128)(2,1)}), bf16[4,8,4096]{2,1,0:T(8,128)(2,1)S(1)}, u32[]{:S(2)}, u32[]{:S(2)}) async-start(bf16[4,8,4096]{2,1,0:T(8,128)(2,1)} %bitcast.13), calls=%async_computation | async-start | bytes 524288 | tf_op jit(solution)/shard_map/all_to_all | solution.py:145
  9.1 0.0 copy-start
  9.1 0.7 copy-done
  9.8 0.0 copy-start.1
  9.8 1.5 %places.1.place_ref = s32[32]{0:T(128)S(1)} custom-call(s32[1]{0:T(128)} %bitcast.shard_ref, s32[4,32]{1,0:T(4,128)S(1)} %copy-done), custom_call_target="tpu_custom_call" | custom-call | flops 1000 | bytes 1000 | tf_op jit(solution)/shard_map/places/pallas_call | solution.py:166
  11.3 8.6 %all-to-all-done.in_ref = bf16[4,8,4096]{2,1,0:T(8,128)(2,1)S(1)} async-done(((bf16[4,8,4096]{2,1,0:T(8,128)(2,1)}), bf16[4,8,4096]{2,1,0:T(8,128)(2,1)S(1)}, u32[]{:S(2)}, u32[]{:S(2)}) %all-to-all-start) | async-done | bytes 262176 | tf_op jit(solution)/shard_map/all_to_all | solution.py:145
  19.8 1.7 %route.1 = bf16[64,8,1024]{2,1,0:T(8,128)(2,1)} custom-call(s32[32]{0:T(128)S(1)} %places.1.place_ref, bf16[4,8,4096]{2,1,0:T(8,128)(2,1)S(1)} %all-to-all-done.in_ref), custom_call_target="tpu_custom_call" | custom-call | tf_op jit(solution)/shard_map/route/pallas_call | solution.py:177
  21.5 6.6 %all-to-all-start.1 = ((bf16[64,8,1024]{2,1,0:T(8,128)(2,1)}), bf16[64,8,1024]{2,1,0:T(8,128)(2,1)S(1)}, u32[]{:S(2)}, u32[]{:S(2)}) async-start(bf16[64,8,1024]{2,1,0:T(8,128)(2,1)} %route.1), calls=%async_computation.1 | async-start | bytes 2097152 | tf_op jit(solution)/shard_map/all_to_all | solution.py:145
  28.2 27.1 %all-to-all-done.1 = bf16[64,8,1024]{2,1,0:T(8,128)(2,1)S(1)} async-done(((bf16[64,8,1024]{2,1,0:T(8,128)(2,1)}), bf16[64,8,1024]{2,1,0:T(8,128)(2,1)S(1)}, u32[]{:S(2)}, u32[]{:S(2)}) %all-to-all-start.1) | async-done | bytes 1048608 | tf_op jit(solution)/shard_map/all_to_all | solution.py:145
  55.2 0.0 copy-done.1
  55.2 0.0 copy-start.2
  55.2 1.6 %copy-done.2 = f32[1,1,2,512,512]{4,3,2,1,0:T(8,128)S(1)} copy-done((f32[1,1,2,512,512]{4,3,2,1,0:T(8,128)S(1)}, f32[1,1,2,512,512]{4,3,2,1,0:T(8,128)}, u32[]{:S(2)}) %copy-start.2) | copy-done | bytes 2097176
  56.8 18.9 %owner.1 = (f32[2,512,512]{2,1,0:T(8,128)}, f32[2,512,512]{2,1,0:T(8,128)}, s16[64,8,1152]{2,1,0:T(8,128)(2,1)}, f32[8,128]{1,0:T(8,128)S(1)}) custom-call(s32[1]{0:T(128)} %bitcast.1.me_ref, s32[32]{0:T(128)S(1)} %places.1.place_ref, bf16[512,1024]{1,0:T(8,128)(2,1)S(1)} %bitcast.9, f32[2,512,512]{2,1,0:T(8,128)S(1)} %bitcast.10, f32[2,512,512]{2,1,0:T(8,128)S(1)} %bitcast.11), custom_call_target="tpu_custom_call" | custom-call | flops 13421772800 | bytes 12582912 | tf_op jit(solution)/shard_map/owner/pallas_call | solution.py:190
  75.7 7.7 %all-to-all-start.2 = ((s16[64,8,1152]{2,1,0:T(8,128)(2,1)}), s16[64,8,1152]{2,1,0:T(8,128)(2,1)S(1)}, u32[]{:S(2)}, u32[]{:S(2)}) async-start(s16[64,8,1152]{2,1,0:T(8,128)(2,1)} %get-tuple-element.8), calls=%async_computation.2 | async-start | bytes 2359296 | tf_op jit(solution)/shard_map/all_to_all | solution.py:145
  83.4 2.8 %collective-permute-start.2 = (f32[8,128]{1,0:T(8,128)S(1)}, f32[8,128]{1,0:T(8,128)S(1)}, u32[]{:S(2)}, u32[]{:S(2)}) collective-permute-start(f32[8,128]{1,0:T(8,128)S(1)} %get-tuple-element.7), channel_id=1, source_target_pairs={{0,3},{1,0},{2,1},{3,2},{4,7},{5,4},{6,5},{7,6},{8,11},{9,8},{10,9... | collective-permute-start | bytes 12296 | tf_op jit(solution)/shard_map/ppermute | solution.py:156
  86.3 0.8 collective-permute-start.1
  87.1 0.9 collective-permute-start
  88.0 0.0 collective-permute-done.2
  88.0 3.4 %collective-permute-done.1 = f32[8,128]{1,0:T(8,128)S(1)} collective-permute-done((f32[8,128]{1,0:T(8,128)S(1)}, f32[8,128]{1,0:T(8,128)S(1)}, u32[]{:S(2)}, u32[]{:S(2)}) %collective-permute-start.1) | collective-permute-done | bytes 4128 | tf_op jit(solution)/shard_map/ppermute | solution.py:156
  91.4 0.5 collective-permute-done
  91.9 0.5 collective-permute-start.5
  92.4 2.5 %collective-permute-start.4 = (f32[8,128]{1,0:T(8,128)S(1)}, f32[8,128]{1,0:T(8,128)S(1)}, u32[]{:S(2)}, u32[]{:S(2)}) collective-permute-start(f32[8,128]{1,0:T(8,128)S(1)} %add_add_fusion.3), channel_id=1, source_target_pairs={{0,16},{4,20},{8,24},{12,28},{16,0},{20,4},{24,8},{28,12},{32,48},... | collective-permute-start | bytes 12296 | tf_op jit(solution)/shard_map/ppermute | solution.py:156
  94.8 1.8 %collective-permute-start.3 = (f32[8,128]{1,0:T(8,128)S(1)}, f32[8,128]{1,0:T(8,128)S(1)}, u32[]{:S(2)}, u32[]{:S(2)}) collective-permute-start(f32[8,128]{1,0:T(8,128)S(1)} %add_add_fusion.3), channel_id=1, source_target_pairs={{0,8},{4,12},{8,16},{12,20},{16,24},{20,28},{24,0},{28,4},{32,40},... | collective-permute-start | bytes 12296 | tf_op jit(solution)/shard_map/ppermute | solution.py:156
  96.6 0.0 collective-permute-done.5
  96.6 0.9 collective-permute-done.4
  97.5 1.2 collective-permute-done.3
  98.7 0.0 collective-permute-start.8
  98.7 1.5 %collective-permute-start.7 = (f32[8,128]{1,0:T(8,128)S(1)}, f32[8,128]{1,0:T(8,128)S(1)}, u32[]{:S(2)}, u32[]{:S(2)}) collective-permute-start(f32[8,128]{1,0:T(8,128)S(1)} %add_add_fusion.2), channel_id=1, source_target_pairs={{0,32},{4,36},{8,40},{12,44},{16,48},{20,52},{24,56},{28,60},{32,0... | collective-permute-start | bytes 12296 | tf_op jit(solution)/shard_map/ppermute | solution.py:156
  100.2 0.3 collective-permute-start.6
  100.6 10.2 %collective-permute-done.8 = f32[8,128]{1,0:T(8,128)S(1)} collective-permute-done((f32[8,128]{1,0:T(8,128)S(1)}, f32[8,128]{1,0:T(8,128)S(1)}, u32[]{:S(2)}, u32[]{:S(2)}) %collective-permute-start.8) | collective-permute-done | bytes 4128 | tf_op jit(solution)/shard_map/ppermute | solution.py:156
  110.8 0.6 collective-permute-done.7
  111.4 0.0 collective-permute-done.6
  111.4 2.6 %collective-permute-start.11 = (f32[8,128]{1,0:T(8,128)S(1)}, f32[8,128]{1,0:T(8,128)S(1)}, u32[]{:S(2)}, u32[]{:S(2)}) collective-permute-start(f32[8,128]{1,0:T(8,128)S(1)} %add_add_fusion.1), channel_id=1, source_target_pairs={{0,192},{64,0},{128,64},{192,128},{1,193},{65,1},{129,65},{193,129... | collective-permute-start | bytes 12296 | tf_op jit(solution)/shard_map/ppermute | solution.py:156
  114.0 2.1 %collective-permute-start.10 = (f32[8,128]{1,0:T(8,128)S(1)}, f32[8,128]{1,0:T(8,128)S(1)}, u32[]{:S(2)}, u32[]{:S(2)}) collective-permute-start(f32[8,128]{1,0:T(8,128)S(1)} %add_add_fusion.1), channel_id=1, source_target_pairs={{0,128},{64,192},{128,0},{192,64},{1,129},{65,193},{129,1},{193,65... | collective-permute-start | bytes 12296 | tf_op jit(solution)/shard_map/ppermute | solution.py:156
  116.1 2.6 %collective-permute-start.9 = (f32[8,128]{1,0:T(8,128)S(1)}, f32[8,128]{1,0:T(8,128)S(1)}, u32[]{:S(2)}, u32[]{:S(2)}) collective-permute-start(f32[8,128]{1,0:T(8,128)S(1)} %add_add_fusion.1), channel_id=1, source_target_pairs={{0,64},{64,128},{128,192},{192,0},{1,65},{65,129},{129,193},{193,1... | collective-permute-start | bytes 12296 | tf_op jit(solution)/shard_map/ppermute | solution.py:156
  118.7 0.0 collective-permute-done.11
  118.7 2.8 %collective-permute-done.10 = f32[8,128]{1,0:T(8,128)S(1)} collective-permute-done((f32[8,128]{1,0:T(8,128)S(1)}, f32[8,128]{1,0:T(8,128)S(1)}, u32[]{:S(2)}, u32[]{:S(2)}) %collective-permute-start.10) | collective-permute-done | bytes 4128 | tf_op jit(solution)/shard_map/ppermute | solution.py:156
  121.5 0.3 collective-permute-done.9
  121.8 0.0 all-to-all-done.2.in_ref
  121.8 0.9 collect.1
  122.7 15.4 %all_to_all.20 = bf16[4,8,4096]{2,1,0:T(8,128)(2,1)S(1)} all-to-all(bf16[4,8,4096]{2,1,0:T(8,128)(2,1)S(1)} %collect.1), channel_id=1, replica_groups=mesh['g'=4,'r'=16,'mp'=4] {'g'}, dimensions={0} | all-to-all | bytes 524288 | tf_op jit(solution)/shard_map/all_to_all | solution.py:145
  138.1 0.7 copy.8
  (4 shorter events, 0.0 us)
Async XLA Ops:
  0.6 19.2 %all-to-all-start = ((bf16[4,8,4096]{2,1,0:T(8,128)(2,1)}), bf16[4,8,4096]{2,1,0:T(8,128)(2,1)S(1)}, u32[]{:S(2)}, u32[]{:S(2)}) async-start(bf16[4,8,4096]{2,1,0:T(8,128)(2,1)} %bitcast.13), calls=%async_computation | async-start | bytes 524288 | tf_op jit(solution)/shard_map/all_to_all | solution.py:145
  9.1 0.7 copy-start
  9.8 45.5 %copy-start.1 = (f32[1,1,2,512,512]{4,3,2,1,0:T(8,128)S(1)}, f32[1,1,2,512,512]{4,3,2,1,0:T(8,128)}, u32[]{:S(2)}) copy-start(f32[1,1,2,512,512]{4,3,2,1,0:T(8,128)} %param.6) | copy-start | bytes 6291460
  21.5 33.7 %all-to-all-start.1 = ((bf16[64,8,1024]{2,1,0:T(8,128)(2,1)}), bf16[64,8,1024]{2,1,0:T(8,128)(2,1)S(1)}, u32[]{:S(2)}, u32[]{:S(2)}) async-start(bf16[64,8,1024]{2,1,0:T(8,128)(2,1)} %route.1), calls=%async_computation.1 | async-start | bytes 2097152 | tf_op jit(solution)/shard_map/all_to_all | solution.py:145
  55.2 1.6 %copy-start.2 = (f32[1,1,2,512,512]{4,3,2,1,0:T(8,128)S(1)}, f32[1,1,2,512,512]{4,3,2,1,0:T(8,128)}, u32[]{:S(2)}) copy-start(f32[1,1,2,512,512]{4,3,2,1,0:T(8,128)} %param.7) | copy-start | bytes 6291460
  75.7 46.1 %all-to-all-start.2 = ((s16[64,8,1152]{2,1,0:T(8,128)(2,1)}), s16[64,8,1152]{2,1,0:T(8,128)(2,1)S(1)}, u32[]{:S(2)}, u32[]{:S(2)}) async-start(s16[64,8,1152]{2,1,0:T(8,128)(2,1)} %get-tuple-element.8), calls=%async_computation.2 | async-start | bytes 2359296 | tf_op jit(solution)/shard_map/all_to_all | solution.py:145
  83.4 4.5 %collective-permute-start.2 = (f32[8,128]{1,0:T(8,128)S(1)}, f32[8,128]{1,0:T(8,128)S(1)}, u32[]{:S(2)}, u32[]{:S(2)}) collective-permute-start(f32[8,128]{1,0:T(8,128)S(1)} %get-tuple-element.7), channel_id=1, source_target_pairs={{0,3},{1,0},{2,1},{3,2},{4,7},{5,4},{6,5},{7,6},{8,11},{9,8},{10,9... | collective-permute-start | bytes 12296 | tf_op jit(solution)/shard_map/ppermute | solution.py:156
  86.3 5.1 %collective-permute-start.1 = (f32[8,128]{1,0:T(8,128)S(1)}, f32[8,128]{1,0:T(8,128)S(1)}, u32[]{:S(2)}, u32[]{:S(2)}) collective-permute-start(f32[8,128]{1,0:T(8,128)S(1)} %get-tuple-element.7), channel_id=1, source_target_pairs={{0,2},{1,3},{2,0},{3,1},{4,6},{5,7},{6,4},{7,5},{8,10},{9,11},{10,... | collective-permute-start | bytes 12296 | tf_op jit(solution)/shard_map/ppermute | solution.py:156
  87.1 4.8 %collective-permute-start = (f32[8,128]{1,0:T(8,128)S(1)}, f32[8,128]{1,0:T(8,128)S(1)}, u32[]{:S(2)}, u32[]{:S(2)}) collective-permute-start(f32[8,128]{1,0:T(8,128)S(1)} %get-tuple-element.7), channel_id=1, source_target_pairs={{0,1},{1,2},{2,3},{3,0},{4,5},{5,6},{6,7},{7,4},{8,9},{9,10},{10,1... | collective-permute-start | bytes 12296 | tf_op jit(solution)/shard_map/ppermute | solution.py:156
  91.9 4.7 %collective-permute-start.5 = (f32[8,128]{1,0:T(8,128)S(1)}, f32[8,128]{1,0:T(8,128)S(1)}, u32[]{:S(2)}, u32[]{:S(2)}) collective-permute-start(f32[8,128]{1,0:T(8,128)S(1)} %add_add_fusion.3), channel_id=1, source_target_pairs={{0,24},{4,28},{8,0},{12,4},{16,8},{20,12},{24,16},{28,20},{32,56},... | collective-permute-start | bytes 12296 | tf_op jit(solution)/shard_map/ppermute | solution.py:156
  92.4 5.1 %collective-permute-start.4 = (f32[8,128]{1,0:T(8,128)S(1)}, f32[8,128]{1,0:T(8,128)S(1)}, u32[]{:S(2)}, u32[]{:S(2)}) collective-permute-start(f32[8,128]{1,0:T(8,128)S(1)} %add_add_fusion.3), channel_id=1, source_target_pairs={{0,16},{4,20},{8,24},{12,28},{16,0},{20,4},{24,8},{28,12},{32,48},... | collective-permute-start | bytes 12296 | tf_op jit(solution)/shard_map/ppermute | solution.py:156
  94.8 3.9 %collective-permute-start.3 = (f32[8,128]{1,0:T(8,128)S(1)}, f32[8,128]{1,0:T(8,128)S(1)}, u32[]{:S(2)}, u32[]{:S(2)}) collective-permute-start(f32[8,128]{1,0:T(8,128)S(1)} %add_add_fusion.3), channel_id=1, source_target_pairs={{0,8},{4,12},{8,16},{12,20},{16,24},{20,28},{24,0},{28,4},{32,40},... | collective-permute-start | bytes 12296 | tf_op jit(solution)/shard_map/ppermute | solution.py:156
  98.7 12.1 %collective-permute-start.8 = (f32[8,128]{1,0:T(8,128)S(1)}, f32[8,128]{1,0:T(8,128)S(1)}, u32[]{:S(2)}, u32[]{:S(2)}) collective-permute-start(f32[8,128]{1,0:T(8,128)S(1)} %add_add_fusion.2), channel_id=1, source_target_pairs={{0,36},{4,32},{8,44},{12,40},{16,52},{20,48},{24,60},{28,56},{32,4... | collective-permute-start | bytes 12296 | tf_op jit(solution)/shard_map/ppermute | solution.py:156
  98.7 12.6 %collective-permute-start.7 = (f32[8,128]{1,0:T(8,128)S(1)}, f32[8,128]{1,0:T(8,128)S(1)}, u32[]{:S(2)}, u32[]{:S(2)}) collective-permute-start(f32[8,128]{1,0:T(8,128)S(1)} %add_add_fusion.2), channel_id=1, source_target_pairs={{0,32},{4,36},{8,40},{12,44},{16,48},{20,52},{24,56},{28,60},{32,0... | collective-permute-start | bytes 12296 | tf_op jit(solution)/shard_map/ppermute | solution.py:156
  100.2 11.1 %collective-permute-start.6 = (f32[8,128]{1,0:T(8,128)S(1)}, f32[8,128]{1,0:T(8,128)S(1)}, u32[]{:S(2)}, u32[]{:S(2)}) collective-permute-start(f32[8,128]{1,0:T(8,128)S(1)} %add_add_fusion.2), channel_id=1, source_target_pairs={{0,4},{4,0},{8,12},{12,8},{16,20},{20,16},{24,28},{28,24},{32,36},... | collective-permute-start | bytes 12296 | tf_op jit(solution)/shard_map/ppermute | solution.py:156
  111.4 7.3 %collective-permute-start.11 = (f32[8,128]{1,0:T(8,128)S(1)}, f32[8,128]{1,0:T(8,128)S(1)}, u32[]{:S(2)}, u32[]{:S(2)}) collective-permute-start(f32[8,128]{1,0:T(8,128)S(1)} %add_add_fusion.1), channel_id=1, source_target_pairs={{0,192},{64,0},{128,64},{192,128},{1,193},{65,1},{129,65},{193,129... | collective-permute-start | bytes 12296 | tf_op jit(solution)/shard_map/ppermute | solution.py:156
  114.0 7.5 %collective-permute-start.10 = (f32[8,128]{1,0:T(8,128)S(1)}, f32[8,128]{1,0:T(8,128)S(1)}, u32[]{:S(2)}, u32[]{:S(2)}) collective-permute-start(f32[8,128]{1,0:T(8,128)S(1)} %add_add_fusion.1), channel_id=1, source_target_pairs={{0,128},{64,192},{128,0},{192,64},{1,129},{65,193},{129,1},{193,65... | collective-permute-start | bytes 12296 | tf_op jit(solution)/shard_map/ppermute | solution.py:156
  116.1 5.7 %collective-permute-start.9 = (f32[8,128]{1,0:T(8,128)S(1)}, f32[8,128]{1,0:T(8,128)S(1)}, u32[]{:S(2)}, u32[]{:S(2)}) collective-permute-start(f32[8,128]{1,0:T(8,128)S(1)} %add_add_fusion.1), channel_id=1, source_target_pairs={{0,64},{64,128},{128,192},{192,0},{1,65},{65,129},{129,193},{193,1... | collective-permute-start | bytes 12296 | tf_op jit(solution)/shard_map/ppermute | solution.py:156

commit v3 on v2

--- a/solution.py
+++ b/solution.py
@@ -78,21 +78,22 @@
 
 
 def dot3(a, b):
-    return dot(a[0], b[0]) + (dot(a[0], b[1]) + dot(a[1], b[0]))
-
-
-def root(stat, eye):
-    damped = stat + EPS_DAMP * eye
-    total = jnp.sum(damped * damped, keepdims=True)
-    norm = jnp.sqrt(total)
-    n = damped * (1.0 / norm)
-    n_split = split(n)
-    n2 = dot3(n_split, n_split)
-    q = split(1.5625 * eye - 2.5 * n + n2)
-    h = split(1.25 * n - n2)
-    r = split(dot3(q, q))
-    product = 1.5625 * eye - 1.25 * n - dot3(h, r)
-    return product * lax.rsqrt(jnp.sqrt(0.25 * norm))
+    return dot(
+        jnp.concatenate([a[0], a[0], a[1]], axis=1), jnp.concatenate([b[0], b[1], b[0]], axis=0)
+    )
+
+
+def roots(stats, eye):
+    damped = [stat + EPS_DAMP * eye for stat in stats]
+    norms = [jnp.sqrt(jnp.sum(a * a, keepdims=True)) for a in damped]
+    ns = [a * (1.0 / norm) for a, norm in zip(damped, norms)]
+    n_splits = [split(n) for n in ns]
+    n2s = [dot3(n, n) for n in n_splits]
+    qs = [split(1.5625 * eye - 2.5 * n + n2) for n, n2 in zip(ns, n2s)]
+    hs = [split(1.25 * n - n2) for n, n2 in zip(ns, n2s)]
+    rs = [split(dot3(q, q)) for q in qs]
+    products = [1.5625 * eye - 1.25 * n - dot3(h, r) for n, h, r in zip(ns, hs, rs)]
+    return [p * lax.rsqrt(jnp.sqrt(0.25 * norm)) for p, norm in zip(products, norms)]
 
 
 def owner_kernel(me_ref, place_ref, got_ref, left_ref, right_ref, new_left_ref, new_right_ref, coded_ref,
@@ -112,9 +113,9 @@
     new_left_ref[0] = left
     right = BETA * right_ref[0] + dot(turned, block)
     new_right_ref[0] = right
-    left_root = split(root(left, eye))
+    left_root, right_root = (split(p) for p in roots((left, right), eye))
     half = split(dot(left_root[0], block) + dot(left_root[1], block))
-    raw = dot3(half, split(root(right, eye)))
+    raw = dot3(half, right_root)
     wide = block.astype(jnp.float32)
     grad_sq = jnp.sum(wide * wide, keepdims=True)
     update_sq = jnp.sum(raw * raw, keepdims=True)
@@ -145,16 +146,14 @@
     return lax.all_to_all(x, axes, split_axis=0, concat_axis=0, tiled=True)
 
 
+def add_permuted(x, axis, perms):
+    return sum([lax.ppermute(x, axis, perm) for perm in perms], x)
+
+
 def sum_everywhere(x):
-    stages = [
-        ("mp", [[(d, (d + s) % SHARDS) for d in range(SHARDS)] for s in (1, 2, 3)]),
-        ("r", [[(d, d // 8 * 8 + (d + s) % 8) for d in range(MEMBERS)] for s in (2, 4, 6)]),
-        ("r", [[(d, d ^ s) for d in range(MEMBERS)] for s in (1, 8, 9)]),
-        ("g", [[(d, (d + s) % GROUPS) for d in range(GROUPS)] for s in (1, 2, 3)]),
-    ]
-    for axis, perms in stages:
-        got = [lax.ppermute(x, axis, perm) for perm in perms]
-        x = (x + got[0]) + (got[1] + got[2])
+    x = add_permuted(x, "mp", [[(d, (d + s) % SHARDS) for d in range(SHARDS)] for s in range(1, 4)])
+    x = add_permuted(x, "r", [[(d, d ^ s) for d in range(MEMBERS)] for s in range(1, 8)])
+    x = add_permuted(x, ("g", "r"), [[(d, d ^ (8 * s)) for d in range(OWNERS)] for s in range(1, 8)])
     return x
 
 
@@ -204,7 +203,7 @@
             pl.BlockSpec((8, 128), lambda k: (0, 0)),
         ],
         scratch_shapes=[pltpu.VMEM((BLOCK, 128), jnp.float32)],
-        compiler_params=params(40),
+        compiler_params=params(58),
         cost_estimate=pl.CostEstimate(
             flops=50 * 2 * BLOCK**3, bytes_accessed=12 * MIB, transcendentals=0
         ),

time: 139 us -> 137 us (0.986)
  waiting for transfers between devices: 55.5 us -> 45.3 us
  starting transfers between devices: 41.2 us -> 49.5 us
    ppermute x12 -> x17, waiting for transfers between devices: 19.9 us -> 9.72 us  [add_permuted(): return sum([lax.ppermute(x, axis, perm) for perm in perms], x)]
    ppermute x12 -> x17, starting transfers between devices: 18.5 us -> 26.7 us  [add_permuted(): return sum([lax.ppermute(x, axis, perm) for perm in perms], x)]
    unnamed x7 -> x11, local copies, waits for them, and re-layouts: 2.98 us -> 2.35 us
  transfers between devices with their start and end apart: 15 -> 20, of which waited for: 10 -> 9; matrix products, arithmetic and copies ran while one was open for 0% -> 0% of each run, Pallas kernels for 1% -> 1%
where the time goes in v3:
time: 137 us
  starting transfers between devices  49.5 us (36%)
  waiting for transfers between devices  45.3 us (33%)
  Pallas kernels  23.2 us (17%)
  blocking collectives  15.5 us (11%)
  local copies, waits for them, and re-layouts  2.35 us (2%)
    all_to_all x3, waiting for transfers between devices, exchange(): return lax.all_to_all(x, axes, split_axis=0, concat_axis=0, tiled=True)  35.6 us
    ppermute x17, starting transfers between devices, add_permuted(): return sum([lax.ppermute(x, axis, perm) for perm in perms], x)  26.7 us
    all_to_all x3, starting transfers between devices, exchange(): return lax.all_to_all(x, axes, split_axis=0, concat_axis=0, tiled=True)  22.8 us
    pallas_call x1, Pallas kernels, shards(): pl.pallas_call(owner_kernel, grid=(SLOTS,), out_shape=[stat_shape, stat_s...  19.2 us
    all_to_all x1, blocking collectives, exchange(): return lax.all_to_all(x, axes, split_axis=0, concat_axis=0, tiled=True)  15.5 us
    ppermute x17, waiting for transfers between devices, add_permuted(): return sum([lax.ppermute(x, axis, perm) for perm in perms], x)  9.72 us
  transfers between devices with their start and end apart: 20, of which 9 were waited for; matrix products, arithmetic and copies ran while one was open for 0% of the time, Pallas kernels for 1%

profile of v3, /device:TPU:8, one launch (start us, length us, event | category | flops | bytes accessed | tf_op | source)
XLA Modules:
  0.0 136.8 jit_solution(11526295622904743996)
XLA Ops:
  0.6 8.5 %all-to-all-start = ((bf16[4,8,4096]{2,1,0:T(8,128)(2,1)}), bf16[4,8,4096]{2,1,0:T(8,128)(2,1)S(1)}, u32[]{:S(2)}, u32[]{:S(2)}) async-start(bf16[4,8,4096]{2,1,0:T(8,128)(2,1)} %bitcast.11), calls=%async_computation | async-start | bytes 524288 | tf_op jit(solution)/shard_map/all_to_all | solution.py:146
  9.1 0.7 copy-done.2
  9.8 1.5 %places.1.place_ref = s32[32]{0:T(128)S(1)} custom-call(s32[1]{0:T(128)} %bitcast.shard_ref, s32[4,32]{1,0:T(4,128)S(1)} %copy-done.2), custom_call_target="tpu_custom_call" | custom-call | flops 1000 | bytes 1000 | tf_op jit(solution)/shard_map/places/pallas_call | solution.py:165
  11.3 8.6 %all-to-all-done.in_ref = bf16[4,8,4096]{2,1,0:T(8,128)(2,1)S(1)} async-done(((bf16[4,8,4096]{2,1,0:T(8,128)(2,1)}), bf16[4,8,4096]{2,1,0:T(8,128)(2,1)S(1)}, u32[]{:S(2)}, u32[]{:S(2)}) %all-to-all-start) | async-done | bytes 262176 | tf_op jit(solution)/shard_map/all_to_all | solution.py:146
  19.8 1.7 %route.1 = bf16[64,8,1024]{2,1,0:T(8,128)(2,1)} custom-call(s32[32]{0:T(128)S(1)} %places.1.place_ref, bf16[4,8,4096]{2,1,0:T(8,128)(2,1)S(1)} %all-to-all-done.in_ref), custom_call_target="tpu_custom_call" | custom-call | tf_op jit(solution)/shard_map/route/pallas_call | solution.py:176
  21.5 6.6 %all-to-all-start.1 = ((bf16[64,8,1024]{2,1,0:T(8,128)(2,1)}), bf16[64,8,1024]{2,1,0:T(8,128)(2,1)S(1)}, u32[]{:S(2)}, u32[]{:S(2)}) async-start(bf16[64,8,1024]{2,1,0:T(8,128)(2,1)} %route.1), calls=%async_computation.1 | async-start | bytes 2097152 | tf_op jit(solution)/shard_map/all_to_all | solution.py:146
  28.2 27.1 %all-to-all-done.1 = bf16[64,8,1024]{2,1,0:T(8,128)(2,1)S(1)} async-done(((bf16[64,8,1024]{2,1,0:T(8,128)(2,1)}), bf16[64,8,1024]{2,1,0:T(8,128)(2,1)S(1)}, u32[]{:S(2)}, u32[]{:S(2)}) %all-to-all-start.1) | async-done | bytes 1048608 | tf_op jit(solution)/shard_map/all_to_all | solution.py:146
  55.2 0.9 copy-done.3
  56.2 19.2 %owner.1 = (f32[2,512,512]{2,1,0:T(8,128)}, f32[2,512,512]{2,1,0:T(8,128)}, s16[64,8,1152]{2,1,0:T(8,128)(2,1)}, f32[8,128]{1,0:T(8,128)}) custom-call(s32[1]{0:T(128)} %bitcast.1.me_ref, s32[32]{0:T(128)} %copy-done, bf16[512,1024]{1,0:T(8,128)(2,1)} %bitcast.9, f32[2,512,512]{2,1,0:T(8,128)} %bitcast.12, f32[2,512,512]{2,1,0:T(8,128)} %bitcast.13), custom_call_target="tpu_custom_call" | custom-call | flops 13421772800 | bytes 12582912 | tf_op jit(solution)/shard_map/owner/pallas_call | solution.py:189
  75.4 0.0 copy-start.4
  75.4 7.7 %all-to-all-start.2 = ((s16[64,8,1152]{2,1,0:T(8,128)(2,1)}), s16[64,8,1152]{2,1,0:T(8,128)(2,1)S(1)}, u32[]{:S(2)}, u32[]{:S(2)}) async-start(s16[64,8,1152]{2,1,0:T(8,128)(2,1)} %get-tuple-element.8), calls=%async_computation.2 | async-start | bytes 2359296 | tf_op jit(solution)/shard_map/all_to_all | solution.py:146
  83.1 2.8 %collective-permute-start.2 = (f32[8,128]{1,0:T(8,128)S(1)}, f32[8,128]{1,0:T(8,128)S(1)}, u32[]{:S(2)}, u32[]{:S(2)}) collective-permute-start(f32[8,128]{1,0:T(8,128)S(1)} %copy-done.4), channel_id=1, source_target_pairs={{0,3},{1,0},{2,1},{3,2},{4,7},{5,4},{6,5},{7,6},{8,11},{9,8},{10,9... | collective-permute-start | bytes 12296 | tf_op jit(solution)/shard_map/ppermute | solution.py:150
  86.0 0.8 collective-permute-start.1
  86.8 0.9 collective-permute-start
  87.6 0.0 collective-permute-done.2
  87.6 3.4 %collective-permute-done.1 = f32[8,128]{1,0:T(8,128)S(1)} collective-permute-done((f32[8,128]{1,0:T(8,128)S(1)}, f32[8,128]{1,0:T(8,128)S(1)}, u32[]{:S(2)}, u32[]{:S(2)}) %collective-permute-start.1) | collective-permute-done | bytes 4128 | tf_op jit(solution)/shard_map/ppermute | solution.py:150
  91.1 0.5 collective-permute-done
  91.6 0.0 collective-permute-start.9
  91.6 1.7 %collective-permute-start.8 = (f32[8,128]{1,0:T(8,128)S(1)}, f32[8,128]{1,0:T(8,128)S(1)}, u32[]{:S(2)}, u32[]{:S(2)}) collective-permute-start(f32[8,128]{1,0:T(8,128)S(1)} %add_add_fusion.2), channel_id=1, source_target_pairs={{0,24},{4,28},{8,16},{12,20},{16,8},{20,12},{24,0},{28,4},{32,56},... | collective-permute-start | bytes 12296 | tf_op jit(solution)/shard_map/ppermute | solution.py:150
  93.3 3.0 %collective-permute-start.7 = (f32[8,128]{1,0:T(8,128)S(1)}, f32[8,128]{1,0:T(8,128)S(1)}, u32[]{:S(2)}, u32[]{:S(2)}) collective-permute-start(f32[8,128]{1,0:T(8,128)S(1)} %add_add_fusion.2), channel_id=1, source_target_pairs={{0,20},{4,16},{8,28},{12,24},{16,4},{20,0},{24,12},{28,8},{32,52},... | collective-permute-start | bytes 12296 | tf_op jit(solution)/shard_map/ppermute | solution.py:150
  96.4 0.2 collective-permute-start.6
  96.6 1.5 %collective-permute-start.5 = (f32[8,128]{1,0:T(8,128)S(1)}, f32[8,128]{1,0:T(8,128)S(1)}, u32[]{:S(2)}, u32[]{:S(2)}) collective-permute-start(f32[8,128]{1,0:T(8,128)S(1)} %add_add_fusion.2), channel_id=1, source_target_pairs={{0,12},{4,8},{8,4},{12,0},{16,28},{20,24},{24,20},{28,16},{32,44},... | collective-permute-start | bytes 12296 | tf_op jit(solution)/shard_map/ppermute | solution.py:150
  98.1 0.0 collective-permute-done.9
  98.1 0.2 collective-permute-start.4
  98.3 0.0 collective-permute-done.8
  98.3 0.2 collective-permute-start.3
  98.5 0.0 collective-permute-done.7
  98.5 3.0 %collective-permute-done.6 = f32[8,128]{1,0:T(8,128)S(1)} collective-permute-done((f32[8,128]{1,0:T(8,128)S(1)}, f32[8,128]{1,0:T(8,128)S(1)}, u32[]{:S(2)}, u32[]{:S(2)}) %collective-permute-start.6) | collective-permute-done | bytes 4128 | tf_op jit(solution)/shard_map/ppermute | solution.py:150
  101.5 0.0 collective-permute-done.5
  101.5 0.3 collective-permute-done.4
  101.8 3.0 %collective-permute-start.16 = (f32[8,128]{1,0:T(8,128)S(1)}, f32[8,128]{1,0:T(8,128)S(1)}, u32[]{:S(2)}, u32[]{:S(2)}) collective-permute-start(f32[8,128]{1,0:T(8,128)S(1)} %add_add_fusion.1), channel_id=1, source_target_pairs={{0,224},{4,228},{8,232},{12,236},{16,240},{20,244},{24,248},{28,25... | collective-permute-start | bytes 12296 | tf_op jit(solution)/shard_map/ppermute | solution.py:150
  104.8 2.3 %collective-permute-start.15 = (f32[8,128]{1,0:T(8,128)S(1)}, f32[8,128]{1,0:T(8,128)S(1)}, u32[]{:S(2)}, u32[]{:S(2)}) collective-permute-start(f32[8,128]{1,0:T(8,128)S(1)} %add_add_fusion.1), channel_id=1, source_target_pairs={{0,192},{4,196},{8,200},{12,204},{16,208},{20,212},{24,216},{28,22... | collective-permute-start | bytes 12296 | tf_op jit(solution)/shard_map/ppermute | solution.py:150
  107.1 3.4 %collective-permute-start.14 = (f32[8,128]{1,0:T(8,128)S(1)}, f32[8,128]{1,0:T(8,128)S(1)}, u32[]{:S(2)}, u32[]{:S(2)}) collective-permute-start(f32[8,128]{1,0:T(8,128)S(1)} %add_add_fusion.1), channel_id=1, source_target_pairs={{0,160},{4,164},{8,168},{12,172},{16,176},{20,180},{24,184},{28,18... | collective-permute-start | bytes 12296 | tf_op jit(solution)/shard_map/ppermute | solution.py:150
  110.5 2.3 %collective-permute-start.13 = (f32[8,128]{1,0:T(8,128)S(1)}, f32[8,128]{1,0:T(8,128)S(1)}, u32[]{:S(2)}, u32[]{:S(2)}) collective-permute-start(f32[8,128]{1,0:T(8,128)S(1)} %add_add_fusion.1), channel_id=1, source_target_pairs={{0,128},{4,132},{8,136},{12,140},{16,144},{20,148},{24,152},{28,15... | collective-permute-start | bytes 12296 | tf_op jit(solution)/shard_map/ppermute | solution.py:150
  112.7 2.4 %collective-permute-start.12 = (f32[8,128]{1,0:T(8,128)S(1)}, f32[8,128]{1,0:T(8,128)S(1)}, u32[]{:S(2)}, u32[]{:S(2)}) collective-permute-start(f32[8,128]{1,0:T(8,128)S(1)} %add_add_fusion.1), channel_id=1, source_target_pairs={{0,96},{4,100},{8,104},{12,108},{16,112},{20,116},{24,120},{28,124... | collective-permute-start | bytes 12296 | tf_op jit(solution)/shard_map/ppermute | solution.py:150
  115.1 0.0 collective-permute-done.16
  115.1 0.2 collective-permute-start.11
  115.3 0.0 collective-permute-done.15
  115.3 1.8 %collective-permute-start.10 = (f32[8,128]{1,0:T(8,128)S(1)}, f32[8,128]{1,0:T(8,128)S(1)}, u32[]{:S(2)}, u32[]{:S(2)}) collective-permute-start(f32[8,128]{1,0:T(8,128)S(1)} %add_add_fusion.1), channel_id=1, source_target_pairs={{0,32},{4,36},{8,40},{12,44},{16,48},{20,52},{24,56},{28,60},{32,0... | collective-permute-start | bytes 12296 | tf_op jit(solution)/shard_map/ppermute | solution.py:150
  117.1 0.0 collective-permute-done.14
  117.1 0.9 collective-permute-done.13
  118.0 0.1 collective-permute-done.12
  118.1 1.5 %collective-permute-done.11 = f32[8,128]{1,0:T(8,128)S(1)} collective-permute-done((f32[8,128]{1,0:T(8,128)S(1)}, f32[8,128]{1,0:T(8,128)S(1)}, u32[]{:S(2)}, u32[]{:S(2)}) %collective-permute-start.11) | collective-permute-done | bytes 4128 | tf_op jit(solution)/shard_map/ppermute | solution.py:150
  119.6 0.0 collective-permute-done.10
  119.6 0.0 all-to-all-done.2.in_ref
  119.6 0.9 collect.1
  120.5 15.5 %all_to_all.20 = bf16[4,8,4096]{2,1,0:T(8,128)(2,1)S(1)} all-to-all(bf16[4,8,4096]{2,1,0:T(8,128)(2,1)S(1)} %collect.1), channel_id=1, replica_groups=mesh['g'=4,'r'=16,'mp'=4] {'g'}, dimensions={0} | all-to-all | bytes 524288 | tf_op jit(solution)/shard_map/all_to_all | solution.py:146
  136.1 0.7 copy.8
  (11 shorter events, 0.0 us)
Async XLA Ops:
  0.6 19.2 %all-to-all-start = ((bf16[4,8,4096]{2,1,0:T(8,128)(2,1)}), bf16[4,8,4096]{2,1,0:T(8,128)(2,1)S(1)}, u32[]{:S(2)}, u32[]{:S(2)}) async-start(bf16[4,8,4096]{2,1,0:T(8,128)(2,1)} %bitcast.11), calls=%async_computation | async-start | bytes 524288 | tf_op jit(solution)/shard_map/all_to_all | solution.py:146
  9.1 0.7 copy-start.2
  11.3 44.0 %copy-start = (s32[32]{0:T(128)}, s32[32]{0:T(128)S(1)}, u32[]{:S(2)}) copy-start(s32[32]{0:T(128)S(1)} %places.1.place_ref) | copy-start | bytes 388
  21.5 33.7 %all-to-all-start.1 = ((bf16[64,8,1024]{2,1,0:T(8,128)(2,1)}), bf16[64,8,1024]{2,1,0:T(8,128)(2,1)S(1)}, u32[]{:S(2)}, u32[]{:S(2)}) async-start(bf16[64,8,1024]{2,1,0:T(8,128)(2,1)} %route.1), calls=%async_computation.1 | async-start | bytes 2097152 | tf_op jit(solution)/shard_map/all_to_all | solution.py:146
  55.2 1.0 copy-start.3
  75.4 7.7 %copy-start.4 = (f32[8,128]{1,0:T(8,128)S(1)}, f32[8,128]{1,0:T(8,128)}, u32[]{:S(2)}) copy-start(f32[8,128]{1,0:T(8,128)} %get-tuple-element.7) | copy-start | bytes 12292
  75.4 44.2 %copy-start.1 = (s32[32]{0:T(128)S(1)}, s32[32]{0:T(128)}, u32[]{:S(2)}) copy-start(s32[32]{0:T(128)} %copy-done) | copy-start | bytes 388
  75.4 44.2 %all-to-all-start.2 = ((s16[64,8,1152]{2,1,0:T(8,128)(2,1)}), s16[64,8,1152]{2,1,0:T(8,128)(2,1)S(1)}, u32[]{:S(2)}, u32[]{:S(2)}) async-start(s16[64,8,1152]{2,1,0:T(8,128)(2,1)} %get-tuple-element.8), calls=%async_computation.2 | async-start | bytes 2359296 | tf_op jit(solution)/shard_map/all_to_all | solution.py:146
  83.1 4.5 %collective-permute-start.2 = (f32[8,128]{1,0:T(8,128)S(1)}, f32[8,128]{1,0:T(8,128)S(1)}, u32[]{:S(2)}, u32[]{:S(2)}) collective-permute-start(f32[8,128]{1,0:T(8,128)S(1)} %copy-done.4), channel_id=1, source_target_pairs={{0,3},{1,0},{2,1},{3,2},{4,7},{5,4},{6,5},{7,6},{8,11},{9,8},{10,9... | collective-permute-start | bytes 12296 | tf_op jit(solution)/shard_map/ppermute | solution.py:150
  86.0 5.1 %collective-permute-start.1 = (f32[8,128]{1,0:T(8,128)S(1)}, f32[8,128]{1,0:T(8,128)S(1)}, u32[]{:S(2)}, u32[]{:S(2)}) collective-permute-start(f32[8,128]{1,0:T(8,128)S(1)} %copy-done.4), channel_id=1, source_target_pairs={{0,2},{1,3},{2,0},{3,1},{4,6},{5,7},{6,4},{7,5},{8,10},{9,11},{10,... | collective-permute-start | bytes 12296 | tf_op jit(solution)/shard_map/ppermute | solution.py:150
  86.8 4.8 %collective-permute-start = (f32[8,128]{1,0:T(8,128)S(1)}, f32[8,128]{1,0:T(8,128)S(1)}, u32[]{:S(2)}, u32[]{:S(2)}) collective-permute-start(f32[8,128]{1,0:T(8,128)S(1)} %copy-done.4), channel_id=1, source_target_pairs={{0,1},{1,2},{2,3},{3,0},{4,5},{5,6},{6,7},{7,4},{8,9},{9,10},{10,1... | collective-permute-start | bytes 12296 | tf_op jit(solution)/shard_map/ppermute | solution.py:150
  91.6 6.5 %collective-permute-start.9 = (f32[8,128]{1,0:T(8,128)S(1)}, f32[8,128]{1,0:T(8,128)S(1)}, u32[]{:S(2)}, u32[]{:S(2)}) collective-permute-start(f32[8,128]{1,0:T(8,128)S(1)} %add_add_fusion.2), channel_id=1, source_target_pairs={{0,28},{4,24},{8,20},{12,16},{16,12},{20,8},{24,4},{28,0},{32,60},... | collective-permute-start | bytes 12296 | tf_op jit(solution)/shard_map/ppermute | solution.py:150
  91.6 6.7 %collective-permute-start.8 = (f32[8,128]{1,0:T(8,128)S(1)}, f32[8,128]{1,0:T(8,128)S(1)}, u32[]{:S(2)}, u32[]{:S(2)}) collective-permute-start(f32[8,128]{1,0:T(8,128)S(1)} %add_add_fusion.2), channel_id=1, source_target_pairs={{0,24},{4,28},{8,16},{12,20},{16,8},{20,12},{24,0},{28,4},{32,56},... | collective-permute-start | bytes 12296 | tf_op jit(solution)/shard_map/ppermute | solution.py:150
  93.3 5.2 %collective-permute-start.7 = (f32[8,128]{1,0:T(8,128)S(1)}, f32[8,128]{1,0:T(8,128)S(1)}, u32[]{:S(2)}, u32[]{:S(2)}) collective-permute-start(f32[8,128]{1,0:T(8,128)S(1)} %add_add_fusion.2), channel_id=1, source_target_pairs={{0,20},{4,16},{8,28},{12,24},{16,4},{20,0},{24,12},{28,8},{32,52},... | collective-permute-start | bytes 12296 | tf_op jit(solution)/shard_map/ppermute | solution.py:150
  96.4 5.1 %collective-permute-start.6 = (f32[8,128]{1,0:T(8,128)S(1)}, f32[8,128]{1,0:T(8,128)S(1)}, u32[]{:S(2)}, u32[]{:S(2)}) collective-permute-start(f32[8,128]{1,0:T(8,128)S(1)} %add_add_fusion.2), channel_id=1, source_target_pairs={{0,16},{4,20},{8,24},{12,28},{16,0},{20,4},{24,8},{28,12},{32,48},... | collective-permute-start | bytes 12296 | tf_op jit(solution)/shard_map/ppermute | solution.py:150
  96.6 4.9 %collective-permute-start.5 = (f32[8,128]{1,0:T(8,128)S(1)}, f32[8,128]{1,0:T(8,128)S(1)}, u32[]{:S(2)}, u32[]{:S(2)}) collective-permute-start(f32[8,128]{1,0:T(8,128)S(1)} %add_add_fusion.2), channel_id=1, source_target_pairs={{0,12},{4,8},{8,4},{12,0},{16,28},{20,24},{24,20},{28,16},{32,44},... | collective-permute-start | bytes 12296 | tf_op jit(solution)/shard_map/ppermute | solution.py:150
  98.1 3.7 %collective-permute-start.4 = (f32[8,128]{1,0:T(8,128)S(1)}, f32[8,128]{1,0:T(8,128)S(1)}, u32[]{:S(2)}, u32[]{:S(2)}) collective-permute-start(f32[8,128]{1,0:T(8,128)S(1)} %add_add_fusion.2), channel_id=1, source_target_pairs={{0,8},{4,12},{8,0},{12,4},{16,24},{20,28},{24,16},{28,20},{32,40},... | collective-permute-start | bytes 12296 | tf_op jit(solution)/shard_map/ppermute | solution.py:150
  98.3 3.5 %collective-permute-start.3 = (f32[8,128]{1,0:T(8,128)S(1)}, f32[8,128]{1,0:T(8,128)S(1)}, u32[]{:S(2)}, u32[]{:S(2)}) collective-permute-start(f32[8,128]{1,0:T(8,128)S(1)} %add_add_fusion.2), channel_id=1, source_target_pairs={{0,4},{4,0},{8,12},{12,8},{16,20},{20,16},{24,28},{28,24},{32,36},... | collective-permute-start | bytes 12296 | tf_op jit(solution)/shard_map/ppermute | solution.py:150
  101.8 13.3 %collective-permute-start.16 = (f32[8,128]{1,0:T(8,128)S(1)}, f32[8,128]{1,0:T(8,128)S(1)}, u32[]{:S(2)}, u32[]{:S(2)}) collective-permute-start(f32[8,128]{1,0:T(8,128)S(1)} %add_add_fusion.1), channel_id=1, source_target_pairs={{0,224},{4,228},{8,232},{12,236},{16,240},{20,244},{24,248},{28,25... | collective-permute-start | bytes 12296 | tf_op jit(solution)/shard_map/ppermute | solution.py:150
  104.8 10.6 %collective-permute-start.15 = (f32[8,128]{1,0:T(8,128)S(1)}, f32[8,128]{1,0:T(8,128)S(1)}, u32[]{:S(2)}, u32[]{:S(2)}) collective-permute-start(f32[8,128]{1,0:T(8,128)S(1)} %add_add_fusion.1), channel_id=1, source_target_pairs={{0,192},{4,196},{8,200},{12,204},{16,208},{20,212},{24,216},{28,22... | collective-permute-start | bytes 12296 | tf_op jit(solution)/shard_map/ppermute | solution.py:150
  107.1 10.1 %collective-permute-start.14 = (f32[8,128]{1,0:T(8,128)S(1)}, f32[8,128]{1,0:T(8,128)S(1)}, u32[]{:S(2)}, u32[]{:S(2)}) collective-permute-start(f32[8,128]{1,0:T(8,128)S(1)} %add_add_fusion.1), channel_id=1, source_target_pairs={{0,160},{4,164},{8,168},{12,172},{16,176},{20,180},{24,184},{28,18... | collective-permute-start | bytes 12296 | tf_op jit(solution)/shard_map/ppermute | solution.py:150
  110.5 7.5 %collective-permute-start.13 = (f32[8,128]{1,0:T(8,128)S(1)}, f32[8,128]{1,0:T(8,128)S(1)}, u32[]{:S(2)}, u32[]{:S(2)}) collective-permute-start(f32[8,128]{1,0:T(8,128)S(1)} %add_add_fusion.1), channel_id=1, source_target_pairs={{0,128},{4,132},{8,136},{12,140},{16,144},{20,148},{24,152},{28,15... | collective-permute-start | bytes 12296 | tf_op jit(solution)/shard_map/ppermute | solution.py:150
  112.7 5.4 %collective-permute-start.12 = (f32[8,128]{1,0:T(8,128)S(1)}, f32[8,128]{1,0:T(8,128)S(1)}, u32[]{:S(2)}, u32[]{:S(2)}) collective-permute-start(f32[8,128]{1,0:T(8,128)S(1)} %add_add_fusion.1), channel_id=1, source_target_pairs={{0,96},{4,100},{8,104},{12,108},{16,112},{20,116},{24,120},{28,124... | collective-permute-start | bytes 12296 | tf_op jit(solution)/shard_map/ppermute | solution.py:150
  115.1 4.5 %collective-permute-start.11 = (f32[8,128]{1,0:T(8,128)S(1)}, f32[8,128]{1,0:T(8,128)S(1)}, u32[]{:S(2)}, u32[]{:S(2)}) collective-permute-start(f32[8,128]{1,0:T(8,128)S(1)} %add_add_fusion.1), channel_id=1, source_target_pairs={{0,64},{4,68},{8,72},{12,76},{16,80},{20,84},{24,88},{28,92},{32,9... | collective-permute-start | bytes 12296 | tf_op jit(solution)/shard_map/ppermute | solution.py:150
  115.3 4.3 %collective-permute-start.10 = (f32[8,128]{1,0:T(8,128)S(1)}, f32[8,128]{1,0:T(8,128)S(1)}, u32[]{:S(2)}, u32[]{:S(2)}) collective-permute-start(f32[8,128]{1,0:T(8,128)S(1)} %add_add_fusion.1), channel_id=1, source_target_pairs={{0,32},{4,36},{8,40},{12,44},{16,48},{20,52},{24,56},{28,60},{32,0... | collective-permute-start | bytes 12296 | tf_op jit(solution)/shard_map/ppermute | solution.py:150

commit v4 on v3

--- a/solution.py
+++ b/solution.py
@@ -77,28 +77,36 @@
     return high, (x - high.astype(jnp.float32)).astype(jnp.bfloat16)
 
 
-def dot3(a, b):
+def dot3(a, b, columns):
     return dot(
-        jnp.concatenate([a[0], a[0], a[1]], axis=1), jnp.concatenate([b[0], b[1], b[0]], axis=0)
+        jnp.concatenate([a[0][...], a[0][...], a[1][...]], axis=1),
+        jnp.concatenate([b[0][:, columns], b[1][:, columns], b[0][:, columns]], axis=0),
     )
 
 
-def roots(stats, eye):
-    damped = [stat + EPS_DAMP * eye for stat in stats]
-    norms = [jnp.sqrt(jnp.sum(a * a, keepdims=True)) for a in damped]
-    ns = [a * (1.0 / norm) for a, norm in zip(damped, norms)]
-    n_splits = [split(n) for n in ns]
-    n2s = [dot3(n, n) for n in n_splits]
-    qs = [split(1.5625 * eye - 2.5 * n + n2) for n, n2 in zip(ns, n2s)]
-    hs = [split(1.25 * n - n2) for n, n2 in zip(ns, n2s)]
-    rs = [split(dot3(q, q)) for q in qs]
-    products = [1.5625 * eye - 1.25 * n - dot3(h, r) for n, h, r in zip(ns, hs, rs)]
-    return [p * lax.rsqrt(jnp.sqrt(0.25 * norm)) for p, norm in zip(products, norms)]
+def put(pair, columns, x):
+    pair[0][:, columns], pair[1][:, columns] = split(x)
 
 
 def owner_kernel(me_ref, place_ref, got_ref, left_ref, right_ref, new_left_ref, new_right_ref, coded_ref,
-                 sums_ref, power_ref):
+                 sums_ref, power_ref, prev_ref, new_ref, n_ref, raw_ref, n_parts_ref, q_parts_ref,
+                 h_parts_ref, r_parts_ref, got_sem, new_sem):
     slot = pl.program_id(0)
+
+    def fetch(side, k):
+        source = (left_ref, right_ref)[side]
+        return pltpu.make_async_copy(source.at[k], prev_ref.at[side, k], got_sem.at[side, k])
+
+    def write(side, k):
+        target = (new_left_ref, new_right_ref)[side]
+        return pltpu.make_async_copy(new_ref.at[side, k], target.at[k], new_sem.at[side, k])
+
+    @pl.when(slot == 0)
+    def _():
+        for k in range(SLOTS):
+            for side in range(2):
+                fetch(side, k).start()
+
     wanted = me_ref[0] * SLOTS + slot
     used = place_ref[0] == wanted
     for b in range(1, BLOCKS):
@@ -106,21 +114,57 @@
     block = got_ref[...]
     block = jnp.where(used, block, jnp.zeros_like(block))
     turned = block.T
-    rows = lax.broadcasted_iota(jnp.int32, (BLOCK, BLOCK), 0)
-    columns = lax.broadcasted_iota(jnp.int32, (BLOCK, BLOCK), 1)
-    eye = jnp.where(rows == columns, 1.0, 0.0).astype(jnp.float32)
-    left = BETA * left_ref[0] + dot(block, turned)
-    new_left_ref[0] = left
-    right = BETA * right_ref[0] + dot(turned, block)
-    new_right_ref[0] = right
-    left_root, right_root = (split(p) for p in roots((left, right), eye))
-    half = split(dot(left_root[0], block) + dot(left_root[1], block))
-    raw = dot3(half, right_root)
+    halves = [pl.ds(0, BLOCK // 2), pl.ds(BLOCK // 2, BLOCK // 2)]
+    steps = [(columns, side) for columns in halves for side in range(2)]
+
+    def eye(columns, value):
+        rows = lax.broadcasted_iota(jnp.int32, (BLOCK, columns.size), 0)
+        lanes = lax.broadcasted_iota(jnp.int32, (BLOCK, columns.size), 1) + columns.start
+        return jnp.where(rows == lanes, jnp.float32(value), jnp.float32(0))
+
+    def pair(ref, side):
+        return ref.at[side, 0], ref.at[side, 1]
+
+    norms = []
+    for side in range(2):
+        gram = dot(block, turned) if side == 0 else dot(turned, block)
+        fetch(side, slot).wait()
+        stat = BETA * prev_ref[side, slot] + gram
+        new_ref[side, slot] = stat
+        write(side, slot).start()
+        damped = stat + eye(pl.ds(0, BLOCK), EPS_DAMP)
+        norm = jnp.sqrt(jnp.sum(damped * damped, keepdims=True))
+        n = damped * (1.0 / norm)
+        n_ref[side] = n
+        put(pair(n_parts_ref, side), slice(None), n)
+        norms.append(norm)
+    for columns, side in steps:
+        n = n_ref[side, :, columns]
+        n_parts = pair(n_parts_ref, side)
+        n2 = dot3(n_parts, n_parts, columns)
+        put(pair(q_parts_ref, side), columns, eye(columns, 1.5625) - 2.5 * n + n2)
+        put(pair(h_parts_ref, side), columns, 1.25 * n - n2)
+    for columns, side in steps:
+        q_parts = pair(q_parts_ref, side)
+        put(pair(r_parts_ref, side), columns, dot3(q_parts, q_parts, columns))
+    for columns, side in steps:
+        product = dot3(pair(h_parts_ref, side), pair(r_parts_ref, side), columns)
+        product = eye(columns, 1.5625) - 1.25 * n_ref[side, :, columns] - product
+        put(pair(n_parts_ref, side), columns, product * lax.rsqrt(jnp.sqrt(0.25 * norms[side])))
+    left_root = jnp.concatenate([n_parts_ref[0, 0], n_parts_ref[0, 1]], axis=1)
+    for columns in halves:
+        part = block[:, columns.start : columns.start + columns.size]
+        put(pair(q_parts_ref, 0), columns, dot(left_root, jnp.concatenate([part, part], axis=0)))
+    update_sq = jnp.zeros((1, 1), jnp.float32)
+    for columns in halves:
+        raw = dot3(pair(q_parts_ref, 0), pair(n_parts_ref, 1), columns)
+        raw_ref[:, columns] = raw
+        update_sq += jnp.sum(raw * raw, keepdims=True)
     wide = block.astype(jnp.float32)
     grad_sq = jnp.sum(wide * wide, keepdims=True)
-    update_sq = jnp.sum(raw * raw, keepdims=True)
     line = lax.broadcasted_iota(jnp.int32, sums_ref.shape, 0)
     sums = jnp.where(line == 0, grad_sq, update_sq)
+    raw = raw_ref[...]
     largest = jnp.max(jnp.abs(raw), axis=1, keepdims=True)
     power = jnp.ceil(jnp.log2(jnp.maximum(largest, 1e-30)) + 0.001) - 15.0
     coded = jnp.round(raw * jnp.exp2(-power)).astype(jnp.int32)
@@ -133,13 +177,16 @@
         sums_ref[...] = sums
         power_ref[...] = jnp.broadcast_to(power, power_ref.shape)
 
-    @pl.when(slot > 0)
+    @pl.when(slot == SLOTS - 1)
     def _():
         sums_ref[...] += sums
         lane = lax.broadcasted_iota(jnp.int32, power_ref.shape, 1)
         powers = jnp.where(lane < 64, power_ref[...], power).astype(jnp.int32)
         for p in range(OWNERS):
             coded_ref[p, :, pl.ds(SLOTS * BLOCK, 128)] = powers[p * LINES : (p + 1) * LINES].astype(jnp.int16)
+        for k in range(SLOTS):
+            for side in range(2):
+                write(side, k).wait()
 
 
 def exchange(x, axes):
@@ -153,7 +200,8 @@
 def sum_everywhere(x):
     x = add_permuted(x, "mp", [[(d, (d + s) % SHARDS) for d in range(SHARDS)] for s in range(1, 4)])
     x = add_permuted(x, "r", [[(d, d ^ s) for d in range(MEMBERS)] for s in range(1, 8)])
-    x = add_permuted(x, ("g", "r"), [[(d, d ^ (8 * s)) for d in range(OWNERS)] for s in range(1, 8)])
+    x = add_permuted(x, ("g", "r"), [[(d, d ^ (8 * s)) for d in range(OWNERS)] for s in range(1, 4)])
+    x = add_permuted(x, "g", [[(d, d ^ 2) for d in range(GROUPS)]])
     return x
 
 
@@ -183,7 +231,8 @@
     )(places, pieces)
     got = exchange(routed, ("r", "g")).reshape(BLOCK, SLOTS * BLOCK)
 
-    stat_spec = pl.BlockSpec((1, BLOCK, BLOCK), lambda k: (k, 0, 0))
+    stat_spec = pl.BlockSpec(memory_space=pl.ANY)
+    parts = pltpu.VMEM((2, 2, BLOCK, BLOCK), jnp.bfloat16)
     stat_shape = jax.ShapeDtypeStruct((SLOTS, BLOCK, BLOCK), jnp.float32)
     coded_shape = (OWNERS, LINES, SLOTS * BLOCK + 128)
     new_left, new_right, coded, sums = pl.pallas_call(
@@ -202,8 +251,20 @@
             pl.BlockSpec(coded_shape, lambda k: (0, 0, 0)),
             pl.BlockSpec((8, 128), lambda k: (0, 0)),
         ],
-        scratch_shapes=[pltpu.VMEM((BLOCK, 128), jnp.float32)],
-        compiler_params=params(58),
+        scratch_shapes=[
+            pltpu.VMEM((BLOCK, 128), jnp.float32),
+            pltpu.VMEM((2, SLOTS, BLOCK, BLOCK), jnp.float32),
+            pltpu.VMEM((2, SLOTS, BLOCK, BLOCK), jnp.float32),
+            pltpu.VMEM((2, BLOCK, BLOCK), jnp.float32),
+            pltpu.VMEM((BLOCK, BLOCK), jnp.float32),
+            parts,
+            parts,
+            parts,
+            parts,
+            pltpu.SemaphoreType.DMA((2, SLOTS)),
+            pltpu.SemaphoreType.DMA((2, SLOTS)),
+        ],
+        compiler_params=params(48),
         cost_estimate=pl.CostEstimate(
             flops=50 * 2 * BLOCK**3, bytes_accessed=12 * MIB, transcendentals=0
         ),

time: 137 us -> 136 us (level)
  starting transfers between devices: 49.5 us -> 42.7 us
  waiting for transfers between devices: 45.3 us -> 51.7 us
    ppermute x17 -> x14, starting transfers between devices: 26.7 us -> 19.9 us  [add_permuted(): return sum([lax.ppermute(x, axis, perm) for perm in perms], x)]
    ppermute x17 -> x14, waiting for transfers between devices: 9.72 us -> 16.1 us  [add_permuted(): return sum([lax.ppermute(x, axis, perm) for perm in perms], x)]
  transfers between devices with their start and end apart: 20 -> 17, of which waited for: 9 -> 7; matrix products, arithmetic and copies ran while one was open for 0% -> 0% of each run, Pallas kernels for 1% -> 1%
where the time goes in v4:
time: 136 us; the launch traced here: 135 us
  waiting for transfers between devices  51.7 us (38%)
  starting transfers between devices  42.7 us (31%)
  Pallas kernels  23.5 us (17%)
  blocking collectives  14.7 us (11%)
  local copies, waits for them, and re-layouts  1.39 us (1%)
    all_to_all x3, waiting for transfers between devices, exchange(): return lax.all_to_all(x, axes, split_axis=0, concat_axis=0, tiled=True)  35.6 us
    all_to_all x3, starting transfers between devices, exchange(): return lax.all_to_all(x, axes, split_axis=0, concat_axis=0, tiled=True)  22.8 us
    ppermute x14, starting transfers between devices, add_permuted(): return sum([lax.ppermute(x, axis, perm) for perm in perms], x)  19.9 us
    pallas_call x1, Pallas kernels, shards(): pl.pallas_call(owner_kernel, grid=(SLOTS,), out_shape=[stat_shape, stat_s...  19.5 us
    ppermute x14, waiting for transfers between devices, add_permuted(): return sum([lax.ppermute(x, axis, perm) for perm in perms], x)  16.1 us
    all_to_all x1, blocking collectives, exchange(): return lax.all_to_all(x, axes, split_axis=0, concat_axis=0, tiled=True)  14.7 us
  transfers between devices with their start and end apart: 17, of which 7 were waited for; matrix products, arithmetic and copies ran while one was open for 0% of the time, Pallas kernels for 1%

profile of v4, /device:TPU:8, one launch (start us, length us, event | category | flops | bytes accessed | tf_op | source)
XLA Modules:
  0.0 134.8 jit_solution(3007883256326388495)
XLA Ops:
  0.6 8.5 %all-to-all-start = ((bf16[4,8,4096]{2,1,0:T(8,128)(2,1)}), bf16[4,8,4096]{2,1,0:T(8,128)(2,1)S(1)}, u32[]{:S(2)}, u32[]{:S(2)}) async-start(bf16[4,8,4096]{2,1,0:T(8,128)(2,1)} %bitcast.12), calls=%async_computation | async-start | bytes 524288 | tf_op jit(solution)/shard_map/all_to_all | solution.py:193
  9.1 0.0 copy-start
  9.1 0.7 copy-done
  9.8 0.0 copy-start.1
  9.8 1.5 %places.1.place_ref = s32[32]{0:T(128)S(1)} custom-call(s32[1]{0:T(128)} %bitcast.shard_ref, s32[4,32]{1,0:T(4,128)S(1)} %copy-done), custom_call_target="tpu_custom_call" | custom-call | flops 1000 | bytes 1000 | tf_op jit(solution)/shard_map/places/pallas_call | solution.py:213
  11.3 8.6 %all-to-all-done.in_ref = bf16[4,8,4096]{2,1,0:T(8,128)(2,1)S(1)} async-done(((bf16[4,8,4096]{2,1,0:T(8,128)(2,1)}), bf16[4,8,4096]{2,1,0:T(8,128)(2,1)S(1)}, u32[]{:S(2)}, u32[]{:S(2)}) %all-to-all-start) | async-done | bytes 262176 | tf_op jit(solution)/shard_map/all_to_all | solution.py:193
  19.8 1.7 %route.1 = bf16[64,8,1024]{2,1,0:T(8,128)(2,1)} custom-call(s32[32]{0:T(128)S(1)} %places.1.place_ref, bf16[4,8,4096]{2,1,0:T(8,128)(2,1)S(1)} %all-to-all-done.in_ref), custom_call_target="tpu_custom_call" | custom-call | tf_op jit(solution)/shard_map/route/pallas_call | solution.py:224
  21.5 6.6 %all-to-all-start.1 = ((bf16[64,8,1024]{2,1,0:T(8,128)(2,1)}), bf16[64,8,1024]{2,1,0:T(8,128)(2,1)S(1)}, u32[]{:S(2)}, u32[]{:S(2)}) async-start(bf16[64,8,1024]{2,1,0:T(8,128)(2,1)} %route.1), calls=%async_computation.1 | async-start | bytes 2097152 | tf_op jit(solution)/shard_map/all_to_all | solution.py:193
  28.2 27.1 %all-to-all-done.1 = bf16[64,8,1024]{2,1,0:T(8,128)(2,1)S(1)} async-done(((bf16[64,8,1024]{2,1,0:T(8,128)(2,1)}), bf16[64,8,1024]{2,1,0:T(8,128)(2,1)S(1)}, u32[]{:S(2)}, u32[]{:S(2)}) %all-to-all-start.1) | async-done | bytes 1048608 | tf_op jit(solution)/shard_map/all_to_all | solution.py:193
  55.2 0.0 copy-done.1
  55.2 19.5 %owner.1 = (f32[2,512,512]{2,1,0:T(8,128)}, f32[2,512,512]{2,1,0:T(8,128)}, s16[64,8,1152]{2,1,0:T(8,128)(2,1)}, f32[8,128]{1,0:T(8,128)S(1)}) custom-call(s32[1]{0:T(128)} %bitcast.1.me_ref, s32[32]{0:T(128)S(1)} %places.1.place_ref, bf16[512,1024]{1,0:T(8,128)(2,1)S(1)} %bitcast.9, f32[2,512,512]{2,1,0:T(8,128)S(1)} %bitcast.10, f32[2,512,512]{2,1,0:T(8,128)} %bitcast.13), custom_call_target="tpu_custom_call" | custom-call | flops 13421772800 | bytes 12582912 | tf_op jit(solution)/shard_map/owner/pallas_call | solution.py:238
  74.7 7.7 %all-to-all-start.2 = ((s16[64,8,1152]{2,1,0:T(8,128)(2,1)}), s16[64,8,1152]{2,1,0:T(8,128)(2,1)S(1)}, u32[]{:S(2)}, u32[]{:S(2)}) async-start(s16[64,8,1152]{2,1,0:T(8,128)(2,1)} %get-tuple-element.8), calls=%async_computation.2 | async-start | bytes 2359296 | tf_op jit(solution)/shard_map/all_to_all | solution.py:193
  82.4 2.8 %collective-permute-start.2 = (f32[8,128]{1,0:T(8,128)S(1)}, f32[8,128]{1,0:T(8,128)S(1)}, u32[]{:S(2)}, u32[]{:S(2)}) collective-permute-start(f32[8,128]{1,0:T(8,128)S(1)} %get-tuple-element.7), channel_id=1, source_target_pairs={{0,3},{1,0},{2,1},{3,2},{4,7},{5,4},{6,5},{7,6},{8,11},{9,8},{10,9... | collective-permute-start | bytes 12296 | tf_op jit(solution)/shard_map/ppermute | solution.py:197
  85.3 0.8 collective-permute-start.1
  86.1 0.9 collective-permute-start
  87.0 0.0 collective-permute-done.2
  87.0 3.4 %collective-permute-done.1 = f32[8,128]{1,0:T(8,128)S(1)} collective-permute-done((f32[8,128]{1,0:T(8,128)S(1)}, f32[8,128]{1,0:T(8,128)S(1)}, u32[]{:S(2)}, u32[]{:S(2)}) %collective-permute-start.1) | collective-permute-done | bytes 4128 | tf_op jit(solution)/shard_map/ppermute | solution.py:197
  90.4 0.5 collective-permute-done
  90.9 0.0 collective-permute-start.9
  90.9 1.6 %collective-permute-start.8 = (f32[8,128]{1,0:T(8,128)S(1)}, f32[8,128]{1,0:T(8,128)S(1)}, u32[]{:S(2)}, u32[]{:S(2)}) collective-permute-start(f32[8,128]{1,0:T(8,128)S(1)} %add_add_fusion.2), channel_id=1, source_target_pairs={{0,24},{4,28},{8,16},{12,20},{16,8},{20,12},{24,0},{28,4},{32,56},... | collective-permute-start | bytes 12296 | tf_op jit(solution)/shard_map/ppermute | solution.py:197
  92.5 3.2 %collective-permute-start.7 = (f32[8,128]{1,0:T(8,128)S(1)}, f32[8,128]{1,0:T(8,128)S(1)}, u32[]{:S(2)}, u32[]{:S(2)}) collective-permute-start(f32[8,128]{1,0:T(8,128)S(1)} %add_add_fusion.2), channel_id=1, source_target_pairs={{0,20},{4,16},{8,28},{12,24},{16,4},{20,0},{24,12},{28,8},{32,52},... | collective-permute-start | bytes 12296 | tf_op jit(solution)/shard_map/ppermute | solution.py:197
  95.7 0.2 collective-permute-start.6
  95.9 1.3 collective-permute-start.5
  97.2 0.0 collective-permute-done.9
  97.2 0.4 collective-permute-start.4
  97.6 0.0 collective-permute-done.8
  97.6 0.2 collective-permute-start.3
  97.8 0.0 collective-permute-done.7
  97.8 3.1 %collective-permute-done.6 = f32[8,128]{1,0:T(8,128)S(1)} collective-permute-done((f32[8,128]{1,0:T(8,128)S(1)}, f32[8,128]{1,0:T(8,128)S(1)}, u32[]{:S(2)}, u32[]{:S(2)}) %collective-permute-start.6) | collective-permute-done | bytes 4128 | tf_op jit(solution)/shard_map/ppermute | solution.py:197
  100.9 0.0 collective-permute-done.5
  100.9 0.0 collective-permute-done.4
  100.9 0.0 collective-permute-done.3
  100.9 3.6 %collective-permute-start.12 = (f32[8,128]{1,0:T(8,128)S(1)}, f32[8,128]{1,0:T(8,128)S(1)}, u32[]{:S(2)}, u32[]{:S(2)}) collective-permute-start(f32[8,128]{1,0:T(8,128)S(1)} %add_add_fusion.1), channel_id=1, source_target_pairs={{0,96},{4,100},{8,104},{12,108},{16,112},{20,116},{24,120},{28,124... | collective-permute-start | bytes 12296 | tf_op jit(solution)/shard_map/ppermute | solution.py:197
  104.5 0.0 collective-permute-start.11
  104.5 0.8 collective-permute-start.10
  105.4 5.5 %collective-permute-done.12 = f32[8,128]{1,0:T(8,128)S(1)} collective-permute-done((f32[8,128]{1,0:T(8,128)S(1)}, f32[8,128]{1,0:T(8,128)S(1)}, u32[]{:S(2)}, u32[]{:S(2)}) %collective-permute-start.12) | collective-permute-done | bytes 4128 | tf_op jit(solution)/shard_map/ppermute | solution.py:197
  110.9 0.0 collective-permute-done.11
  110.9 0.0 collective-permute-done.10
  110.9 4.0 %collective-permute-start.13 = (f32[8,128]{1,0:T(8,128)S(1)}, f32[8,128]{1,0:T(8,128)S(1)}, u32[]{:S(2)}, u32[]{:S(2)}) collective-permute-start(f32[8,128]{1,0:T(8,128)S(1)} %add_add_fusion), channel_id=1, source_target_pairs={{0,128},{64,192},{128,0},{192,64},{1,129},{65,193},{129,1},{193,65... | collective-permute-start | bytes 12296 | tf_op jit(solution)/shard_map/ppermute | solution.py:197
  114.9 3.6 %collective-permute-done.13 = f32[8,128]{1,0:T(8,128)S(1)} collective-permute-done((f32[8,128]{1,0:T(8,128)S(1)}, f32[8,128]{1,0:T(8,128)S(1)}, u32[]{:S(2)}, u32[]{:S(2)}) %collective-permute-start.13) | collective-permute-done | bytes 4128 | tf_op jit(solution)/shard_map/ppermute | solution.py:197
  118.5 0.0 all-to-all-done.2.in_ref
  118.5 0.9 collect.1
  119.4 14.7 %all_to_all.20 = bf16[4,8,4096]{2,1,0:T(8,128)(2,1)S(1)} all-to-all(bf16[4,8,4096]{2,1,0:T(8,128)(2,1)S(1)} %collect.1), channel_id=1, replica_groups=mesh['g'=4,'r'=16,'mp'=4] {'g'}, dimensions={0} | all-to-all | bytes 524288 | tf_op jit(solution)/shard_map/all_to_all | solution.py:193
  134.1 0.7 copy.8
  (4 shorter events, 0.0 us)
Async XLA Ops:
  0.6 19.2 %all-to-all-start = ((bf16[4,8,4096]{2,1,0:T(8,128)(2,1)}), bf16[4,8,4096]{2,1,0:T(8,128)(2,1)S(1)}, u32[]{:S(2)}, u32[]{:S(2)}) async-start(bf16[4,8,4096]{2,1,0:T(8,128)(2,1)} %bitcast.12), calls=%async_computation | async-start | bytes 524288 | tf_op jit(solution)/shard_map/all_to_all | solution.py:193
  9.1 0.7 copy-start
  9.8 45.5 %copy-start.1 = (f32[1,1,2,512,512]{4,3,2,1,0:T(8,128)S(1)}, f32[1,1,2,512,512]{4,3,2,1,0:T(8,128)}, u32[]{:S(2)}) copy-start(f32[1,1,2,512,512]{4,3,2,1,0:T(8,128)} %param.6) | copy-start | bytes 6291460
  21.5 33.7 %all-to-all-start.1 = ((bf16[64,8,1024]{2,1,0:T(8,128)(2,1)}), bf16[64,8,1024]{2,1,0:T(8,128)(2,1)S(1)}, u32[]{:S(2)}, u32[]{:S(2)}) async-start(bf16[64,8,1024]{2,1,0:T(8,128)(2,1)} %route.1), calls=%async_computation.1 | async-start | bytes 2097152 | tf_op jit(solution)/shard_map/all_to_all | solution.py:193
  74.7 43.8 %all-to-all-start.2 = ((s16[64,8,1152]{2,1,0:T(8,128)(2,1)}), s16[64,8,1152]{2,1,0:T(8,128)(2,1)S(1)}, u32[]{:S(2)}, u32[]{:S(2)}) async-start(s16[64,8,1152]{2,1,0:T(8,128)(2,1)} %get-tuple-element.8), calls=%async_computation.2 | async-start | bytes 2359296 | tf_op jit(solution)/shard_map/all_to_all | solution.py:193
  82.4 4.5 %collective-permute-start.2 = (f32[8,128]{1,0:T(8,128)S(1)}, f32[8,128]{1,0:T(8,128)S(1)}, u32[]{:S(2)}, u32[]{:S(2)}) collective-permute-start(f32[8,128]{1,0:T(8,128)S(1)} %get-tuple-element.7), channel_id=1, source_target_pairs={{0,3},{1,0},{2,1},{3,2},{4,7},{5,4},{6,5},{7,6},{8,11},{9,8},{10,9... | collective-permute-start | bytes 12296 | tf_op jit(solution)/shard_map/ppermute | solution.py:197
  85.3 5.1 %collective-permute-start.1 = (f32[8,128]{1,0:T(8,128)S(1)}, f32[8,128]{1,0:T(8,128)S(1)}, u32[]{:S(2)}, u32[]{:S(2)}) collective-permute-start(f32[8,128]{1,0:T(8,128)S(1)} %get-tuple-element.7), channel_id=1, source_target_pairs={{0,2},{1,3},{2,0},{3,1},{4,6},{5,7},{6,4},{7,5},{8,10},{9,11},{10,... | collective-permute-start | bytes 12296 | tf_op jit(solution)/shard_map/ppermute | solution.py:197
  86.1 4.8 %collective-permute-start = (f32[8,128]{1,0:T(8,128)S(1)}, f32[8,128]{1,0:T(8,128)S(1)}, u32[]{:S(2)}, u32[]{:S(2)}) collective-permute-start(f32[8,128]{1,0:T(8,128)S(1)} %get-tuple-element.7), channel_id=1, source_target_pairs={{0,1},{1,2},{2,3},{3,0},{4,5},{5,6},{6,7},{7,4},{8,9},{9,10},{10,1... | collective-permute-start | bytes 12296 | tf_op jit(solution)/shard_map/ppermute | solution.py:197
  90.9 6.3 %collective-permute-start.9 = (f32[8,128]{1,0:T(8,128)S(1)}, f32[8,128]{1,0:T(8,128)S(1)}, u32[]{:S(2)}, u32[]{:S(2)}) collective-permute-start(f32[8,128]{1,0:T(8,128)S(1)} %add_add_fusion.2), channel_id=1, source_target_pairs={{0,28},{4,24},{8,20},{12,16},{16,12},{20,8},{24,4},{28,0},{32,60},... | collective-permute-start | bytes 12296 | tf_op jit(solution)/shard_map/ppermute | solution.py:197
  90.9 6.7 %collective-permute-start.8 = (f32[8,128]{1,0:T(8,128)S(1)}, f32[8,128]{1,0:T(8,128)S(1)}, u32[]{:S(2)}, u32[]{:S(2)}) collective-permute-start(f32[8,128]{1,0:T(8,128)S(1)} %add_add_fusion.2), channel_id=1, source_target_pairs={{0,24},{4,28},{8,16},{12,20},{16,8},{20,12},{24,0},{28,4},{32,56},... | collective-permute-start | bytes 12296 | tf_op jit(solution)/shard_map/ppermute | solution.py:197
  92.5 5.3 %collective-permute-start.7 = (f32[8,128]{1,0:T(8,128)S(1)}, f32[8,128]{1,0:T(8,128)S(1)}, u32[]{:S(2)}, u32[]{:S(2)}) collective-permute-start(f32[8,128]{1,0:T(8,128)S(1)} %add_add_fusion.2), channel_id=1, source_target_pairs={{0,20},{4,16},{8,28},{12,24},{16,4},{20,0},{24,12},{28,8},{32,52},... | collective-permute-start | bytes 12296 | tf_op jit(solution)/shard_map/ppermute | solution.py:197
  95.7 5.2 %collective-permute-start.6 = (f32[8,128]{1,0:T(8,128)S(1)}, f32[8,128]{1,0:T(8,128)S(1)}, u32[]{:S(2)}, u32[]{:S(2)}) collective-permute-start(f32[8,128]{1,0:T(8,128)S(1)} %add_add_fusion.2), channel_id=1, source_target_pairs={{0,16},{4,20},{8,24},{12,28},{16,0},{20,4},{24,8},{28,12},{32,48},... | collective-permute-start | bytes 12296 | tf_op jit(solution)/shard_map/ppermute | solution.py:197
  95.9 5.0 %collective-permute-start.5 = (f32[8,128]{1,0:T(8,128)S(1)}, f32[8,128]{1,0:T(8,128)S(1)}, u32[]{:S(2)}, u32[]{:S(2)}) collective-permute-start(f32[8,128]{1,0:T(8,128)S(1)} %add_add_fusion.2), channel_id=1, source_target_pairs={{0,12},{4,8},{8,4},{12,0},{16,28},{20,24},{24,20},{28,16},{32,44},... | collective-permute-start | bytes 12296 | tf_op jit(solution)/shard_map/ppermute | solution.py:197
  97.2 3.6 %collective-permute-start.4 = (f32[8,128]{1,0:T(8,128)S(1)}, f32[8,128]{1,0:T(8,128)S(1)}, u32[]{:S(2)}, u32[]{:S(2)}) collective-permute-start(f32[8,128]{1,0:T(8,128)S(1)} %add_add_fusion.2), channel_id=1, source_target_pairs={{0,8},{4,12},{8,0},{12,4},{16,24},{20,28},{24,16},{28,20},{32,40},... | collective-permute-start | bytes 12296 | tf_op jit(solution)/shard_map/ppermute | solution.py:197
  97.6 3.3 %collective-permute-start.3 = (f32[8,128]{1,0:T(8,128)S(1)}, f32[8,128]{1,0:T(8,128)S(1)}, u32[]{:S(2)}, u32[]{:S(2)}) collective-permute-start(f32[8,128]{1,0:T(8,128)S(1)} %add_add_fusion.2), channel_id=1, source_target_pairs={{0,4},{4,0},{8,12},{12,8},{16,20},{20,16},{24,28},{28,24},{32,36},... | collective-permute-start | bytes 12296 | tf_op jit(solution)/shard_map/ppermute | solution.py:197
  100.9 10.0 %collective-permute-start.12 = (f32[8,128]{1,0:T(8,128)S(1)}, f32[8,128]{1,0:T(8,128)S(1)}, u32[]{:S(2)}, u32[]{:S(2)}) collective-permute-start(f32[8,128]{1,0:T(8,128)S(1)} %add_add_fusion.1), channel_id=1, source_target_pairs={{0,96},{4,100},{8,104},{12,108},{16,112},{20,116},{24,120},{28,124... | collective-permute-start | bytes 12296 | tf_op jit(solution)/shard_map/ppermute | solution.py:197
  104.5 6.3 %collective-permute-start.11 = (f32[8,128]{1,0:T(8,128)S(1)}, f32[8,128]{1,0:T(8,128)S(1)}, u32[]{:S(2)}, u32[]{:S(2)}) collective-permute-start(f32[8,128]{1,0:T(8,128)S(1)} %add_add_fusion.1), channel_id=1, source_target_pairs={{0,64},{4,68},{8,72},{12,76},{16,80},{20,84},{24,88},{28,92},{32,9... | collective-permute-start | bytes 12296 | tf_op jit(solution)/shard_map/ppermute | solution.py:197
  104.5 6.3 %collective-permute-start.10 = (f32[8,128]{1,0:T(8,128)S(1)}, f32[8,128]{1,0:T(8,128)S(1)}, u32[]{:S(2)}, u32[]{:S(2)}) collective-permute-start(f32[8,128]{1,0:T(8,128)S(1)} %add_add_fusion.1), channel_id=1, source_target_pairs={{0,32},{4,36},{8,40},{12,44},{16,48},{20,52},{24,56},{28,60},{32,0... | collective-permute-start | bytes 12296 | tf_op jit(solution)/shard_map/ppermute | solution.py:197
  110.9 7.6 %collective-permute-start.13 = (f32[8,128]{1,0:T(8,128)S(1)}, f32[8,128]{1,0:T(8,128)S(1)}, u32[]{:S(2)}, u32[]{:S(2)}) collective-permute-start(f32[8,128]{1,0:T(8,128)S(1)} %add_add_fusion), channel_id=1, source_target_pairs={{0,128},{64,192},{128,0},{192,64},{1,129},{65,193},{129,1},{193,65... | collective-permute-start | bytes 12296 | tf_op jit(solution)/shard_map/ppermute | solution.py:197

commit v5 on v4

--- a/solution.py
+++ b/solution.py
@@ -77,15 +77,26 @@
     return high, (x - high.astype(jnp.float32)).astype(jnp.bfloat16)
 
 
-def dot3(a, b, columns):
+HALF = BLOCK // 2
+ALL = slice(0, BLOCK)
+LOW = slice(0, HALF)
+HIGH = slice(HALF, BLOCK)
+
+
+def dot3(a, b, rows, columns):
     return dot(
-        jnp.concatenate([a[0][...], a[0][...], a[1][...]], axis=1),
+        jnp.concatenate([a[0][rows], a[0][rows], a[1][rows]], axis=1),
         jnp.concatenate([b[0][:, columns], b[1][:, columns], b[0][:, columns]], axis=0),
     )
 
 
-def put(pair, columns, x):
-    pair[0][:, columns], pair[1][:, columns] = split(x)
+def put(pair, rows, columns, x):
+    pair[0][rows, columns], pair[1][rows, columns] = split(x)
+
+
+def mirror(pair):
+    for part in pair:
+        part[LOW, HIGH] = part[HIGH, LOW].T
 
 
 def owner_kernel(me_ref, place_ref, got_ref, left_ref, right_ref, new_left_ref, new_right_ref, coded_ref,
@@ -114,13 +125,13 @@
     block = got_ref[...]
     block = jnp.where(used, block, jnp.zeros_like(block))
     turned = block.T
-    halves = [pl.ds(0, BLOCK // 2), pl.ds(BLOCK // 2, BLOCK // 2)]
-    steps = [(columns, side) for columns in halves for side in range(2)]
-
-    def eye(columns, value):
-        rows = lax.broadcasted_iota(jnp.int32, (BLOCK, columns.size), 0)
-        lanes = lax.broadcasted_iota(jnp.int32, (BLOCK, columns.size), 1) + columns.start
-        return jnp.where(rows == lanes, jnp.float32(value), jnp.float32(0))
+    steps = [(rows, columns, side) for rows, columns in ((ALL, LOW), (HIGH, HIGH)) for side in range(2)]
+
+    def eye(rows, columns, value):
+        shape = (rows.stop - rows.start, columns.stop - columns.start)
+        down = lax.broadcasted_iota(jnp.int32, shape, 0) + rows.start
+        across = lax.broadcasted_iota(jnp.int32, shape, 1) + columns.start
+        return jnp.where(down == across, jnp.float32(value), jnp.float32(0))
 
     def pair(ref, side):
         return ref.at[side, 0], ref.at[side, 1]
@@ -132,32 +143,40 @@
         stat = BETA * prev_ref[side, slot] + gram
         new_ref[side, slot] = stat
         write(side, slot).start()
-        damped = stat + eye(pl.ds(0, BLOCK), EPS_DAMP)
+        damped = stat + eye(ALL, ALL, EPS_DAMP)
         norm = jnp.sqrt(jnp.sum(damped * damped, keepdims=True))
         n = damped * (1.0 / norm)
         n_ref[side] = n
-        put(pair(n_parts_ref, side), slice(None), n)
+        put(pair(n_parts_ref, side), ALL, ALL, n)
         norms.append(norm)
-    for columns, side in steps:
-        n = n_ref[side, :, columns]
+    for rows, columns, side in steps:
+        n = n_ref[side, rows, columns]
         n_parts = pair(n_parts_ref, side)
-        n2 = dot3(n_parts, n_parts, columns)
-        put(pair(q_parts_ref, side), columns, eye(columns, 1.5625) - 2.5 * n + n2)
-        put(pair(h_parts_ref, side), columns, 1.25 * n - n2)
-    for columns, side in steps:
+        n2 = dot3(n_parts, n_parts, rows, columns)
+        put(pair(q_parts_ref, side), rows, columns, eye(rows, columns, 1.5625) - 2.5 * n + n2)
+        put(pair(h_parts_ref, side), rows, columns, 1.25 * n - n2)
+        if columns == LOW:
+            mirror(pair(q_parts_ref, side))
+            mirror(pair(h_parts_ref, side))
+    for rows, columns, side in steps:
         q_parts = pair(q_parts_ref, side)
-        put(pair(r_parts_ref, side), columns, dot3(q_parts, q_parts, columns))
-    for columns, side in steps:
-        product = dot3(pair(h_parts_ref, side), pair(r_parts_ref, side), columns)
-        product = eye(columns, 1.5625) - 1.25 * n_ref[side, :, columns] - product
-        put(pair(n_parts_ref, side), columns, product * lax.rsqrt(jnp.sqrt(0.25 * norms[side])))
+        put(pair(r_parts_ref, side), rows, columns, dot3(q_parts, q_parts, rows, columns))
+        if columns == LOW:
+            mirror(pair(r_parts_ref, side))
+    for rows, columns, side in steps:
+        product = dot3(pair(h_parts_ref, side), pair(r_parts_ref, side), rows, columns)
+        product = eye(rows, columns, 1.5625) - 1.25 * n_ref[side, rows, columns] - product
+        product = product * lax.rsqrt(jnp.sqrt(0.25 * norms[side]))
+        put(pair(n_parts_ref, side), rows, columns, product)
+        if columns == LOW:
+            mirror(pair(n_parts_ref, side))
     left_root = jnp.concatenate([n_parts_ref[0, 0], n_parts_ref[0, 1]], axis=1)
-    for columns in halves:
-        part = block[:, columns.start : columns.start + columns.size]
-        put(pair(q_parts_ref, 0), columns, dot(left_root, jnp.concatenate([part, part], axis=0)))
+    for columns in (LOW, HIGH):
+        part = block[:, columns]
+        put(pair(q_parts_ref, 0), ALL, columns, dot(left_root, jnp.concatenate([part, part], axis=0)))
     update_sq = jnp.zeros((1, 1), jnp.float32)
-    for columns in halves:
-        raw = dot3(pair(q_parts_ref, 0), pair(n_parts_ref, 1), columns)
+    for columns in (LOW, HIGH):
+        raw = dot3(pair(q_parts_ref, 0), pair(n_parts_ref, 1), ALL, columns)
         raw_ref[:, columns] = raw
         update_sq += jnp.sum(raw * raw, keepdims=True)
     wide = block.astype(jnp.float32)
@@ -198,10 +217,10 @@
 
 
 def sum_everywhere(x):
-    x = add_permuted(x, "mp", [[(d, (d + s) % SHARDS) for d in range(SHARDS)] for s in range(1, 4)])
+    ends = [[(d, (d ^ t) // 4 * 4 + (d + s) % 4) for d in range(16)] for t in (0, 8) for s in range(4)]
+    x = add_permuted(x, ("g", "mp"), ends[1:])
     x = add_permuted(x, "r", [[(d, d ^ s) for d in range(MEMBERS)] for s in range(1, 8)])
     x = add_permuted(x, ("g", "r"), [[(d, d ^ (8 * s)) for d in range(OWNERS)] for s in range(1, 4)])
-    x = add_permuted(x, "g", [[(d, d ^ 2) for d in range(GROUPS)]])
     return x
 
 

time: 136 us -> 152 us (1.12)
  starting transfers between devices: 42.7 us -> 55.4 us
  waiting for transfers between devices: 51.7 us -> 59.5 us
  Pallas kernels: 23.5 us -> 21.1 us
    ppermute x14 -> x17, starting transfers between devices: 19.9 us -> 32.6 us  [add_permuted(): return sum([lax.ppermute(x, axis, perm) for perm in perms], x)]
    ppermute x14 -> x17, waiting for transfers between devices: 16.1 us -> 23.9 us  [add_permuted(): return sum([lax.ppermute(x, axis, perm) for perm in perms], x)]
    pallas_call x1, Pallas kernels: 19.5 us -> 17.1 us  [shards(): pl.pallas_call(owner_kernel, grid=(SLOTS,), out_shape=[stat_shape, stat_s...]
  transfers between devices with their start and end apart: 17 -> 20, of which waited for: 7 -> 9; matrix products, arithmetic and copies ran while one was open for 0% -> 0% of each run, Pallas kernels for 1% -> 1%
where the time goes in v5:
time: 152 us; the launch traced here: 151 us
  waiting for transfers between devices  59.5 us (39%)
  starting transfers between devices  55.4 us (36%)
  Pallas kernels  21.1 us (14%)
  blocking collectives  13.2 us (9%)
    all_to_all x3, waiting for transfers between devices, exchange(): return lax.all_to_all(x, axes, split_axis=0, concat_axis=0, tiled=True)  35.6 us
    ppermute x17, starting transfers between devices, add_permuted(): return sum([lax.ppermute(x, axis, perm) for perm in perms], x)  32.6 us
    ppermute x17, waiting for transfers between devices, add_permuted(): return sum([lax.ppermute(x, axis, perm) for perm in perms], x)  23.9 us
    all_to_all x3, starting transfers between devices, exchange(): return lax.all_to_all(x, axes, split_axis=0, concat_axis=0, tiled=True)  22.8 us
    pallas_call x1, Pallas kernels, shards(): pl.pallas_call(owner_kernel, grid=(SLOTS,), out_shape=[stat_shape, stat_s...  17.1 us
    all_to_all x1, blocking collectives, exchange(): return lax.all_to_all(x, axes, split_axis=0, concat_axis=0, tiled=True)  13.2 us
  transfers between devices with their start and end apart: 20, of which 9 were waited for; matrix products, arithmetic and copies ran while one was open for 0% of the time, Pallas kernels for 1%

profile of v5, /device:TPU:8, one launch (start us, length us, event | category | flops | bytes accessed | tf_op | source)
XLA Modules:
  0.0 151.4 jit_solution(3098409727059851945)
XLA Ops:
  0.6 8.5 %all-to-all-start = ((bf16[4,8,4096]{2,1,0:T(8,128)(2,1)}), bf16[4,8,4096]{2,1,0:T(8,128)(2,1)S(1)}, u32[]{:S(2)}, u32[]{:S(2)}) async-start(bf16[4,8,4096]{2,1,0:T(8,128)(2,1)} %bitcast.12), calls=%async_computation | async-start | bytes 524288 | tf_op jit(solution)/shard_map/all_to_all | solution.py:212
  9.1 0.7 copy-done
  9.8 1.5 places.1.place_ref
  11.3 8.6 %all-to-all-done.in_ref = bf16[4,8,4096]{2,1,0:T(8,128)(2,1)S(1)} async-done(((bf16[4,8,4096]{2,1,0:T(8,128)(2,1)}), bf16[4,8,4096]{2,1,0:T(8,128)(2,1)S(1)}, u32[]{:S(2)}, u32[]{:S(2)}) %all-to-all-start) | async-done | bytes 262176 | tf_op jit(solution)/shard_map/all_to_all | solution.py:212
  19.8 1.7 %route.1 = bf16[64,8,1024]{2,1,0:T(8,128)(2,1)} custom-call(s32[32]{0:T(128)S(1)} %places.1.place_ref, bf16[4,8,4096]{2,1,0:T(8,128)(2,1)S(1)} %all-to-all-done.in_ref), custom_call_target="tpu_custom_call" | custom-call | tf_op jit(solution)/shard_map/route/pallas_call | solution.py:243
  21.5 6.6 %all-to-all-start.1 = ((bf16[64,8,1024]{2,1,0:T(8,128)(2,1)}), bf16[64,8,1024]{2,1,0:T(8,128)(2,1)S(1)}, u32[]{:S(2)}, u32[]{:S(2)}) async-start(bf16[64,8,1024]{2,1,0:T(8,128)(2,1)} %route.1), calls=%async_computation.1 | async-start | bytes 2097152 | tf_op jit(solution)/shard_map/all_to_all | solution.py:212
  28.2 27.1 %all-to-all-done.1 = bf16[64,8,1024]{2,1,0:T(8,128)(2,1)S(1)} async-done(((bf16[64,8,1024]{2,1,0:T(8,128)(2,1)}), bf16[64,8,1024]{2,1,0:T(8,128)(2,1)S(1)}, u32[]{:S(2)}, u32[]{:S(2)}) %all-to-all-start.1) | async-done | bytes 1048608 | tf_op jit(solution)/shard_map/all_to_all | solution.py:212
  55.2 0.0 copy-done.1
  55.2 17.1 %owner.1 = (f32[2,512,512]{2,1,0:T(8,128)}, f32[2,512,512]{2,1,0:T(8,128)}, s16[64,8,1152]{2,1,0:T(8,128)(2,1)}, f32[8,128]{1,0:T(8,128)S(1)}) custom-call(s32[1]{0:T(128)} %bitcast.1.me_ref, s32[32]{0:T(128)S(1)} %places.1.place_ref, bf16[512,1024]{1,0:T(8,128)(2,1)S(1)} %bitcast.9, f32[2,512,512]{2,1,0:T(8,128)S(1)} %bitcast.10, f32[2,512,512]{2,1,0:T(8,128)} %bitcast.13), custom_call_target="tpu_custom_call" | custom-call | flops 13421772800 | bytes 12582912 | tf_op jit(solution)/shard_map/owner/pallas_call | solution.py:257
  72.3 7.7 %all-to-all-start.2 = ((s16[64,8,1152]{2,1,0:T(8,128)(2,1)}), s16[64,8,1152]{2,1,0:T(8,128)(2,1)S(1)}, u32[]{:S(2)}, u32[]{:S(2)}) async-start(s16[64,8,1152]{2,1,0:T(8,128)(2,1)} %get-tuple-element.8), calls=%async_computation.2 | async-start | bytes 2359296 | tf_op jit(solution)/shard_map/all_to_all | solution.py:212
  80.0 7.6 %collective-permute-start.6 = (f32[8,128]{1,0:T(8,128)S(1)}, f32[8,128]{1,0:T(8,128)S(1)}, u32[]{:S(2)}, u32[]{:S(2)}) collective-permute-start(f32[8,128]{1,0:T(8,128)S(1)} %get-tuple-element.7), channel_id=1, source_target_pairs={{0,131},{1,128},{2,129},{3,130},{64,195},{65,192},{66,193},{67,194... | collective-permute-start | bytes 12296 | tf_op jit(solution)/shard_map/ppermute | solution.py:216
  87.7 0.8 collective-permute-start.5
  88.5 5.7 %collective-permute-start.4 = (f32[8,128]{1,0:T(8,128)S(1)}, f32[8,128]{1,0:T(8,128)S(1)}, u32[]{:S(2)}, u32[]{:S(2)}) collective-permute-start(f32[8,128]{1,0:T(8,128)S(1)} %get-tuple-element.7), channel_id=1, source_target_pairs={{0,129},{1,130},{2,131},{3,128},{64,193},{65,194},{66,195},{67,192... | collective-permute-start | bytes 12296 | tf_op jit(solution)/shard_map/ppermute | solution.py:216
  94.2 0.6 collective-permute-start.3
  94.7 2.4 %collective-permute-start.2 = (f32[8,128]{1,0:T(8,128)S(1)}, f32[8,128]{1,0:T(8,128)S(1)}, u32[]{:S(2)}, u32[]{:S(2)}) collective-permute-start(f32[8,128]{1,0:T(8,128)S(1)} %get-tuple-element.7), channel_id=1, source_target_pairs={{0,3},{1,0},{2,1},{3,2},{64,67},{65,64},{66,65},{67,66},{128,131},... | collective-permute-start | bytes 12296 | tf_op jit(solution)/shard_map/ppermute | solution.py:216
  97.1 14.4 %collective-permute-done.6 = f32[8,128]{1,0:T(8,128)S(1)} collective-permute-done((f32[8,128]{1,0:T(8,128)S(1)}, f32[8,128]{1,0:T(8,128)S(1)}, u32[]{:S(2)}, u32[]{:S(2)}) %collective-permute-start.6) | collective-permute-done | bytes 4128 | tf_op jit(solution)/shard_map/ppermute | solution.py:216
  111.5 2.7 %collective-permute-start.1 = (f32[8,128]{1,0:T(8,128)S(1)}, f32[8,128]{1,0:T(8,128)S(1)}, u32[]{:S(2)}, u32[]{:S(2)}) collective-permute-start(f32[8,128]{1,0:T(8,128)S(1)} %get-tuple-element.7), channel_id=1, source_target_pairs={{0,2},{1,3},{2,0},{3,1},{64,66},{65,67},{66,64},{67,65},{128,130},... | collective-permute-start | bytes 12296 | tf_op jit(solution)/shard_map/ppermute | solution.py:216
  114.2 0.0 collective-permute-done.5
  114.2 0.0 collective-permute-start
  114.2 0.0 collective-permute-done.4
  114.2 0.0 collective-permute-done.3
  114.2 0.0 collective-permute-done.2
  114.2 2.4 %collective-permute-done.1 = f32[8,128]{1,0:T(8,128)S(1)} collective-permute-done((f32[8,128]{1,0:T(8,128)S(1)}, f32[8,128]{1,0:T(8,128)S(1)}, u32[]{:S(2)}, u32[]{:S(2)}) %collective-permute-start.1) | collective-permute-done | bytes 4128 | tf_op jit(solution)/shard_map/ppermute | solution.py:216
  116.6 2.4 %collective-permute-done = f32[8,128]{1,0:T(8,128)S(1)} collective-permute-done((f32[8,128]{1,0:T(8,128)S(1)}, f32[8,128]{1,0:T(8,128)S(1)}, u32[]{:S(2)}, u32[]{:S(2)}) %collective-permute-start) | collective-permute-done | bytes 4128 | tf_op jit(solution)/shard_map/ppermute | solution.py:216
  119.0 0.1 collective-permute-start.13
  119.1 2.5 %collective-permute-start.12 = (f32[8,128]{1,0:T(8,128)S(1)}, f32[8,128]{1,0:T(8,128)S(1)}, u32[]{:S(2)}, u32[]{:S(2)}) collective-permute-start(f32[8,128]{1,0:T(8,128)S(1)} %add_add_fusion.2), channel_id=1, source_target_pairs={{0,24},{4,28},{8,16},{12,20},{16,8},{20,12},{24,0},{28,4},{32,56},... | collective-permute-start | bytes 12296 | tf_op jit(solution)/shard_map/ppermute | solution.py:216
  121.6 3.2 %collective-permute-start.11 = (f32[8,128]{1,0:T(8,128)S(1)}, f32[8,128]{1,0:T(8,128)S(1)}, u32[]{:S(2)}, u32[]{:S(2)}) collective-permute-start(f32[8,128]{1,0:T(8,128)S(1)} %add_add_fusion.2), channel_id=1, source_target_pairs={{0,20},{4,16},{8,28},{12,24},{16,4},{20,0},{24,12},{28,8},{32,52},... | collective-permute-start | bytes 12296 | tf_op jit(solution)/shard_map/ppermute | solution.py:216
  124.8 0.0 collective-permute-start.10
  124.8 1.6 %collective-permute-start.9 = (f32[8,128]{1,0:T(8,128)S(1)}, f32[8,128]{1,0:T(8,128)S(1)}, u32[]{:S(2)}, u32[]{:S(2)}) collective-permute-start(f32[8,128]{1,0:T(8,128)S(1)} %add_add_fusion.2), channel_id=1, source_target_pairs={{0,12},{4,8},{8,4},{12,0},{16,28},{20,24},{24,20},{28,16},{32,44},... | collective-permute-start | bytes 12296 | tf_op jit(solution)/shard_map/ppermute | solution.py:216
  126.4 0.0 collective-permute-done.13
  126.4 0.8 collective-permute-start.8
  127.2 0.0 collective-permute-done.12
  127.2 0.2 collective-permute-start.7
  127.3 0.0 collective-permute-done.11
  127.4 2.6 %collective-permute-done.10 = f32[8,128]{1,0:T(8,128)S(1)} collective-permute-done((f32[8,128]{1,0:T(8,128)S(1)}, f32[8,128]{1,0:T(8,128)S(1)}, u32[]{:S(2)}, u32[]{:S(2)}) %collective-permute-start.10) | collective-permute-done | bytes 4128 | tf_op jit(solution)/shard_map/ppermute | solution.py:216
  129.9 0.0 collective-permute-done.9
  129.9 0.1 collective-permute-done.8
  130.0 0.0 collective-permute-done.7
  130.0 0.7 collective-permute-start.16
  130.7 2.3 %collective-permute-start.15 = (f32[8,128]{1,0:T(8,128)S(1)}, f32[8,128]{1,0:T(8,128)S(1)}, u32[]{:S(2)}, u32[]{:S(2)}) collective-permute-start(f32[8,128]{1,0:T(8,128)S(1)} %add_add_fusion.1), channel_id=1, source_target_pairs={{0,64},{4,68},{8,72},{12,76},{16,80},{20,84},{24,88},{28,92},{32,9... | collective-permute-start | bytes 12296 | tf_op jit(solution)/shard_map/ppermute | solution.py:216
  133.0 1.5 collective-permute-start.14
  134.5 1.0 collective-permute-done.16
  135.5 0.0 collective-permute-done.15
  135.5 1.1 collective-permute-done.14
  136.6 0.0 all-to-all-done.2.in_ref
  136.6 0.9 collect.1
  137.5 13.2 %all_to_all.20 = bf16[4,8,4096]{2,1,0:T(8,128)(2,1)S(1)} all-to-all(bf16[4,8,4096]{2,1,0:T(8,128)(2,1)S(1)} %collect.1), channel_id=1, replica_groups=mesh['g'=4,'r'=16,'mp'=4] {'g'}, dimensions={0} | all-to-all | bytes 524288 | tf_op jit(solution)/shard_map/all_to_all | solution.py:212
  150.7 0.7 copy.8
  (5 shorter events, 0.0 us)
Async XLA Ops:
  0.6 19.2 %all-to-all-start = ((bf16[4,8,4096]{2,1,0:T(8,128)(2,1)}), bf16[4,8,4096]{2,1,0:T(8,128)(2,1)S(1)}, u32[]{:S(2)}, u32[]{:S(2)}) async-start(bf16[4,8,4096]{2,1,0:T(8,128)(2,1)} %bitcast.12), calls=%async_computation | async-start | bytes 524288 | tf_op jit(solution)/shard_map/all_to_all | solution.py:212
  9.1 0.7 copy-start
  9.8 45.5 %copy-start.1 = (f32[1,1,2,512,512]{4,3,2,1,0:T(8,128)S(1)}, f32[1,1,2,512,512]{4,3,2,1,0:T(8,128)}, u32[]{:S(2)}) copy-start(f32[1,1,2,512,512]{4,3,2,1,0:T(8,128)} %param.6) | copy-start | bytes 6291460
  21.5 33.7 %all-to-all-start.1 = ((bf16[64,8,1024]{2,1,0:T(8,128)(2,1)}), bf16[64,8,1024]{2,1,0:T(8,128)(2,1)S(1)}, u32[]{:S(2)}, u32[]{:S(2)}) async-start(bf16[64,8,1024]{2,1,0:T(8,128)(2,1)} %route.1), calls=%async_computation.1 | async-start | bytes 2097152 | tf_op jit(solution)/shard_map/all_to_all | solution.py:212
  72.3 64.3 %all-to-all-start.2 = ((s16[64,8,1152]{2,1,0:T(8,128)(2,1)}), s16[64,8,1152]{2,1,0:T(8,128)(2,1)S(1)}, u32[]{:S(2)}, u32[]{:S(2)}) async-start(s16[64,8,1152]{2,1,0:T(8,128)(2,1)} %get-tuple-element.8), calls=%async_computation.2 | async-start | bytes 2359296 | tf_op jit(solution)/shard_map/all_to_all | solution.py:212
  80.0 31.4 %collective-permute-start.6 = (f32[8,128]{1,0:T(8,128)S(1)}, f32[8,128]{1,0:T(8,128)S(1)}, u32[]{:S(2)}, u32[]{:S(2)}) collective-permute-start(f32[8,128]{1,0:T(8,128)S(1)} %get-tuple-element.7), channel_id=1, source_target_pairs={{0,131},{1,128},{2,129},{3,130},{64,195},{65,192},{66,193},{67,194... | collective-permute-start | bytes 12296 | tf_op jit(solution)/shard_map/ppermute | solution.py:216
  87.7 26.5 %collective-permute-start.5 = (f32[8,128]{1,0:T(8,128)S(1)}, f32[8,128]{1,0:T(8,128)S(1)}, u32[]{:S(2)}, u32[]{:S(2)}) collective-permute-start(f32[8,128]{1,0:T(8,128)S(1)} %get-tuple-element.7), channel_id=1, source_target_pairs={{0,130},{1,131},{2,128},{3,129},{64,194},{65,195},{66,192},{67,193... | collective-permute-start | bytes 12296 | tf_op jit(solution)/shard_map/ppermute | solution.py:216
  88.5 25.7 %collective-permute-start.4 = (f32[8,128]{1,0:T(8,128)S(1)}, f32[8,128]{1,0:T(8,128)S(1)}, u32[]{:S(2)}, u32[]{:S(2)}) collective-permute-start(f32[8,128]{1,0:T(8,128)S(1)} %get-tuple-element.7), channel_id=1, source_target_pairs={{0,129},{1,130},{2,131},{3,128},{64,193},{65,194},{66,195},{67,192... | collective-permute-start | bytes 12296 | tf_op jit(solution)/shard_map/ppermute | solution.py:216
  94.2 20.0 %collective-permute-start.3 = (f32[8,128]{1,0:T(8,128)S(1)}, f32[8,128]{1,0:T(8,128)S(1)}, u32[]{:S(2)}, u32[]{:S(2)}) collective-permute-start(f32[8,128]{1,0:T(8,128)S(1)} %get-tuple-element.7), channel_id=1, source_target_pairs={{0,128},{1,129},{2,130},{3,131},{64,192},{65,193},{66,194},{67,195... | collective-permute-start | bytes 12296 | tf_op jit(solution)/shard_map/ppermute | solution.py:216
  94.7 19.5 %collective-permute-start.2 = (f32[8,128]{1,0:T(8,128)S(1)}, f32[8,128]{1,0:T(8,128)S(1)}, u32[]{:S(2)}, u32[]{:S(2)}) collective-permute-start(f32[8,128]{1,0:T(8,128)S(1)} %get-tuple-element.7), channel_id=1, source_target_pairs={{0,3},{1,0},{2,1},{3,2},{64,67},{65,64},{66,65},{67,66},{128,131},... | collective-permute-start | bytes 12296 | tf_op jit(solution)/shard_map/ppermute | solution.py:216
  111.5 5.1 %collective-permute-start.1 = (f32[8,128]{1,0:T(8,128)S(1)}, f32[8,128]{1,0:T(8,128)S(1)}, u32[]{:S(2)}, u32[]{:S(2)}) collective-permute-start(f32[8,128]{1,0:T(8,128)S(1)} %get-tuple-element.7), channel_id=1, source_target_pairs={{0,2},{1,3},{2,0},{3,1},{64,66},{65,67},{66,64},{67,65},{128,130},... | collective-permute-start | bytes 12296 | tf_op jit(solution)/shard_map/ppermute | solution.py:216
  114.2 4.8 %collective-permute-start = (f32[8,128]{1,0:T(8,128)S(1)}, f32[8,128]{1,0:T(8,128)S(1)}, u32[]{:S(2)}, u32[]{:S(2)}) collective-permute-start(f32[8,128]{1,0:T(8,128)S(1)} %get-tuple-element.7), channel_id=1, source_target_pairs={{0,1},{1,2},{2,3},{3,0},{64,65},{65,66},{66,67},{67,64},{128,129},... | collective-permute-start | bytes 12296 | tf_op jit(solution)/shard_map/ppermute | solution.py:216
  119.0 7.4 %collective-permute-start.13 = (f32[8,128]{1,0:T(8,128)S(1)}, f32[8,128]{1,0:T(8,128)S(1)}, u32[]{:S(2)}, u32[]{:S(2)}) collective-permute-start(f32[8,128]{1,0:T(8,128)S(1)} %add_add_fusion.2), channel_id=1, source_target_pairs={{0,28},{4,24},{8,20},{12,16},{16,12},{20,8},{24,4},{28,0},{32,60},... | collective-permute-start | bytes 12296 | tf_op jit(solution)/shard_map/ppermute | solution.py:216
  119.1 8.1 %collective-permute-start.12 = (f32[8,128]{1,0:T(8,128)S(1)}, f32[8,128]{1,0:T(8,128)S(1)}, u32[]{:S(2)}, u32[]{:S(2)}) collective-permute-start(f32[8,128]{1,0:T(8,128)S(1)} %add_add_fusion.2), channel_id=1, source_target_pairs={{0,24},{4,28},{8,16},{12,20},{16,8},{20,12},{24,0},{28,4},{32,56},... | collective-permute-start | bytes 12296 | tf_op jit(solution)/shard_map/ppermute | solution.py:216
  121.6 5.7 %collective-permute-start.11 = (f32[8,128]{1,0:T(8,128)S(1)}, f32[8,128]{1,0:T(8,128)S(1)}, u32[]{:S(2)}, u32[]{:S(2)}) collective-permute-start(f32[8,128]{1,0:T(8,128)S(1)} %add_add_fusion.2), channel_id=1, source_target_pairs={{0,20},{4,16},{8,28},{12,24},{16,4},{20,0},{24,12},{28,8},{32,52},... | collective-permute-start | bytes 12296 | tf_op jit(solution)/shard_map/ppermute | solution.py:216
  124.8 5.1 %collective-permute-start.10 = (f32[8,128]{1,0:T(8,128)S(1)}, f32[8,128]{1,0:T(8,128)S(1)}, u32[]{:S(2)}, u32[]{:S(2)}) collective-permute-start(f32[8,128]{1,0:T(8,128)S(1)} %add_add_fusion.2), channel_id=1, source_target_pairs={{0,16},{4,20},{8,24},{12,28},{16,0},{20,4},{24,8},{28,12},{32,48},... | collective-permute-start | bytes 12296 | tf_op jit(solution)/shard_map/ppermute | solution.py:216
  124.8 5.1 %collective-permute-start.9 = (f32[8,128]{1,0:T(8,128)S(1)}, f32[8,128]{1,0:T(8,128)S(1)}, u32[]{:S(2)}, u32[]{:S(2)}) collective-permute-start(f32[8,128]{1,0:T(8,128)S(1)} %add_add_fusion.2), channel_id=1, source_target_pairs={{0,12},{4,8},{8,4},{12,0},{16,28},{20,24},{24,20},{28,16},{32,44},... | collective-permute-start | bytes 12296 | tf_op jit(solution)/shard_map/ppermute | solution.py:216
  126.4 3.6 %collective-permute-start.8 = (f32[8,128]{1,0:T(8,128)S(1)}, f32[8,128]{1,0:T(8,128)S(1)}, u32[]{:S(2)}, u32[]{:S(2)}) collective-permute-start(f32[8,128]{1,0:T(8,128)S(1)} %add_add_fusion.2), channel_id=1, source_target_pairs={{0,8},{4,12},{8,0},{12,4},{16,24},{20,28},{24,16},{28,20},{32,40},... | collective-permute-start | bytes 12296 | tf_op jit(solution)/shard_map/ppermute | solution.py:216
  127.2 2.8 %collective-permute-start.7 = (f32[8,128]{1,0:T(8,128)S(1)}, f32[8,128]{1,0:T(8,128)S(1)}, u32[]{:S(2)}, u32[]{:S(2)}) collective-permute-start(f32[8,128]{1,0:T(8,128)S(1)} %add_add_fusion.2), channel_id=1, source_target_pairs={{0,4},{4,0},{8,12},{12,8},{16,20},{20,16},{24,28},{28,24},{32,36},... | collective-permute-start | bytes 12296 | tf_op jit(solution)/shard_map/ppermute | solution.py:216
  130.0 5.5 %collective-permute-start.16 = (f32[8,128]{1,0:T(8,128)S(1)}, f32[8,128]{1,0:T(8,128)S(1)}, u32[]{:S(2)}, u32[]{:S(2)}) collective-permute-start(f32[8,128]{1,0:T(8,128)S(1)} %add_add_fusion.1), channel_id=1, source_target_pairs={{0,96},{4,100},{8,104},{12,108},{16,112},{20,116},{24,120},{28,124... | collective-permute-start | bytes 12296 | tf_op jit(solution)/shard_map/ppermute | solution.py:216
  130.7 4.8 %collective-permute-start.15 = (f32[8,128]{1,0:T(8,128)S(1)}, f32[8,128]{1,0:T(8,128)S(1)}, u32[]{:S(2)}, u32[]{:S(2)}) collective-permute-start(f32[8,128]{1,0:T(8,128)S(1)} %add_add_fusion.1), channel_id=1, source_target_pairs={{0,64},{4,68},{8,72},{12,76},{16,80},{20,84},{24,88},{28,92},{32,9... | collective-permute-start | bytes 12296 | tf_op jit(solution)/shard_map/ppermute | solution.py:216
  133.0 3.6 %collective-permute-start.14 = (f32[8,128]{1,0:T(8,128)S(1)}, f32[8,128]{1,0:T(8,128)S(1)}, u32[]{:S(2)}, u32[]{:S(2)}) collective-permute-start(f32[8,128]{1,0:T(8,128)S(1)} %add_add_fusion.1), channel_id=1, source_target_pairs={{0,32},{4,36},{8,40},{12,44},{16,48},{20,52},{24,56},{28,60},{32,0... | collective-permute-start | bytes 12296 | tf_op jit(solution)/shard_map/ppermute | solution.py:216

commit v6 on v5

--- a/solution.py
+++ b/solution.py
@@ -51,21 +51,31 @@
             out_ref[place // SLOTS, :, columns] = in_ref[row, :, pl.ds(j * BLOCK, BLOCK)]
 
 
-def collect_kernel(place_ref, sums_ref, in_ref, out_ref):
+def collect_kernel(place_ref, in_ref, out_ref):
+    lane = lax.broadcasted_iota(jnp.int32, (LINES, 128), 1)
+    for row in range(GROUPS):
+        powers = jnp.zeros((LINES, 128), jnp.int32)
+        for j in range(PER_SHARD):
+            place = place_ref[row * PER_SHARD + j]
+            position, slot = place // SLOTS, lax.rem(place, SLOTS)
+            columns = pl.ds(pl.multiple_of(slot * BLOCK, BLOCK), BLOCK)
+            out_ref[row, :, pl.ds(j * BLOCK, BLOCK)] = in_ref[position, :, columns]
+            both = in_ref[position, :, pl.ds(SLOTS * BLOCK, 128)].astype(jnp.int32)
+            powers = jnp.where(lane == j, jnp.where(slot == 0, both[:, 0:1], both[:, 64:65]), powers)
+        out_ref[row, :, pl.ds(PER_SHARD * BLOCK, 128)] = powers.astype(jnp.int16)
+
+
+def finish_kernel(sums_ref, in_ref, out_ref):
     grad_total = sums_ref[0:1, 0:1]
     update_total = sums_ref[1:2, 0:1]
     graft = jnp.sqrt(grad_total / CELLS) * lax.rsqrt(update_total / CELLS + 1e-06)
-    for row in range(GROUPS):
+    for chunk in range(GROUPS):
+        powers = in_ref[chunk, :, pl.ds(PER_SHARD * BLOCK, 128)].astype(jnp.int32).astype(jnp.float32)
+        steps = jnp.exp2(powers) * graft
         for j in range(PER_SHARD):
-            place = place_ref[row * PER_SHARD + j]
-            slot = lax.rem(place, SLOTS)
-            columns = pl.ds(pl.multiple_of(slot * BLOCK, BLOCK), BLOCK)
-            coded = in_ref[place // SLOTS, :, columns].astype(jnp.int32).astype(jnp.float32)
-            steps = jnp.exp2(
-                in_ref[place // SLOTS, :, pl.ds(SLOTS * BLOCK, 128)].astype(jnp.int32).astype(jnp.float32)
-            )
-            step = jnp.where(slot == 0, steps[:, 0:1], steps[:, 64:65])
-            out_ref[row, :, pl.ds(j * BLOCK, BLOCK)] = (coded * (step * graft)).astype(jnp.bfloat16)
+            columns = pl.ds(j * BLOCK, BLOCK)
+            coded = in_ref[chunk, :, columns].astype(jnp.int32).astype(jnp.float32)
+            out_ref[chunk, :, columns] = (coded * steps[:, j : j + 1]).astype(jnp.bfloat16)
 
 
 def dot(a, b):
@@ -216,12 +226,14 @@
     return sum([lax.ppermute(x, axis, perm) for perm in perms], x)
 
 
-def sum_everywhere(x):
-    ends = [[(d, (d ^ t) // 4 * 4 + (d + s) % 4) for d in range(16)] for t in (0, 8) for s in range(4)]
-    x = add_permuted(x, ("g", "mp"), ends[1:])
+def sum_near(x):
+    x = add_permuted(x, "mp", [[(d, (d + s) % SHARDS) for d in range(SHARDS)] for s in range(1, 4)])
     x = add_permuted(x, "r", [[(d, d ^ s) for d in range(MEMBERS)] for s in range(1, 8)])
-    x = add_permuted(x, ("g", "r"), [[(d, d ^ (8 * s)) for d in range(OWNERS)] for s in range(1, 4)])
-    return x
+    return add_permuted(x, ("g", "r"), [[(d, d ^ (8 * s)) for d in range(OWNERS)] for s in range(1, 4)])
+
+
+def sum_far(x):
+    return add_permuted(x, "g", [[(d, d ^ 2) for d in range(GROUPS)]])
 
 
 def shards(gradient, block_owner, prev_left, prev_right):
@@ -291,16 +303,25 @@
     )(me, places, got, prev_left[0, 0], prev_right[0, 0])
 
     returned = exchange(coded, ("r", "g"))
-    sums = sum_everywhere(sums)
+    sums = sum_near(sums)
     back = pl.pallas_call(
         collect_kernel,
-        out_shape=jax.ShapeDtypeStruct(spread_shape, jnp.bfloat16),
-        in_specs=[SMEM, WHOLE, WHOLE],
+        out_shape=jax.ShapeDtypeStruct((GROUPS, LINES, PER_SHARD * BLOCK + 128), jnp.int16),
+        in_specs=[SMEM, WHOLE],
         out_specs=WHOLE,
         compiler_params=params(8),
         name="collect",
-    )(places, sums, returned)
-    update_out = exchange(back, "g").reshape(gradient.shape)
+    )(places, returned)
+    sums, back = lax.optimization_barrier((sums, back))
+    back = exchange(back, "g")
+    update_out = pl.pallas_call(
+        finish_kernel,
+        out_shape=jax.ShapeDtypeStruct(spread_shape, jnp.bfloat16),
+        in_specs=[WHOLE, WHOLE],
+        out_specs=WHOLE,
+        compiler_params=params(8),
+        name="finish",
+    )(sum_far(sums), back).reshape(gradient.shape)
     return (update_out, new_left[None, None], new_right[None, None])
 
 

time: 152 us -> 131 us (0.86)
  blocking collectives: 13.2 us -> 0 us
  starting transfers between devices: 55.4 us -> 49 us
  waiting for transfers between devices: 59.5 us -> 56 us
  Pallas kernels: 21.1 us -> 22.7 us
    all_to_all x1 -> x0, blocking collectives: 13.2 us -> none  [exchange(): return lax.all_to_all(x, axes, split_axis=0, concat_axis=0, tiled=True)]
    ppermute x17 -> x14, starting transfers between devices: 32.6 us -> 21.8 us  [add_permuted(): return sum([lax.ppermute(x, axis, perm) for perm in perms], x)]
    ppermute x17 -> x14, waiting for transfers between devices: 23.9 us -> 18.7 us  [add_permuted(): return sum([lax.ppermute(x, axis, perm) for perm in perms], x)]
    all_to_all x3 -> x4, starting transfers between devices: 22.8 us -> 27.2 us  [exchange(): return lax.all_to_all(x, axes, split_axis=0, concat_axis=0, tiled=True)]
    all_to_all x3 -> x4, waiting for transfers between devices: 35.6 us -> 37.3 us  [exchange(): return lax.all_to_all(x, axes, split_axis=0, concat_axis=0, tiled=True)]
    pallas_call x1 -> x2, Pallas kernels: 0.87 us -> 2.49 us  [the longest x1 1.61 us: shards(): pl.pallas_call(collect_kernel, out_shape=jax.ShapeDtypeStruct((GROUPS, LI...]
  transfers between devices with their start and end apart: 20 -> 18, of which waited for: 9 -> 8; matrix products, arithmetic and copies ran while one was open for 0% -> 0% of each run, Pallas kernels for 1% -> 1%
where the time goes in v6:
time: 131 us; the launch traced here: 129 us
  waiting for transfers between devices  56 us (43%)
  starting transfers between devices  49 us (37%)
  Pallas kernels  22.7 us (17%)
    all_to_all x4, waiting for transfers between devices, exchange(): return lax.all_to_all(x, axes, split_axis=0, concat_axis=0, tiled=True)  37.3 us
    all_to_all x4, starting transfers between devices, exchange(): return lax.all_to_all(x, axes, split_axis=0, concat_axis=0, tiled=True)  27.2 us
    ppermute x14, starting transfers between devices, add_permuted(): return sum([lax.ppermute(x, axis, perm) for perm in perms], x)  21.8 us
    ppermute x14, waiting for transfers between devices, add_permuted(): return sum([lax.ppermute(x, axis, perm) for perm in perms], x)  18.7 us
    pallas_call x1, Pallas kernels, shards(): pl.pallas_call(owner_kernel, grid=(SLOTS,), out_shape=[stat_shape, stat_s...  17.1 us
  transfers between devices with their start and end apart: 18, of which 8 were waited for; matrix products, arithmetic and copies ran while one was open for 0% of the time, Pallas kernels for 1%

profile of v6, /device:TPU:8, one launch (start us, length us, event | category | flops | bytes accessed | tf_op | source)
XLA Modules:
  0.0 129.2 jit_solution(3204962282986958194)
XLA Ops:
  0.6 8.5 %all-to-all-start = ((bf16[4,8,4096]{2,1,0:T(8,128)(2,1)}), bf16[4,8,4096]{2,1,0:T(8,128)(2,1)S(1)}, u32[]{:S(2)}, u32[]{:S(2)}) async-start(bf16[4,8,4096]{2,1,0:T(8,128)(2,1)} %bitcast.11), calls=%async_computation | async-start | bytes 524288 | tf_op jit(solution)/shard_map/all_to_all | solution.py:222
  9.1 0.0 copy-start
  9.1 0.7 copy-done
  9.8 0.0 copy-start.1
  9.8 1.5 %places.1.place_ref = s32[32]{0:T(128)S(1)} custom-call(s32[1]{0:T(128)} %bitcast.1.shard_ref, s32[4,32]{1,0:T(4,128)S(1)} %copy-done), custom_call_target="tpu_custom_call" | custom-call | flops 1000 | bytes 1000 | tf_op jit(solution)/shard_map/places/pallas_call | solution.py:244
  11.3 8.6 %all-to-all-done.in_ref = bf16[4,8,4096]{2,1,0:T(8,128)(2,1)S(1)} async-done(((bf16[4,8,4096]{2,1,0:T(8,128)(2,1)}), bf16[4,8,4096]{2,1,0:T(8,128)(2,1)S(1)}, u32[]{:S(2)}, u32[]{:S(2)}) %all-to-all-start) | async-done | bytes 262176 | tf_op jit(solution)/shard_map/all_to_all | solution.py:222
  19.8 1.7 %route.1 = bf16[64,8,1024]{2,1,0:T(8,128)(2,1)} custom-call(s32[32]{0:T(128)S(1)} %places.1.place_ref, bf16[4,8,4096]{2,1,0:T(8,128)(2,1)S(1)} %all-to-all-done.in_ref), custom_call_target="tpu_custom_call" | custom-call | tf_op jit(solution)/shard_map/route/pallas_call | solution.py:255
  21.5 6.6 %all-to-all-start.1 = ((bf16[64,8,1024]{2,1,0:T(8,128)(2,1)}), bf16[64,8,1024]{2,1,0:T(8,128)(2,1)S(1)}, u32[]{:S(2)}, u32[]{:S(2)}) async-start(bf16[64,8,1024]{2,1,0:T(8,128)(2,1)} %route.1), calls=%async_computation.1 | async-start | bytes 2097152 | tf_op jit(solution)/shard_map/all_to_all | solution.py:222
  28.2 27.1 %all-to-all-done.1 = bf16[64,8,1024]{2,1,0:T(8,128)(2,1)S(1)} async-done(((bf16[64,8,1024]{2,1,0:T(8,128)(2,1)}), bf16[64,8,1024]{2,1,0:T(8,128)(2,1)S(1)}, u32[]{:S(2)}, u32[]{:S(2)}) %all-to-all-start.1) | async-done | bytes 1048608 | tf_op jit(solution)/shard_map/all_to_all | solution.py:222
  55.2 0.0 copy-done.1
  55.2 17.1 %owner.1 = (f32[2,512,512]{2,1,0:T(8,128)}, f32[2,512,512]{2,1,0:T(8,128)}, s16[64,8,1152]{2,1,0:T(8,128)(2,1)}, f32[8,128]{1,0:T(8,128)S(1)}) custom-call(s32[1]{0:T(128)} %bitcast.me_ref, s32[32]{0:T(128)S(1)} %places.1.place_ref, bf16[512,1024]{1,0:T(8,128)(2,1)S(1)} %bitcast.9, f32[2,512,512]{2,1,0:T(8,128)S(1)} %bitcast.10, f32[2,512,512]{2,1,0:T(8,128)} %bitcast.13), custom_call_target="tpu_custom_call" | custom-call | flops 13421772800 | bytes 12582912 | tf_op jit(solution)/shard_map/owner/pallas_call | solution.py:269
  72.3 7.7 %all-to-all-start.2 = ((s16[64,8,1152]{2,1,0:T(8,128)(2,1)}), s16[64,8,1152]{2,1,0:T(8,128)(2,1)S(1)}, u32[]{:S(2)}, u32[]{:S(2)}) async-start(s16[64,8,1152]{2,1,0:T(8,128)(2,1)} %get-tuple-element.10), calls=%async_computation.2 | async-start | bytes 2359296 | tf_op jit(solution)/shard_map/all_to_all | solution.py:222
  80.0 2.8 %collective-permute-start.2 = (f32[8,128]{1,0:T(8,128)S(1)}, f32[8,128]{1,0:T(8,128)S(1)}, u32[]{:S(2)}, u32[]{:S(2)}) collective-permute-start(f32[8,128]{1,0:T(8,128)S(1)} %get-tuple-element.9), channel_id=1, source_target_pairs={{0,3},{1,0},{2,1},{3,2},{4,7},{5,4},{6,5},{7,6},{8,11},{9,8},{10,9... | collective-permute-start | bytes 12296 | tf_op jit(solution)/shard_map/ppermute | solution.py:226
  82.9 0.8 collective-permute-start.1
  83.7 0.9 collective-permute-start
  84.5 0.0 collective-permute-done.2
  84.5 3.4 %collective-permute-done.1 = f32[8,128]{1,0:T(8,128)S(1)} collective-permute-done((f32[8,128]{1,0:T(8,128)S(1)}, f32[8,128]{1,0:T(8,128)S(1)}, u32[]{:S(2)}, u32[]{:S(2)}) %collective-permute-start.1) | collective-permute-done | bytes 4128 | tf_op jit(solution)/shard_map/ppermute | solution.py:226
  88.0 0.5 collective-permute-done
  88.5 0.0 collective-permute-start.9
  88.5 1.6 %collective-permute-start.8 = (f32[8,128]{1,0:T(8,128)S(1)}, f32[8,128]{1,0:T(8,128)S(1)}, u32[]{:S(2)}, u32[]{:S(2)}) collective-permute-start(f32[8,128]{1,0:T(8,128)S(1)} %add_add_fusion.2), channel_id=1, source_target_pairs={{0,24},{4,28},{8,16},{12,20},{16,8},{20,12},{24,0},{28,4},{32,56},... | collective-permute-start | bytes 12296 | tf_op jit(solution)/shard_map/ppermute | solution.py:226
  90.0 3.2 %collective-permute-start.7 = (f32[8,128]{1,0:T(8,128)S(1)}, f32[8,128]{1,0:T(8,128)S(1)}, u32[]{:S(2)}, u32[]{:S(2)}) collective-permute-start(f32[8,128]{1,0:T(8,128)S(1)} %add_add_fusion.2), channel_id=1, source_target_pairs={{0,20},{4,16},{8,28},{12,24},{16,4},{20,0},{24,12},{28,8},{32,52},... | collective-permute-start | bytes 12296 | tf_op jit(solution)/shard_map/ppermute | solution.py:226
  93.3 0.2 collective-permute-start.6
  93.5 1.3 %collective-permute-start.5 = (f32[8,128]{1,0:T(8,128)S(1)}, f32[8,128]{1,0:T(8,128)S(1)}, u32[]{:S(2)}, u32[]{:S(2)}) collective-permute-start(f32[8,128]{1,0:T(8,128)S(1)} %add_add_fusion.2), channel_id=1, source_target_pairs={{0,12},{4,8},{8,4},{12,0},{16,28},{20,24},{24,20},{28,16},{32,44},... | collective-permute-start | bytes 12296 | tf_op jit(solution)/shard_map/ppermute | solution.py:226
  94.8 0.0 collective-permute-done.9
  94.8 0.4 collective-permute-start.4
  95.2 0.0 collective-permute-done.8
  95.2 0.2 collective-permute-start.3
  95.4 0.0 collective-permute-done.7
  95.4 3.1 %collective-permute-done.6 = f32[8,128]{1,0:T(8,128)S(1)} collective-permute-done((f32[8,128]{1,0:T(8,128)S(1)}, f32[8,128]{1,0:T(8,128)S(1)}, u32[]{:S(2)}, u32[]{:S(2)}) %collective-permute-start.6) | collective-permute-done | bytes 4128 | tf_op jit(solution)/shard_map/ppermute | solution.py:226
  98.5 0.0 collective-permute-done.5
  98.5 0.0 collective-permute-done.4
  98.5 0.0 collective-permute-done.3
  98.5 3.6 %collective-permute-start.12 = (f32[8,128]{1,0:T(8,128)S(1)}, f32[8,128]{1,0:T(8,128)S(1)}, u32[]{:S(2)}, u32[]{:S(2)}) collective-permute-start(f32[8,128]{1,0:T(8,128)S(1)} %add_add_fusion.1), channel_id=1, source_target_pairs={{0,96},{4,100},{8,104},{12,108},{16,112},{20,116},{24,120},{28,124... | collective-permute-start | bytes 12296 | tf_op jit(solution)/shard_map/ppermute | solution.py:226
  102.1 0.0 collective-permute-start.11
  102.1 0.8 collective-permute-start.10
  103.0 5.5 %collective-permute-done.12 = f32[8,128]{1,0:T(8,128)S(1)} collective-permute-done((f32[8,128]{1,0:T(8,128)S(1)}, f32[8,128]{1,0:T(8,128)S(1)}, u32[]{:S(2)}, u32[]{:S(2)}) %collective-permute-start.12) | collective-permute-done | bytes 4128 | tf_op jit(solution)/shard_map/ppermute | solution.py:226
  108.5 0.0 collective-permute-done.11
  108.5 0.0 collective-permute-done.10
  108.5 1.7 %all-to-all-done.2.in_ref = s16[64,8,1152]{2,1,0:T(8,128)(2,1)S(1)} async-done(((s16[64,8,1152]{2,1,0:T(8,128)(2,1)}), s16[64,8,1152]{2,1,0:T(8,128)(2,1)S(1)}, u32[]{:S(2)}, u32[]{:S(2)}) %all-to-all-start.2) | async-done | bytes 1179680 | tf_op jit(solution)/shard_map/all_to_all | solution.py:222
  110.2 1.6 %collect.1 = s16[4,8,4224]{2,1,0:T(8,128)(2,1)} custom-call(s32[32]{0:T(128)S(1)} %places.1.place_ref, s16[64,8,1152]{2,1,0:T(8,128)(2,1)S(1)} %all-to-all-done.2.in_ref), custom_call_target="tpu_custom_call" | custom-call | tf_op jit(solution)/shard_map/collect/pallas_call | solution.py:307
  111.8 4.4 %all-to-all-start.3 = ((s16[4,8,4224]{2,1,0:T(8,128)(2,1)}), s16[4,8,4224]{2,1,0:T(8,128)(2,1)S(1)}, u32[]{:S(2)}, u32[]{:S(2)}) async-start(s16[4,8,4224]{2,1,0:T(8,128)(2,1)} %collect.1), calls=%async_computation.3 | async-start | bytes 540672 | tf_op jit(solution)/shard_map/all_to_all | solution.py:222
  116.2 5.9 %collective-permute-start.13 = (f32[8,128]{1,0:T(8,128)S(1)}, f32[8,128]{1,0:T(8,128)S(1)}, u32[]{:S(2)}, u32[]{:S(2)}) collective-permute-start(f32[8,128]{1,0:T(8,128)S(1)} %add_add_fusion), channel_id=1, source_target_pairs={{0,128},{64,192},{128,0},{192,64},{1,129},{65,193},{129,1},{193,65... | collective-permute-start | bytes 12296 | tf_op jit(solution)/shard_map/ppermute | solution.py:226
  122.1 6.1 %collective-permute-done.13 = f32[8,128]{1,0:T(8,128)S(1)} collective-permute-done((f32[8,128]{1,0:T(8,128)S(1)}, f32[8,128]{1,0:T(8,128)S(1)}, u32[]{:S(2)}, u32[]{:S(2)}) %collective-permute-start.13) | collective-permute-done | bytes 4128 | tf_op jit(solution)/shard_map/ppermute | solution.py:226
  128.3 0.0 all-to-all-done.3.in_ref
  128.3 0.9 finish.1
  (4 shorter events, 0.0 us)
Async XLA Ops:
  0.6 19.2 %all-to-all-start = ((bf16[4,8,4096]{2,1,0:T(8,128)(2,1)}), bf16[4,8,4096]{2,1,0:T(8,128)(2,1)S(1)}, u32[]{:S(2)}, u32[]{:S(2)}) async-start(bf16[4,8,4096]{2,1,0:T(8,128)(2,1)} %bitcast.11), calls=%async_computation | async-start | bytes 524288 | tf_op jit(solution)/shard_map/all_to_all | solution.py:222
  9.1 0.7 copy-start
  9.8 45.5 %copy-start.1 = (f32[1,1,2,512,512]{4,3,2,1,0:T(8,128)S(1)}, f32[1,1,2,512,512]{4,3,2,1,0:T(8,128)}, u32[]{:S(2)}) copy-start(f32[1,1,2,512,512]{4,3,2,1,0:T(8,128)} %param.6) | copy-start | bytes 6291460
  21.5 33.7 %all-to-all-start.1 = ((bf16[64,8,1024]{2,1,0:T(8,128)(2,1)}), bf16[64,8,1024]{2,1,0:T(8,128)(2,1)S(1)}, u32[]{:S(2)}, u32[]{:S(2)}) async-start(bf16[64,8,1024]{2,1,0:T(8,128)(2,1)} %route.1), calls=%async_computation.1 | async-start | bytes 2097152 | tf_op jit(solution)/shard_map/all_to_all | solution.py:222
  72.3 37.8 %all-to-all-start.2 = ((s16[64,8,1152]{2,1,0:T(8,128)(2,1)}), s16[64,8,1152]{2,1,0:T(8,128)(2,1)S(1)}, u32[]{:S(2)}, u32[]{:S(2)}) async-start(s16[64,8,1152]{2,1,0:T(8,128)(2,1)} %get-tuple-element.10), calls=%async_computation.2 | async-start | bytes 2359296 | tf_op jit(solution)/shard_map/all_to_all | solution.py:222
  80.0 4.5 %collective-permute-start.2 = (f32[8,128]{1,0:T(8,128)S(1)}, f32[8,128]{1,0:T(8,128)S(1)}, u32[]{:S(2)}, u32[]{:S(2)}) collective-permute-start(f32[8,128]{1,0:T(8,128)S(1)} %get-tuple-element.9), channel_id=1, source_target_pairs={{0,3},{1,0},{2,1},{3,2},{4,7},{5,4},{6,5},{7,6},{8,11},{9,8},{10,9... | collective-permute-start | bytes 12296 | tf_op jit(solution)/shard_map/ppermute | solution.py:226
  82.9 5.1 %collective-permute-start.1 = (f32[8,128]{1,0:T(8,128)S(1)}, f32[8,128]{1,0:T(8,128)S(1)}, u32[]{:S(2)}, u32[]{:S(2)}) collective-permute-start(f32[8,128]{1,0:T(8,128)S(1)} %get-tuple-element.9), channel_id=1, source_target_pairs={{0,2},{1,3},{2,0},{3,1},{4,6},{5,7},{6,4},{7,5},{8,10},{9,11},{10,... | collective-permute-start | bytes 12296 | tf_op jit(solution)/shard_map/ppermute | solution.py:226
  83.7 4.8 %collective-permute-start = (f32[8,128]{1,0:T(8,128)S(1)}, f32[8,128]{1,0:T(8,128)S(1)}, u32[]{:S(2)}, u32[]{:S(2)}) collective-permute-start(f32[8,128]{1,0:T(8,128)S(1)} %get-tuple-element.9), channel_id=1, source_target_pairs={{0,1},{1,2},{2,3},{3,0},{4,5},{5,6},{6,7},{7,4},{8,9},{9,10},{10,1... | collective-permute-start | bytes 12296 | tf_op jit(solution)/shard_map/ppermute | solution.py:226
  88.5 6.3 %collective-permute-start.9 = (f32[8,128]{1,0:T(8,128)S(1)}, f32[8,128]{1,0:T(8,128)S(1)}, u32[]{:S(2)}, u32[]{:S(2)}) collective-permute-start(f32[8,128]{1,0:T(8,128)S(1)} %add_add_fusion.2), channel_id=1, source_target_pairs={{0,28},{4,24},{8,20},{12,16},{16,12},{20,8},{24,4},{28,0},{32,60},... | collective-permute-start | bytes 12296 | tf_op jit(solution)/shard_map/ppermute | solution.py:226
  88.5 6.7 %collective-permute-start.8 = (f32[8,128]{1,0:T(8,128)S(1)}, f32[8,128]{1,0:T(8,128)S(1)}, u32[]{:S(2)}, u32[]{:S(2)}) collective-permute-start(f32[8,128]{1,0:T(8,128)S(1)} %add_add_fusion.2), channel_id=1, source_target_pairs={{0,24},{4,28},{8,16},{12,20},{16,8},{20,12},{24,0},{28,4},{32,56},... | collective-permute-start | bytes 12296 | tf_op jit(solution)/shard_map/ppermute | solution.py:226
  90.0 5.3 %collective-permute-start.7 = (f32[8,128]{1,0:T(8,128)S(1)}, f32[8,128]{1,0:T(8,128)S(1)}, u32[]{:S(2)}, u32[]{:S(2)}) collective-permute-start(f32[8,128]{1,0:T(8,128)S(1)} %add_add_fusion.2), channel_id=1, source_target_pairs={{0,20},{4,16},{8,28},{12,24},{16,4},{20,0},{24,12},{28,8},{32,52},... | collective-permute-start | bytes 12296 | tf_op jit(solution)/shard_map/ppermute | solution.py:226
  93.3 5.2 %collective-permute-start.6 = (f32[8,128]{1,0:T(8,128)S(1)}, f32[8,128]{1,0:T(8,128)S(1)}, u32[]{:S(2)}, u32[]{:S(2)}) collective-permute-start(f32[8,128]{1,0:T(8,128)S(1)} %add_add_fusion.2), channel_id=1, source_target_pairs={{0,16},{4,20},{8,24},{12,28},{16,0},{20,4},{24,8},{28,12},{32,48},... | collective-permute-start | bytes 12296 | tf_op jit(solution)/shard_map/ppermute | solution.py:226
  93.5 5.0 %collective-permute-start.5 = (f32[8,128]{1,0:T(8,128)S(1)}, f32[8,128]{1,0:T(8,128)S(1)}, u32[]{:S(2)}, u32[]{:S(2)}) collective-permute-start(f32[8,128]{1,0:T(8,128)S(1)} %add_add_fusion.2), channel_id=1, source_target_pairs={{0,12},{4,8},{8,4},{12,0},{16,28},{20,24},{24,20},{28,16},{32,44},... | collective-permute-start | bytes 12296 | tf_op jit(solution)/shard_map/ppermute | solution.py:226
  94.8 3.6 %collective-permute-start.4 = (f32[8,128]{1,0:T(8,128)S(1)}, f32[8,128]{1,0:T(8,128)S(1)}, u32[]{:S(2)}, u32[]{:S(2)}) collective-permute-start(f32[8,128]{1,0:T(8,128)S(1)} %add_add_fusion.2), channel_id=1, source_target_pairs={{0,8},{4,12},{8,0},{12,4},{16,24},{20,28},{24,16},{28,20},{32,40},... | collective-permute-start | bytes 12296 | tf_op jit(solution)/shard_map/ppermute | solution.py:226
  95.2 3.3 %collective-permute-start.3 = (f32[8,128]{1,0:T(8,128)S(1)}, f32[8,128]{1,0:T(8,128)S(1)}, u32[]{:S(2)}, u32[]{:S(2)}) collective-permute-start(f32[8,128]{1,0:T(8,128)S(1)} %add_add_fusion.2), channel_id=1, source_target_pairs={{0,4},{4,0},{8,12},{12,8},{16,20},{20,16},{24,28},{28,24},{32,36},... | collective-permute-start | bytes 12296 | tf_op jit(solution)/shard_map/ppermute | solution.py:226
  98.5 10.0 %collective-permute-start.12 = (f32[8,128]{1,0:T(8,128)S(1)}, f32[8,128]{1,0:T(8,128)S(1)}, u32[]{:S(2)}, u32[]{:S(2)}) collective-permute-start(f32[8,128]{1,0:T(8,128)S(1)} %add_add_fusion.1), channel_id=1, source_target_pairs={{0,96},{4,100},{8,104},{12,108},{16,112},{20,116},{24,120},{28,124... | collective-permute-start | bytes 12296 | tf_op jit(solution)/shard_map/ppermute | solution.py:226
  102.1 6.3 %collective-permute-start.11 = (f32[8,128]{1,0:T(8,128)S(1)}, f32[8,128]{1,0:T(8,128)S(1)}, u32[]{:S(2)}, u32[]{:S(2)}) collective-permute-start(f32[8,128]{1,0:T(8,128)S(1)} %add_add_fusion.1), channel_id=1, source_target_pairs={{0,64},{4,68},{8,72},{12,76},{16,80},{20,84},{24,88},{28,92},{32,9... | collective-permute-start | bytes 12296 | tf_op jit(solution)/shard_map/ppermute | solution.py:226
  102.1 6.3 %collective-permute-start.10 = (f32[8,128]{1,0:T(8,128)S(1)}, f32[8,128]{1,0:T(8,128)S(1)}, u32[]{:S(2)}, u32[]{:S(2)}) collective-permute-start(f32[8,128]{1,0:T(8,128)S(1)} %add_add_fusion.1), channel_id=1, source_target_pairs={{0,32},{4,36},{8,40},{12,44},{16,48},{20,52},{24,56},{28,60},{32,0... | collective-permute-start | bytes 12296 | tf_op jit(solution)/shard_map/ppermute | solution.py:226
  111.8 16.5 %all-to-all-start.3 = ((s16[4,8,4224]{2,1,0:T(8,128)(2,1)}), s16[4,8,4224]{2,1,0:T(8,128)(2,1)S(1)}, u32[]{:S(2)}, u32[]{:S(2)}) async-start(s16[4,8,4224]{2,1,0:T(8,128)(2,1)} %collect.1), calls=%async_computation.3 | async-start | bytes 540672 | tf_op jit(solution)/shard_map/all_to_all | solution.py:222
  116.2 12.1 %collective-permute-start.13 = (f32[8,128]{1,0:T(8,128)S(1)}, f32[8,128]{1,0:T(8,128)S(1)}, u32[]{:S(2)}, u32[]{:S(2)}) collective-permute-start(f32[8,128]{1,0:T(8,128)S(1)} %add_add_fusion), channel_id=1, source_target_pairs={{0,128},{64,192},{128,0},{192,64},{1,129},{65,193},{129,1},{193,65... | collective-permute-start | bytes 12296 | tf_op jit(solution)/shard_map/ppermute | solution.py:226

commit v7 on v6

--- a/solution.py
+++ b/solution.py
@@ -43,12 +43,16 @@
         place_ref[b] = (lax.rem(owner, MEMBERS) * GROUPS + owner // MEMBERS) * SLOTS + slot
 
 
-def route_kernel(place_ref, in_ref, out_ref):
+def route_kernel(group_ref, place_ref, in_ref, out_ref):
     for row in range(GROUPS):
         for j in range(PER_SHARD):
             place = place_ref[row * PER_SHARD + j]
-            columns = pl.ds(pl.multiple_of(lax.rem(place, SLOTS) * BLOCK, BLOCK), BLOCK)
-            out_ref[place // SLOTS, :, columns] = in_ref[row, :, pl.ds(j * BLOCK, BLOCK)]
+            position = place // SLOTS
+
+            @pl.when(lax.rem(position, GROUPS) == group_ref[0])
+            def _():
+                columns = pl.ds(pl.multiple_of(lax.rem(place, SLOTS) * BLOCK, BLOCK), BLOCK)
+                out_ref[position // GROUPS, :, columns] = in_ref[row, :, pl.ds(j * BLOCK, BLOCK)]
 
 
 def collect_kernel(place_ref, in_ref, out_ref):
@@ -61,7 +65,7 @@
             columns = pl.ds(pl.multiple_of(slot * BLOCK, BLOCK), BLOCK)
             out_ref[row, :, pl.ds(j * BLOCK, BLOCK)] = in_ref[position, :, columns]
             both = in_ref[position, :, pl.ds(SLOTS * BLOCK, 128)].astype(jnp.int32)
-            powers = jnp.where(lane == j, jnp.where(slot == 0, both[:, 0:1], both[:, 64:65]), powers)
+            powers = jnp.where(lane == j + 64 * slot, both, powers)
         out_ref[row, :, pl.ds(PER_SHARD * BLOCK, 128)] = powers.astype(jnp.int16)
 
 
@@ -71,7 +75,7 @@
     graft = jnp.sqrt(grad_total / CELLS) * lax.rsqrt(update_total / CELLS + 1e-06)
     for chunk in range(GROUPS):
         powers = in_ref[chunk, :, pl.ds(PER_SHARD * BLOCK, 128)].astype(jnp.int32).astype(jnp.float32)
-        steps = jnp.exp2(powers) * graft
+        steps = jnp.exp2(powers + pltpu.roll(powers, 64, 1)) * graft
         for j in range(PER_SHARD):
             columns = pl.ds(j * BLOCK, BLOCK)
             coded = in_ref[chunk, :, columns].astype(jnp.int32).astype(jnp.float32)
@@ -226,14 +230,14 @@
     return sum([lax.ppermute(x, axis, perm) for perm in perms], x)
 
 
-def sum_near(x):
-    x = add_permuted(x, "mp", [[(d, (d + s) % SHARDS) for d in range(SHARDS)] for s in range(1, 4)])
+def sum_dp(x):
     x = add_permuted(x, "r", [[(d, d ^ s) for d in range(MEMBERS)] for s in range(1, 8)])
-    return add_permuted(x, ("g", "r"), [[(d, d ^ (8 * s)) for d in range(OWNERS)] for s in range(1, 4)])
-
-
-def sum_far(x):
+    x = add_permuted(x, ("g", "r"), [[(d, d ^ (8 * s)) for d in range(OWNERS)] for s in range(1, 4)])
     return add_permuted(x, "g", [[(d, d ^ 2) for d in range(GROUPS)]])
+
+
+def sum_mp(x):
+    return add_permuted(x, "mp", [[(d, (d + s) % SHARDS) for d in range(SHARDS)] for s in range(1, 4)])
 
 
 def shards(gradient, block_owner, prev_left, prev_right):
@@ -251,16 +255,17 @@
         cost_estimate=pl.CostEstimate(flops=1000, bytes_accessed=1000, transcendentals=0),
         name="places",
     )(shard, block_owner)
-    pieces = exchange(gradient.reshape(spread_shape), "g")
+    group = jnp.reshape(lax.axis_index("g"), (1,)).astype(jnp.int32)
+    rows = lax.all_gather(gradient, "g", axis=0)
     routed = pl.pallas_call(
         route_kernel,
-        out_shape=jax.ShapeDtypeStruct((OWNERS, LINES, SLOTS * BLOCK), jnp.bfloat16),
-        in_specs=[SMEM, WHOLE],
+        out_shape=jax.ShapeDtypeStruct((MEMBERS, BLOCK // MEMBERS, SLOTS * BLOCK), jnp.bfloat16),
+        in_specs=[SMEM, SMEM, WHOLE],
         out_specs=WHOLE,
-        compiler_params=params(4),
+        compiler_params=params(8),
         name="route",
-    )(places, pieces)
-    got = exchange(routed, ("r", "g")).reshape(BLOCK, SLOTS * BLOCK)
+    )(group, places, rows)
+    got = exchange(routed, "r").reshape(BLOCK, SLOTS * BLOCK)
 
     stat_spec = pl.BlockSpec(memory_space=pl.ANY)
     parts = pltpu.VMEM((2, 2, BLOCK, BLOCK), jnp.bfloat16)
@@ -303,7 +308,7 @@
     )(me, places, got, prev_left[0, 0], prev_right[0, 0])
 
     returned = exchange(coded, ("r", "g"))
-    sums = sum_near(sums)
+    sums = sum_dp(sums)
     back = pl.pallas_call(
         collect_kernel,
         out_shape=jax.ShapeDtypeStruct((GROUPS, LINES, PER_SHARD * BLOCK + 128), jnp.int16),
@@ -321,7 +326,7 @@
         out_specs=WHOLE,
         compiler_params=params(8),
         name="finish",
-    )(sum_far(sums), back).reshape(gradient.shape)
+    )(sum_mp(sums), back).reshape(gradient.shape)
     return (update_out, new_left[None, None], new_right[None, None])
 
 

time: 131 us -> 156 us (1.19)
  waiting for transfers between devices: 56 us -> 78.1 us
  between operations: 0.7 us -> 14.1 us
  starting transfers between devices: 49 us -> 38.6 us
    all_gather x0 -> x1, waiting for transfers between devices: none -> 38 us  [shards(): rows = lax.all_gather(gradient, 'g', axis=0)]
    all_to_all x4 -> x3, waiting for transfers between devices: 37.3 us -> 15 us  [exchange(): return lax.all_to_all(x, axes, split_axis=0, concat_axis=0, tiled=True)]
    all_to_all x4 -> x3, starting transfers between devices: 27.2 us -> 18.5 us  [exchange(): return lax.all_to_all(x, axes, split_axis=0, concat_axis=0, tiled=True)]
    ppermute x14, waiting for transfers between devices: 18.7 us -> 24.4 us  [add_permuted(): return sum([lax.ppermute(x, axis, perm) for perm in perms], x)]
    ppermute x14, starting transfers between devices: 21.8 us -> 20 us  [add_permuted(): return sum([lax.ppermute(x, axis, perm) for perm in perms], x)]
where the time goes in v7:
time: 156 us
  waiting for transfers between devices  78.1 us (50%)
  starting transfers between devices  38.6 us (25%)
  Pallas kernels  22.9 us (15%)
  between operations  14.1 us (9%)
  local copies, waits for them, and re-layouts  1.9 us (1%)
    all_gather x1, waiting for transfers between devices, shards(): rows = lax.all_gather(gradient, 'g', axis=0)  38 us
    ppermute x14, waiting for transfers between devices, add_permuted(): return sum([lax.ppermute(x, axis, perm) for perm in perms], x)  24.4 us
    ppermute x14, starting transfers between devices, add_permuted(): return sum([lax.ppermute(x, axis, perm) for perm in perms], x)  20 us
    all_to_all x3, starting transfers between devices, exchange(): return lax.all_to_all(x, axes, split_axis=0, concat_axis=0, tiled=True)  18.5 us
    pallas_call x1, Pallas kernels, shards(): pl.pallas_call(owner_kernel, grid=(SLOTS,), out_shape=[stat_shape, stat_s...  16.9 us
    all_to_all x3, waiting for transfers between devices, exchange(): return lax.all_to_all(x, axes, split_axis=0, concat_axis=0, tiled=True)  15 us
  transfers between devices with their start and end apart: 18, of which 8 were waited for; matrix products, arithmetic and copies ran while one was open for 0% of the time, Pallas kernels for 1%

profile of v7, /device:TPU:8, one launch (start us, length us, event | category | flops | bytes accessed | tf_op | source)
XLA Modules:
  0.0 155.6 jit_solution(7434947322899041326)
XLA Ops:
  7.2 0.0 all-gather.3.cloned.1.call-start
  7.2 0.7 all-gather.3.cloned.1.call-update
  7.9 0.0 copy-start.1
  7.9 0.7 copy-done.1
  8.6 1.5 places.1.place_ref
  10.1 38.0 %all-gather.3.cloned.1.call-done = bf16[128,4096]{1,0:T(8,128)(2,1)} async-done(((bf16[32,4096]{1,0:T(8,128)(2,1)}), bf16[128,4096]{1,0:T(8,128)(2,1)}) %all-gather.3.cloned.1.call-update) | async-done | bytes 1048592 | tf_op jit(solution)/shard_map/all_gather | solution.py:259
  48.1 0.0 copy-start
  48.1 1.2 copy-done
  49.3 0.0 copy-start.2
  49.3 2.1 %route.1 = bf16[16,32,1024]{2,1,0:T(8,128)(2,1)} custom-call(s32[1]{0:T(128)} %bitcast.2.group_ref, s32[32]{0:T(128)S(1)} %places.1.place_ref, bf16[4,32,4096]{2,1,0:T(8,128)(2,1)S(1)} %bitcast.11), custom_call_target="tpu_custom_call" | custom-call | tf_op jit(solution)/shard_map/route/pallas_call | solution.py:260
  51.4 4.8 %all-to-all-start = ((bf16[16,32,1024]{2,1,0:T(8,128)(2,1)}), bf16[16,32,1024]{2,1,0:T(8,128)(2,1)S(1)}, u32[]{:S(2)}, u32[]{:S(2)}) async-start(bf16[16,32,1024]{2,1,0:T(8,128)(2,1)} %route.1), calls=%async_computation | async-start | bytes 2097152 | tf_op jit(solution)/shard_map/all_to_all | solution.py:226
  56.3 13.5 %all-to-all-done = bf16[16,32,1024]{2,1,0:T(8,128)(2,1)S(1)} async-done(((bf16[16,32,1024]{2,1,0:T(8,128)(2,1)}), bf16[16,32,1024]{2,1,0:T(8,128)(2,1)S(1)}, u32[]{:S(2)}, u32[]{:S(2)}) %all-to-all-start) | async-done | bytes 1048608 | tf_op jit(solution)/shard_map/all_to_all | solution.py:226
  69.8 0.0 copy-done.2
  69.8 16.9 %owner.1 = (f32[2,512,512]{2,1,0:T(8,128)}, f32[2,512,512]{2,1,0:T(8,128)}, s16[64,8,1152]{2,1,0:T(8,128)(2,1)}, f32[8,128]{1,0:T(8,128)S(1)}) custom-call(s32[1]{0:T(128)} %bitcast.me_ref, s32[32]{0:T(128)S(1)} %places.1.place_ref, bf16[512,1024]{1,0:T(8,128)(2,1)S(1)} %bitcast.10, f32[2,512,512]{2,1,0:T(8,128)S(1)} %bitcast.12, f32[2,512,512]{2,1,0:T(8,128)} %bitcast.14), custom_call_target="tpu_custom_call" | custom-call | flops 13421772800 | bytes 12582912 | tf_op jit(solution)/shard_map/owner/pallas_call | solution.py:274
  86.7 8.4 %all-to-all-start.1 = ((s16[64,8,1152]{2,1,0:T(8,128)(2,1)}), s16[64,8,1152]{2,1,0:T(8,128)(2,1)S(1)}, u32[]{:S(2)}, u32[]{:S(2)}) async-start(s16[64,8,1152]{2,1,0:T(8,128)(2,1)} %get-tuple-element.10), calls=%async_computation.1 | async-start | bytes 2359296 | tf_op jit(solution)/shard_map/all_to_all | solution.py:226
  95.2 1.3 collective-permute-start.6
  96.5 0.6 collective-permute-start.5
  97.0 3.0 %collective-permute-start.4 = (f32[8,128]{1,0:T(8,128)S(1)}, f32[8,128]{1,0:T(8,128)S(1)}, u32[]{:S(2)}, u32[]{:S(2)}) collective-permute-start(f32[8,128]{1,0:T(8,128)S(1)} %get-tuple-element.9), channel_id=1, source_target_pairs={{0,20},{4,16},{8,28},{12,24},{16,4},{20,0},{24,12},{28,8},{32,52},... | collective-permute-start | bytes 12296 | tf_op jit(solution)/shard_map/ppermute | solution.py:230
  100.0 0.4 collective-permute-start.3
  100.4 1.2 collective-permute-start.2
  101.6 0.0 collective-permute-done.6
  101.6 0.5 collective-permute-start.1
  102.1 0.0 collective-permute-done.5
  102.1 0.2 collective-permute-start
  102.3 0.0 collective-permute-done.4
  102.3 2.9 %collective-permute-done.3 = f32[8,128]{1,0:T(8,128)S(1)} collective-permute-done((f32[8,128]{1,0:T(8,128)S(1)}, f32[8,128]{1,0:T(8,128)S(1)}, u32[]{:S(2)}, u32[]{:S(2)}) %collective-permute-start.3) | collective-permute-done | bytes 4128 | tf_op jit(solution)/shard_map/ppermute | solution.py:230
  105.2 0.0 collective-permute-done.2
  105.2 0.0 collective-permute-done.1
  105.2 0.0 collective-permute-done
  105.2 3.6 %collective-permute-start.9 = (f32[8,128]{1,0:T(8,128)S(1)}, f32[8,128]{1,0:T(8,128)S(1)}, u32[]{:S(2)}, u32[]{:S(2)}) collective-permute-start(f32[8,128]{1,0:T(8,128)S(1)} %add_add_fusion.2), channel_id=1, source_target_pairs={{0,96},{4,100},{8,104},{12,108},{16,112},{20,116},{24,120},{28,124... | collective-permute-start | bytes 12296 | tf_op jit(solution)/shard_map/ppermute | solution.py:230
  108.9 0.0 collective-permute-start.8
  108.9 0.9 collective-permute-start.7
  109.7 13.9 %collective-permute-done.9 = f32[8,128]{1,0:T(8,128)S(1)} collective-permute-done((f32[8,128]{1,0:T(8,128)S(1)}, f32[8,128]{1,0:T(8,128)S(1)}, u32[]{:S(2)}, u32[]{:S(2)}) %collective-permute-start.9) | collective-permute-done | bytes 4128 | tf_op jit(solution)/shard_map/ppermute | solution.py:230
  123.6 0.0 collective-permute-done.8
  123.6 0.0 collective-permute-done.7
  123.6 4.0 %collective-permute-start.10 = (f32[8,128]{1,0:T(8,128)S(1)}, f32[8,128]{1,0:T(8,128)S(1)}, u32[]{:S(2)}, u32[]{:S(2)}) collective-permute-start(f32[8,128]{1,0:T(8,128)S(1)} %add_add_fusion.1), channel_id=1, source_target_pairs={{0,128},{64,192},{128,0},{192,64},{1,129},{65,193},{129,1},{193,65... | collective-permute-start | bytes 12296 | tf_op jit(solution)/shard_map/ppermute | solution.py:230
  127.7 3.6 %collective-permute-done.10 = f32[8,128]{1,0:T(8,128)S(1)} collective-permute-done((f32[8,128]{1,0:T(8,128)S(1)}, f32[8,128]{1,0:T(8,128)S(1)}, u32[]{:S(2)}, u32[]{:S(2)}) %collective-permute-start.10) | collective-permute-done | bytes 4128 | tf_op jit(solution)/shard_map/ppermute | solution.py:230
  131.2 0.0 all-to-all-done.1.in_ref
  131.2 1.5 collect.1
  132.7 5.2 %all-to-all-start.2 = ((s16[4,8,4224]{2,1,0:T(8,128)(2,1)}), s16[4,8,4224]{2,1,0:T(8,128)(2,1)S(1)}, u32[]{:S(2)}, u32[]{:S(2)}) async-start(s16[4,8,4224]{2,1,0:T(8,128)(2,1)} %collect.1), calls=%async_computation.2 | async-start | bytes 540672 | tf_op jit(solution)/shard_map/all_to_all | solution.py:226
  137.9 2.7 %collective-permute-start.13 = (f32[8,128]{1,0:T(8,128)S(1)}, f32[8,128]{1,0:T(8,128)S(1)}, u32[]{:S(2)}, u32[]{:S(2)}) collective-permute-start(f32[8,128]{1,0:T(8,128)S(1)} %add.56), channel_id=1, source_target_pairs={{0,3},{1,0},{2,1},{3,2},{4,7},{5,4},{6,5},{7,6},{8,11},{9,8},{10,9... | collective-permute-start | bytes 12296 | tf_op jit(solution)/shard_map/ppermute | solution.py:230
  140.6 0.8 collective-permute-start.12
  141.5 0.9 collective-permute-start.11
  142.3 0.0 collective-permute-done.13
  142.3 3.4 %collective-permute-done.12 = f32[8,128]{1,0:T(8,128)S(1)} collective-permute-done((f32[8,128]{1,0:T(8,128)S(1)}, f32[8,128]{1,0:T(8,128)S(1)}, u32[]{:S(2)}, u32[]{:S(2)}) %collective-permute-start.12) | collective-permute-done | bytes 4128 | tf_op jit(solution)/shard_map/ppermute | solution.py:230
  145.7 0.5 collective-permute-done.11
  146.3 1.5 all-to-all-done.2.in_ref
  147.8 0.9 finish.1
  (4 shorter events, 0.0 us)
Async XLA Ops:
  7.2 40.9 %all-gather.3.cloned.1.call-start = ((), (), s32[]{:S(2)}) async-start(), calls=%async_computation.3 | async-start | bytes 1310720 | tf_op jit(solution)/shard_map/all_gather | solution.py:259
  7.9 0.7 copy-start.1
  48.1 1.2 copy-start
  49.3 20.5 %copy-start.2 = (f32[1,1,2,512,512]{4,3,2,1,0:T(8,128)S(1)}, f32[1,1,2,512,512]{4,3,2,1,0:T(8,128)}, u32[]{:S(2)}) copy-start(f32[1,1,2,512,512]{4,3,2,1,0:T(8,128)} %param.6) | copy-start | bytes 6291460
  51.4 18.4 %all-to-all-start = ((bf16[16,32,1024]{2,1,0:T(8,128)(2,1)}), bf16[16,32,1024]{2,1,0:T(8,128)(2,1)S(1)}, u32[]{:S(2)}, u32[]{:S(2)}) async-start(bf16[16,32,1024]{2,1,0:T(8,128)(2,1)} %route.1), calls=%async_computation | async-start | bytes 2097152 | tf_op jit(solution)/shard_map/all_to_all | solution.py:226
  86.7 44.5 %all-to-all-start.1 = ((s16[64,8,1152]{2,1,0:T(8,128)(2,1)}), s16[64,8,1152]{2,1,0:T(8,128)(2,1)S(1)}, u32[]{:S(2)}, u32[]{:S(2)}) async-start(s16[64,8,1152]{2,1,0:T(8,128)(2,1)} %get-tuple-element.10), calls=%async_computation.1 | async-start | bytes 2359296 | tf_op jit(solution)/shard_map/all_to_all | solution.py:226
  95.2 6.4 %collective-permute-start.6 = (f32[8,128]{1,0:T(8,128)S(1)}, f32[8,128]{1,0:T(8,128)S(1)}, u32[]{:S(2)}, u32[]{:S(2)}) collective-permute-start(f32[8,128]{1,0:T(8,128)S(1)} %get-tuple-element.9), channel_id=1, source_target_pairs={{0,28},{4,24},{8,20},{12,16},{16,12},{20,8},{24,4},{28,0},{32,60},... | collective-permute-start | bytes 12296 | tf_op jit(solution)/shard_map/ppermute | solution.py:230
  96.5 5.6 %collective-permute-start.5 = (f32[8,128]{1,0:T(8,128)S(1)}, f32[8,128]{1,0:T(8,128)S(1)}, u32[]{:S(2)}, u32[]{:S(2)}) collective-permute-start(f32[8,128]{1,0:T(8,128)S(1)} %get-tuple-element.9), channel_id=1, source_target_pairs={{0,24},{4,28},{8,16},{12,20},{16,8},{20,12},{24,0},{28,4},{32,56},... | collective-permute-start | bytes 12296 | tf_op jit(solution)/shard_map/ppermute | solution.py:230
  97.0 5.2 %collective-permute-start.4 = (f32[8,128]{1,0:T(8,128)S(1)}, f32[8,128]{1,0:T(8,128)S(1)}, u32[]{:S(2)}, u32[]{:S(2)}) collective-permute-start(f32[8,128]{1,0:T(8,128)S(1)} %get-tuple-element.9), channel_id=1, source_target_pairs={{0,20},{4,16},{8,28},{12,24},{16,4},{20,0},{24,12},{28,8},{32,52},... | collective-permute-start | bytes 12296 | tf_op jit(solution)/shard_map/ppermute | solution.py:230
  100.0 5.2 %collective-permute-start.3 = (f32[8,128]{1,0:T(8,128)S(1)}, f32[8,128]{1,0:T(8,128)S(1)}, u32[]{:S(2)}, u32[]{:S(2)}) collective-permute-start(f32[8,128]{1,0:T(8,128)S(1)} %get-tuple-element.9), channel_id=1, source_target_pairs={{0,16},{4,20},{8,24},{12,28},{16,0},{20,4},{24,8},{28,12},{32,48},... | collective-permute-start | bytes 12296 | tf_op jit(solution)/shard_map/ppermute | solution.py:230
  100.4 4.8 %collective-permute-start.2 = (f32[8,128]{1,0:T(8,128)S(1)}, f32[8,128]{1,0:T(8,128)S(1)}, u32[]{:S(2)}, u32[]{:S(2)}) collective-permute-start(f32[8,128]{1,0:T(8,128)S(1)} %get-tuple-element.9), channel_id=1, source_target_pairs={{0,12},{4,8},{8,4},{12,0},{16,28},{20,24},{24,20},{28,16},{32,44},... | collective-permute-start | bytes 12296 | tf_op jit(solution)/shard_map/ppermute | solution.py:230
  101.6 3.6 %collective-permute-start.1 = (f32[8,128]{1,0:T(8,128)S(1)}, f32[8,128]{1,0:T(8,128)S(1)}, u32[]{:S(2)}, u32[]{:S(2)}) collective-permute-start(f32[8,128]{1,0:T(8,128)S(1)} %get-tuple-element.9), channel_id=1, source_target_pairs={{0,8},{4,12},{8,0},{12,4},{16,24},{20,28},{24,16},{28,20},{32,40},... | collective-permute-start | bytes 12296 | tf_op jit(solution)/shard_map/ppermute | solution.py:230
  102.1 3.1 %collective-permute-start = (f32[8,128]{1,0:T(8,128)S(1)}, f32[8,128]{1,0:T(8,128)S(1)}, u32[]{:S(2)}, u32[]{:S(2)}) collective-permute-start(f32[8,128]{1,0:T(8,128)S(1)} %get-tuple-element.9), channel_id=1, source_target_pairs={{0,4},{4,0},{8,12},{12,8},{16,20},{20,16},{24,28},{28,24},{32,36},... | collective-permute-start | bytes 12296 | tf_op jit(solution)/shard_map/ppermute | solution.py:230
  105.2 18.4 %collective-permute-start.9 = (f32[8,128]{1,0:T(8,128)S(1)}, f32[8,128]{1,0:T(8,128)S(1)}, u32[]{:S(2)}, u32[]{:S(2)}) collective-permute-start(f32[8,128]{1,0:T(8,128)S(1)} %add_add_fusion.2), channel_id=1, source_target_pairs={{0,96},{4,100},{8,104},{12,108},{16,112},{20,116},{24,120},{28,124... | collective-permute-start | bytes 12296 | tf_op jit(solution)/shard_map/ppermute | solution.py:230
  108.9 14.7 %collective-permute-start.8 = (f32[8,128]{1,0:T(8,128)S(1)}, f32[8,128]{1,0:T(8,128)S(1)}, u32[]{:S(2)}, u32[]{:S(2)}) collective-permute-start(f32[8,128]{1,0:T(8,128)S(1)} %add_add_fusion.2), channel_id=1, source_target_pairs={{0,64},{4,68},{8,72},{12,76},{16,80},{20,84},{24,88},{28,92},{32,9... | collective-permute-start | bytes 12296 | tf_op jit(solution)/shard_map/ppermute | solution.py:230
  108.9 14.7 %collective-permute-start.7 = (f32[8,128]{1,0:T(8,128)S(1)}, f32[8,128]{1,0:T(8,128)S(1)}, u32[]{:S(2)}, u32[]{:S(2)}) collective-permute-start(f32[8,128]{1,0:T(8,128)S(1)} %add_add_fusion.2), channel_id=1, source_target_pairs={{0,32},{4,36},{8,40},{12,44},{16,48},{20,52},{24,56},{28,60},{32,0... | collective-permute-start | bytes 12296 | tf_op jit(solution)/shard_map/ppermute | solution.py:230
  123.6 7.6 %collective-permute-start.10 = (f32[8,128]{1,0:T(8,128)S(1)}, f32[8,128]{1,0:T(8,128)S(1)}, u32[]{:S(2)}, u32[]{:S(2)}) collective-permute-start(f32[8,128]{1,0:T(8,128)S(1)} %add_add_fusion.1), channel_id=1, source_target_pairs={{0,128},{64,192},{128,0},{192,64},{1,129},{65,193},{129,1},{193,65... | collective-permute-start | bytes 12296 | tf_op jit(solution)/shard_map/ppermute | solution.py:230
  132.7 15.1 %all-to-all-start.2 = ((s16[4,8,4224]{2,1,0:T(8,128)(2,1)}), s16[4,8,4224]{2,1,0:T(8,128)(2,1)S(1)}, u32[]{:S(2)}, u32[]{:S(2)}) async-start(s16[4,8,4224]{2,1,0:T(8,128)(2,1)} %collect.1), calls=%async_computation.2 | async-start | bytes 540672 | tf_op jit(solution)/shard_map/all_to_all | solution.py:226
  137.9 4.4 %collective-permute-start.13 = (f32[8,128]{1,0:T(8,128)S(1)}, f32[8,128]{1,0:T(8,128)S(1)}, u32[]{:S(2)}, u32[]{:S(2)}) collective-permute-start(f32[8,128]{1,0:T(8,128)S(1)} %add.56), channel_id=1, source_target_pairs={{0,3},{1,0},{2,1},{3,2},{4,7},{5,4},{6,5},{7,6},{8,11},{9,8},{10,9... | collective-permute-start | bytes 12296 | tf_op jit(solution)/shard_map/ppermute | solution.py:230
  140.6 5.1 %collective-permute-start.12 = (f32[8,128]{1,0:T(8,128)S(1)}, f32[8,128]{1,0:T(8,128)S(1)}, u32[]{:S(2)}, u32[]{:S(2)}) collective-permute-start(f32[8,128]{1,0:T(8,128)S(1)} %add.56), channel_id=1, source_target_pairs={{0,2},{1,3},{2,0},{3,1},{4,6},{5,7},{6,4},{7,5},{8,10},{9,11},{10,... | collective-permute-start | bytes 12296 | tf_op jit(solution)/shard_map/ppermute | solution.py:230
  141.5 4.8 %collective-permute-start.11 = (f32[8,128]{1,0:T(8,128)S(1)}, f32[8,128]{1,0:T(8,128)S(1)}, u32[]{:S(2)}, u32[]{:S(2)}) collective-permute-start(f32[8,128]{1,0:T(8,128)S(1)} %add.56), channel_id=1, source_target_pairs={{0,1},{1,2},{2,3},{3,0},{4,5},{5,6},{6,7},{7,4},{8,9},{9,10},{10,1... | collective-permute-start | bytes 12296 | tf_op jit(solution)/shard_map/ppermute | solution.py:230
Sparse Core Ops, SparseCore 0:
  9.8 38.2 all-gather.2

commit v8 on v6

--- a/solution.py
+++ b/solution.py
@@ -19,6 +19,7 @@
 LINES = 8
 CELLS = 2048 * 16384
 MIB = 1024 * 1024
+SUM_ROWS = 8
 
 WHOLE = pl.BlockSpec(memory_space=pltpu.VMEM)
 SMEM = pl.BlockSpec(memory_space=pltpu.SMEM)
@@ -52,30 +53,27 @@
 
 
 def collect_kernel(place_ref, in_ref, out_ref):
-    lane = lax.broadcasted_iota(jnp.int32, (LINES, 128), 1)
     for row in range(GROUPS):
-        powers = jnp.zeros((LINES, 128), jnp.int32)
         for j in range(PER_SHARD):
             place = place_ref[row * PER_SHARD + j]
-            position, slot = place // SLOTS, lax.rem(place, SLOTS)
-            columns = pl.ds(pl.multiple_of(slot * BLOCK, BLOCK), BLOCK)
-            out_ref[row, :, pl.ds(j * BLOCK, BLOCK)] = in_ref[position, :, columns]
-            both = in_ref[position, :, pl.ds(SLOTS * BLOCK, 128)].astype(jnp.int32)
-            powers = jnp.where(lane == j, jnp.where(slot == 0, both[:, 0:1], both[:, 64:65]), powers)
-        out_ref[row, :, pl.ds(PER_SHARD * BLOCK, 128)] = powers.astype(jnp.int16)
-
-
-def finish_kernel(sums_ref, in_ref, out_ref):
-    grad_total = sums_ref[0:1, 0:1]
-    update_total = sums_ref[1:2, 0:1]
+            columns = pl.ds(pl.multiple_of(lax.rem(place, SLOTS) * BLOCK, BLOCK), BLOCK)
+            out_ref[row, :, pl.ds(j * BLOCK, BLOCK)] = in_ref[place // SLOTS, :, columns]
+
+
+def finish_kernel(me_ref, place_ref, gathered_ref, in_ref, out_ref):
+    grad_total = gathered_ref[0:1, 0:1]
+    update_total = gathered_ref[1:2, 0:1]
     graft = jnp.sqrt(grad_total / CELLS) * lax.rsqrt(update_total / CELLS + 1e-06)
-    for chunk in range(GROUPS):
-        powers = in_ref[chunk, :, pl.ds(PER_SHARD * BLOCK, 128)].astype(jnp.int32).astype(jnp.float32)
-        steps = jnp.exp2(powers) * graft
-        for j in range(PER_SHARD):
-            columns = pl.ds(j * BLOCK, BLOCK)
+    member, group = me_ref[0] // GROUPS, lax.rem(me_ref[0], GROUPS)
+    scales = gathered_ref[pl.ds(SUM_ROWS + member * GROUPS, GROUPS), :] * graft
+    lane = lax.broadcasted_iota(jnp.int32, scales.shape, 1)
+    for j in range(PER_SHARD):
+        place = place_ref[group * PER_SHARD + j]
+        steps = jnp.sum(jnp.where(lane == place, scales, 0.0), axis=1, keepdims=True)
+        columns = pl.ds(j * BLOCK, BLOCK)
+        for chunk in range(GROUPS):
             coded = in_ref[chunk, :, columns].astype(jnp.int32).astype(jnp.float32)
-            out_ref[chunk, :, columns] = (coded * steps[:, j : j + 1]).astype(jnp.bfloat16)
+            out_ref[chunk, :, columns] = (coded * steps[chunk : chunk + 1]).astype(jnp.bfloat16)
 
 
 def dot(a, b):
@@ -110,7 +108,7 @@
 
 
 def owner_kernel(me_ref, place_ref, got_ref, left_ref, right_ref, new_left_ref, new_right_ref, coded_ref,
-                 sums_ref, power_ref, prev_ref, new_ref, n_ref, raw_ref, n_parts_ref, q_parts_ref,
+                 sums_ref, scales_ref, prev_ref, new_ref, n_ref, raw_ref, n_parts_ref, q_parts_ref,
                  h_parts_ref, r_parts_ref, got_sem, new_sem):
     slot = pl.program_id(0)
 
@@ -132,7 +130,8 @@
     used = place_ref[0] == wanted
     for b in range(1, BLOCKS):
         used = used | (place_ref[b] == wanted)
-    block = got_ref[...]
+    place = pl.ds(pl.multiple_of(slot * BLOCK, BLOCK), BLOCK)
+    block = got_ref[:, place]
     block = jnp.where(used, block, jnp.zeros_like(block))
     turned = block.T
     steps = [(rows, columns, side) for rows, columns in ((ALL, LOW), (HIGH, HIGH)) for side in range(2)]
@@ -193,26 +192,24 @@
     grad_sq = jnp.sum(wide * wide, keepdims=True)
     line = lax.broadcasted_iota(jnp.int32, sums_ref.shape, 0)
     sums = jnp.where(line == 0, grad_sq, update_sq)
-    raw = raw_ref[...]
-    largest = jnp.max(jnp.abs(raw), axis=1, keepdims=True)
-    power = jnp.ceil(jnp.log2(jnp.maximum(largest, 1e-30)) + 0.001) - 15.0
-    coded = jnp.round(raw * jnp.exp2(-power)).astype(jnp.int32)
-    place = pl.ds(pl.multiple_of(slot * BLOCK, BLOCK), BLOCK)
+    raw = raw_ref[...].reshape(OWNERS, LINES, BLOCK)
+    largest = jnp.max(jnp.max(jnp.abs(raw), axis=2, keepdims=True), axis=1, keepdims=True)
+    largest = jnp.maximum(largest, 1e-30)
+    coded = jnp.round(raw * (32767.0 / largest)).astype(jnp.int32)
+    scales = largest * (1.0 / 32767.0)
+    lane = lax.broadcasted_iota(jnp.int32, (1, 128), 1)
     for p in range(OWNERS):
-        coded_ref[p, :, place] = coded[p * LINES : (p + 1) * LINES].astype(jnp.int16)
+        coded_ref[p, :, place] = coded[p].astype(jnp.int16)
+        here = jnp.where(lane == wanted, scales[p], 0.0)
+        scales_ref[pl.ds(p, 1), :] = jnp.where(slot == 0, here, scales_ref[pl.ds(p, 1), :] + here)
 
     @pl.when(slot == 0)
     def _():
         sums_ref[...] = sums
-        power_ref[...] = jnp.broadcast_to(power, power_ref.shape)
 
     @pl.when(slot == SLOTS - 1)
     def _():
         sums_ref[...] += sums
-        lane = lax.broadcasted_iota(jnp.int32, power_ref.shape, 1)
-        powers = jnp.where(lane < 64, power_ref[...], power).astype(jnp.int32)
-        for p in range(OWNERS):
-            coded_ref[p, :, pl.ds(SLOTS * BLOCK, 128)] = powers[p * LINES : (p + 1) * LINES].astype(jnp.int16)
         for k in range(SLOTS):
             for side in range(2):
                 write(side, k).wait()
@@ -226,13 +223,14 @@
     return sum([lax.ppermute(x, axis, perm) for perm in perms], x)
 
 
-def sum_near(x):
-    x = add_permuted(x, "mp", [[(d, (d + s) % SHARDS) for d in range(SHARDS)] for s in range(1, 4)])
+def gather_sums(sums, scales):
+    sums = add_permuted(sums, "mp", [[(d, (d + s) % SHARDS) for d in range(SHARDS)] for s in range(1, 4)])
+    x = jnp.concatenate([sums, scales])
     x = add_permuted(x, "r", [[(d, d ^ s) for d in range(MEMBERS)] for s in range(1, 8)])
     return add_permuted(x, ("g", "r"), [[(d, d ^ (8 * s)) for d in range(OWNERS)] for s in range(1, 4)])
 
 
-def sum_far(x):
+def gather_far(x):
     return add_permuted(x, "g", [[(d, d ^ 2) for d in range(GROUPS)]])
 
 
@@ -265,25 +263,26 @@
     stat_spec = pl.BlockSpec(memory_space=pl.ANY)
     parts = pltpu.VMEM((2, 2, BLOCK, BLOCK), jnp.bfloat16)
     stat_shape = jax.ShapeDtypeStruct((SLOTS, BLOCK, BLOCK), jnp.float32)
-    coded_shape = (OWNERS, LINES, SLOTS * BLOCK + 128)
-    new_left, new_right, coded, sums = pl.pallas_call(
+    coded_shape = (OWNERS, LINES, SLOTS * BLOCK)
+    new_left, new_right, coded, sums, scales = pl.pallas_call(
         owner_kernel,
         grid=(SLOTS,),
         out_shape=[
             stat_shape,
             stat_shape,
             jax.ShapeDtypeStruct(coded_shape, jnp.int16),
-            jax.ShapeDtypeStruct((8, 128), jnp.float32),
+            jax.ShapeDtypeStruct((SUM_ROWS, 128), jnp.float32),
+            jax.ShapeDtypeStruct((OWNERS, OWNERS * SLOTS), jnp.float32),
         ],
-        in_specs=[SMEM, SMEM, pl.BlockSpec((BLOCK, BLOCK), lambda k: (0, k)), stat_spec, stat_spec],
+        in_specs=[SMEM, SMEM, WHOLE, stat_spec, stat_spec],
         out_specs=[
             stat_spec,
             stat_spec,
-            pl.BlockSpec(coded_shape, lambda k: (0, 0, 0)),
-            pl.BlockSpec((8, 128), lambda k: (0, 0)),
+            WHOLE,
+            WHOLE,
+            WHOLE,
         ],
         scratch_shapes=[
-            pltpu.VMEM((BLOCK, 128), jnp.float32),
             pltpu.VMEM((2, SLOTS, BLOCK, BLOCK), jnp.float32),
             pltpu.VMEM((2, SLOTS, BLOCK, BLOCK), jnp.float32),
             pltpu.VMEM((2, BLOCK, BLOCK), jnp.float32),
@@ -303,25 +302,25 @@
     )(me, places, got, prev_left[0, 0], prev_right[0, 0])
 
     returned = exchange(coded, ("r", "g"))
-    sums = sum_near(sums)
+    gathered = gather_sums(sums, scales)
     back = pl.pallas_call(
         collect_kernel,
-        out_shape=jax.ShapeDtypeStruct((GROUPS, LINES, PER_SHARD * BLOCK + 128), jnp.int16),
+        out_shape=jax.ShapeDtypeStruct(spread_shape, jnp.int16),
         in_specs=[SMEM, WHOLE],
         out_specs=WHOLE,
         compiler_params=params(8),
         name="collect",
     )(places, returned)
-    sums, back = lax.optimization_barrier((sums, back))
+    gathered, back = lax.optimization_barrier((gathered, back))
     back = exchange(back, "g")
     update_out = pl.pallas_call(
         finish_kernel,
         out_shape=jax.ShapeDtypeStruct(spread_shape, jnp.bfloat16),
-        in_specs=[WHOLE, WHOLE],
+        in_specs=[SMEM, SMEM, WHOLE, WHOLE],
         out_specs=WHOLE,
         compiler_params=params(8),
         name="finish",
-    )(sum_far(sums), back).reshape(gradient.shape)
+    )(me, places, gather_far(gathered), back).reshape(gradient.shape)
     return (update_out, new_left[None, None], new_right[None, None])
 
 

time: 131 us -> 131 us (level)
  starting transfers between devices: 49 us -> 50.7 us
    all_to_all x4, waiting for transfers between devices: 37.3 us -> 35.6 us  [exchange(): return lax.all_to_all(x, axes, split_axis=0, concat_axis=0, tiled=True)]
  transfers between devices with their start and end apart: 18 -> 18, of which waited for: 8 -> 10; matrix products, arithmetic and copies ran while one was open for 0% -> 0% of each run, Pallas kernels for 1% -> 1%
where the time goes in v8:
time: 131 us; the launch traced here: 130 us
  waiting for transfers between devices  54.8 us (42%)
  starting transfers between devices  50.7 us (39%)
  Pallas kernels  23.1 us (18%)
    all_to_all x4, waiting for transfers between devices, exchange(): return lax.all_to_all(x, axes, split_axis=0, concat_axis=0, tiled=True)  35.6 us
    all_to_all x4, starting transfers between devices, exchange(): return lax.all_to_all(x, axes, split_axis=0, concat_axis=0, tiled=True)  28.1 us
    ppermute x14, starting transfers between devices, add_permuted(): return sum([lax.ppermute(x, axis, perm) for perm in perms], x)  22.6 us
    ppermute x14, waiting for transfers between devices, add_permuted(): return sum([lax.ppermute(x, axis, perm) for perm in perms], x)  19.2 us
    pallas_call x1, Pallas kernels, shards(): pl.pallas_call(owner_kernel, grid=(SLOTS,), out_shape=[stat_shape, stat_s...  17 us
  transfers between devices with their start and end apart: 18, of which 10 were waited for; matrix products, arithmetic and copies ran while one was open for 0% of the time, Pallas kernels for 1%

profile of v8, /device:TPU:8, one launch (start us, length us, event | category | flops | bytes accessed | tf_op | source)
XLA Modules:
  0.0 130.1 jit_solution(3732001556671412611)
XLA Ops:
  0.6 8.5 %all-to-all-start = ((bf16[4,8,4096]{2,1,0:T(8,128)(2,1)}), bf16[4,8,4096]{2,1,0:T(8,128)(2,1)S(1)}, u32[]{:S(2)}, u32[]{:S(2)}) async-start(bf16[4,8,4096]{2,1,0:T(8,128)(2,1)} %bitcast.11), calls=%async_computation | async-start | bytes 524288 | tf_op jit(solution)/shard_map/all_to_all | solution.py:219
  9.1 0.0 copy-start
  9.1 0.7 copy-done
  9.8 0.0 copy-start.1
  9.8 1.5 %places.1.place_ref = s32[32]{0:T(128)S(1)} custom-call(s32[1]{0:T(128)} %bitcast.1.shard_ref, s32[4,32]{1,0:T(4,128)S(1)} %copy-done), custom_call_target="tpu_custom_call" | custom-call | flops 1000 | bytes 1000 | tf_op jit(solution)/shard_map/places/pallas_call | solution.py:242
  11.3 8.6 %all-to-all-done.in_ref = bf16[4,8,4096]{2,1,0:T(8,128)(2,1)S(1)} async-done(((bf16[4,8,4096]{2,1,0:T(8,128)(2,1)}), bf16[4,8,4096]{2,1,0:T(8,128)(2,1)S(1)}, u32[]{:S(2)}, u32[]{:S(2)}) %all-to-all-start) | async-done | bytes 262176 | tf_op jit(solution)/shard_map/all_to_all | solution.py:219
  19.8 1.7 %route.1 = bf16[64,8,1024]{2,1,0:T(8,128)(2,1)} custom-call(s32[32]{0:T(128)S(1)} %places.1.place_ref, bf16[4,8,4096]{2,1,0:T(8,128)(2,1)S(1)} %all-to-all-done.in_ref), custom_call_target="tpu_custom_call" | custom-call | tf_op jit(solution)/shard_map/route/pallas_call | solution.py:253
  21.5 6.6 %all-to-all-start.1 = ((bf16[64,8,1024]{2,1,0:T(8,128)(2,1)}), bf16[64,8,1024]{2,1,0:T(8,128)(2,1)S(1)}, u32[]{:S(2)}, u32[]{:S(2)}) async-start(bf16[64,8,1024]{2,1,0:T(8,128)(2,1)} %route.1), calls=%async_computation.1 | async-start | bytes 2097152 | tf_op jit(solution)/shard_map/all_to_all | solution.py:219
  28.2 27.1 %all-to-all-done.1 = bf16[64,8,1024]{2,1,0:T(8,128)(2,1)S(1)} async-done(((bf16[64,8,1024]{2,1,0:T(8,128)(2,1)}), bf16[64,8,1024]{2,1,0:T(8,128)(2,1)S(1)}, u32[]{:S(2)}, u32[]{:S(2)}) %all-to-all-start.1) | async-done | bytes 1048608 | tf_op jit(solution)/shard_map/all_to_all | solution.py:219
  55.2 0.0 copy-done.1
  55.2 17.0 %owner.1 = (f32[2,512,512]{2,1,0:T(8,128)}, f32[2,512,512]{2,1,0:T(8,128)}, s16[64,8,1024]{2,1,0:T(8,128)(2,1)}, f32[8,128]{1,0:T(8,128)S(1)}, f32[64,128]{1,0:T(8,128)S(1)}) custom-call(s32[1]{0:T(128)} %bitcast.me_ref, s32[32]{0:T(128)S(1)} %places.1.place_ref, bf16[512,1024]{1,0:T(8,128)(2,1)S(1)} %bitcast.9, f32[2,512,512]{2,1,0:T(8,128)S(1)} %bitcast.10, ...), custom_call_target="tpu_custom_call" | custom-call | flops 13421772800 | bytes 12582912 | tf_op jit(solution)/shard_map/owner/pallas_call | solution.py:267
  72.3 7.7 %all-to-all-start.2 = ((s16[64,8,1024]{2,1,0:T(8,128)(2,1)}), s16[64,8,1024]{2,1,0:T(8,128)(2,1)S(1)}, u32[]{:S(2)}, u32[]{:S(2)}) async-start(s16[64,8,1024]{2,1,0:T(8,128)(2,1)} %get-tuple-element.12), calls=%async_computation.2 | async-start | bytes 2097152 | tf_op jit(solution)/shard_map/all_to_all | solution.py:219
  80.0 2.8 %collective-permute-start.2 = (f32[8,128]{1,0:T(8,128)S(1)}, f32[8,128]{1,0:T(8,128)S(1)}, u32[]{:S(2)}, u32[]{:S(2)}) collective-permute-start(f32[8,128]{1,0:T(8,128)S(1)} %get-tuple-element.10), channel_id=1, source_target_pairs={{0,3},{1,0},{2,1},{3,2},{4,7},{5,4},{6,5},{7,6},{8,11},{9,8},{10,9... | collective-permute-start | bytes 12296 | tf_op jit(solution)/shard_map/ppermute | solution.py:223
  82.8 0.8 collective-permute-start.1
  83.6 0.9 collective-permute-start
  84.5 0.0 collective-permute-done.2
  84.5 3.4 %collective-permute-done.1 = f32[8,128]{1,0:T(8,128)S(1)} collective-permute-done((f32[8,128]{1,0:T(8,128)S(1)}, f32[8,128]{1,0:T(8,128)S(1)}, u32[]{:S(2)}, u32[]{:S(2)}) %collective-permute-start.1) | collective-permute-done | bytes 4128 | tf_op jit(solution)/shard_map/ppermute | solution.py:223
  87.9 0.5 collective-permute-done
  88.5 1.7 %collective-permute-start.8 = (f32[72,128]{1,0:T(8,128)S(1)}, f32[72,128]{1,0:T(8,128)S(1)}, u32[]{:S(2)}, u32[]{:S(2)}) collective-permute-start(f32[72,128]{1,0:T(8,128)S(1)} %pad_maximum_fusion), channel_id=1, source_target_pairs={{0,24},{4,28},{8,16},{12,20},{16,8},{20,12},{24,0},{28,4},{32,56},... | collective-permute-start | bytes 110600 | tf_op jit(solution)/shard_map/ppermute | solution.py:223
  90.2 0.0 collective-permute-start.7
  90.2 1.6 %collective-permute-start.6 = (f32[72,128]{1,0:T(8,128)S(1)}, f32[72,128]{1,0:T(8,128)S(1)}, u32[]{:S(2)}, u32[]{:S(2)}) collective-permute-start(f32[72,128]{1,0:T(8,128)S(1)} %pad_maximum_fusion), channel_id=1, source_target_pairs={{0,16},{4,20},{8,24},{12,28},{16,0},{20,4},{24,8},{28,12},{32,48},... | collective-permute-start | bytes 110600 | tf_op jit(solution)/shard_map/ppermute | solution.py:223
  91.8 3.2 %collective-permute-start.5 = (f32[72,128]{1,0:T(8,128)S(1)}, f32[72,128]{1,0:T(8,128)S(1)}, u32[]{:S(2)}, u32[]{:S(2)}) collective-permute-start(f32[72,128]{1,0:T(8,128)S(1)} %pad_maximum_fusion), channel_id=1, source_target_pairs={{0,12},{4,8},{8,4},{12,0},{16,28},{20,24},{24,20},{28,16},{32,44},... | collective-permute-start | bytes 110600 | tf_op jit(solution)/shard_map/ppermute | solution.py:223
  95.0 0.2 collective-permute-start.4
  95.2 0.0 collective-permute-done.8
  95.2 0.0 collective-permute-start.9
  95.2 0.0 collective-permute-done.7
  95.2 0.7 collective-permute-start.3
  95.9 0.4 collective-permute-done.6
  96.2 2.3 %collective-permute-done.5 = f32[72,128]{1,0:T(8,128)S(1)} collective-permute-done((f32[72,128]{1,0:T(8,128)S(1)}, f32[72,128]{1,0:T(8,128)S(1)}, u32[]{:S(2)}, u32[]{:S(2)}) %collective-permute-start.5) | collective-permute-done | bytes 36896 | tf_op jit(solution)/shard_map/ppermute | solution.py:223
  98.5 1.1 collective-permute-done.4
  99.7 0.0 collective-permute-done.9
  99.7 0.0 collective-permute-done.3
  99.7 4.1 %collective-permute-start.12 = (f32[72,128]{1,0:T(8,128)S(1)}, f32[72,128]{1,0:T(8,128)S(1)}, u32[]{:S(2)}, u32[]{:S(2)}) collective-permute-start(f32[72,128]{1,0:T(8,128)S(1)} %add_add_fusion.1), channel_id=1, source_target_pairs={{0,96},{4,100},{8,104},{12,108},{16,112},{20,116},{24,120},{28,124... | collective-permute-start | bytes 110600 | tf_op jit(solution)/shard_map/ppermute | solution.py:223
  103.8 0.0 collective-permute-start.11
  103.8 0.7 collective-permute-start.10
  104.5 2.4 %collective-permute-done.12 = f32[72,128]{1,0:T(8,128)S(1)} collective-permute-done((f32[72,128]{1,0:T(8,128)S(1)}, f32[72,128]{1,0:T(8,128)S(1)}, u32[]{:S(2)}, u32[]{:S(2)}) %collective-permute-start.12) | collective-permute-done | bytes 36896 | tf_op jit(solution)/shard_map/ppermute | solution.py:223
  106.8 2.0 %collective-permute-done.11 = f32[72,128]{1,0:T(8,128)S(1)} collective-permute-done((f32[72,128]{1,0:T(8,128)S(1)}, f32[72,128]{1,0:T(8,128)S(1)}, u32[]{:S(2)}, u32[]{:S(2)}) %collective-permute-start.11) | collective-permute-done | bytes 36896 | tf_op jit(solution)/shard_map/ppermute | solution.py:223
  108.8 0.0 collective-permute-done.10
  108.8 0.0 all-to-all-done.2.in_ref
  108.8 1.4 %collect.1 = s16[4,8,4096]{2,1,0:T(8,128)(2,1)} custom-call(s32[32]{0:T(128)S(1)} %places.1.place_ref, s16[64,8,1024]{2,1,0:T(8,128)(2,1)S(1)} %all-to-all-done.2.in_ref), custom_call_target="tpu_custom_call" | custom-call | tf_op jit(solution)/shard_map/collect/pallas_call | solution.py:306
  110.3 5.3 %all-to-all-start.3 = ((s16[4,8,4096]{2,1,0:T(8,128)(2,1)}), s16[4,8,4096]{2,1,0:T(8,128)(2,1)S(1)}, u32[]{:S(2)}, u32[]{:S(2)}) async-start(s16[4,8,4096]{2,1,0:T(8,128)(2,1)} %collect.1), calls=%async_computation.3 | async-start | bytes 524288 | tf_op jit(solution)/shard_map/all_to_all | solution.py:219
  115.6 5.9 %collective-permute-start.13 = (f32[72,128]{1,0:T(8,128)S(1)}, f32[72,128]{1,0:T(8,128)S(1)}, u32[]{:S(2)}, u32[]{:S(2)}) collective-permute-start(f32[72,128]{1,0:T(8,128)S(1)} %add_add_fusion), channel_id=1, source_target_pairs={{0,128},{64,192},{128,0},{192,64},{1,129},{65,193},{129,1},{193,65... | collective-permute-start | bytes 110600 | tf_op jit(solution)/shard_map/ppermute | solution.py:223
  121.6 7.1 %collective-permute-done.13 = f32[72,128]{1,0:T(8,128)S(1)} collective-permute-done((f32[72,128]{1,0:T(8,128)S(1)}, f32[72,128]{1,0:T(8,128)S(1)}, u32[]{:S(2)}, u32[]{:S(2)}) %collective-permute-start.13) | collective-permute-done | bytes 36896 | tf_op jit(solution)/shard_map/ppermute | solution.py:223
  128.7 0.0 all-to-all-done.3.in_ref
  128.7 1.4 %finish.1 = bf16[4,8,4096]{2,1,0:T(8,128)(2,1)} custom-call(s32[1]{0:T(128)} %bitcast.me_ref, s32[32]{0:T(128)S(1)} %places.1.place_ref, f32[72,128]{1,0:T(8,128)S(1)} %add.59.gathered_ref, s16[4,8,4096]{2,1,0:T(8,128)(2,1)S(1)} %all-to-all-done.3.in_ref), custom_call_target="tpu_custom_call" | custom-call | tf_op jit(solution)/shard_map/finish/pallas_call | solution.py:316
  (5 shorter events, 0.1 us)
Async XLA Ops:
  0.6 19.2 %all-to-all-start = ((bf16[4,8,4096]{2,1,0:T(8,128)(2,1)}), bf16[4,8,4096]{2,1,0:T(8,128)(2,1)S(1)}, u32[]{:S(2)}, u32[]{:S(2)}) async-start(bf16[4,8,4096]{2,1,0:T(8,128)(2,1)} %bitcast.11), calls=%async_computation | async-start | bytes 524288 | tf_op jit(solution)/shard_map/all_to_all | solution.py:219
  9.1 0.7 copy-start
  9.8 45.5 %copy-start.1 = (f32[1,1,2,512,512]{4,3,2,1,0:T(8,128)S(1)}, f32[1,1,2,512,512]{4,3,2,1,0:T(8,128)}, u32[]{:S(2)}) copy-start(f32[1,1,2,512,512]{4,3,2,1,0:T(8,128)} %param.6) | copy-start | bytes 6291460
  21.5 33.7 %all-to-all-start.1 = ((bf16[64,8,1024]{2,1,0:T(8,128)(2,1)}), bf16[64,8,1024]{2,1,0:T(8,128)(2,1)S(1)}, u32[]{:S(2)}, u32[]{:S(2)}) async-start(bf16[64,8,1024]{2,1,0:T(8,128)(2,1)} %route.1), calls=%async_computation.1 | async-start | bytes 2097152 | tf_op jit(solution)/shard_map/all_to_all | solution.py:219
  72.3 36.6 %all-to-all-start.2 = ((s16[64,8,1024]{2,1,0:T(8,128)(2,1)}), s16[64,8,1024]{2,1,0:T(8,128)(2,1)S(1)}, u32[]{:S(2)}, u32[]{:S(2)}) async-start(s16[64,8,1024]{2,1,0:T(8,128)(2,1)} %get-tuple-element.12), calls=%async_computation.2 | async-start | bytes 2097152 | tf_op jit(solution)/shard_map/all_to_all | solution.py:219
  80.0 4.5 %collective-permute-start.2 = (f32[8,128]{1,0:T(8,128)S(1)}, f32[8,128]{1,0:T(8,128)S(1)}, u32[]{:S(2)}, u32[]{:S(2)}) collective-permute-start(f32[8,128]{1,0:T(8,128)S(1)} %get-tuple-element.10), channel_id=1, source_target_pairs={{0,3},{1,0},{2,1},{3,2},{4,7},{5,4},{6,5},{7,6},{8,11},{9,8},{10,9... | collective-permute-start | bytes 12296 | tf_op jit(solution)/shard_map/ppermute | solution.py:223
  82.8 5.1 %collective-permute-start.1 = (f32[8,128]{1,0:T(8,128)S(1)}, f32[8,128]{1,0:T(8,128)S(1)}, u32[]{:S(2)}, u32[]{:S(2)}) collective-permute-start(f32[8,128]{1,0:T(8,128)S(1)} %get-tuple-element.10), channel_id=1, source_target_pairs={{0,2},{1,3},{2,0},{3,1},{4,6},{5,7},{6,4},{7,5},{8,10},{9,11},{10,... | collective-permute-start | bytes 12296 | tf_op jit(solution)/shard_map/ppermute | solution.py:223
  83.6 4.8 %collective-permute-start = (f32[8,128]{1,0:T(8,128)S(1)}, f32[8,128]{1,0:T(8,128)S(1)}, u32[]{:S(2)}, u32[]{:S(2)}) collective-permute-start(f32[8,128]{1,0:T(8,128)S(1)} %get-tuple-element.10), channel_id=1, source_target_pairs={{0,1},{1,2},{2,3},{3,0},{4,5},{5,6},{6,7},{7,4},{8,9},{9,10},{10,1... | collective-permute-start | bytes 12296 | tf_op jit(solution)/shard_map/ppermute | solution.py:223
  88.5 6.7 %collective-permute-start.8 = (f32[72,128]{1,0:T(8,128)S(1)}, f32[72,128]{1,0:T(8,128)S(1)}, u32[]{:S(2)}, u32[]{:S(2)}) collective-permute-start(f32[72,128]{1,0:T(8,128)S(1)} %pad_maximum_fusion), channel_id=1, source_target_pairs={{0,24},{4,28},{8,16},{12,20},{16,8},{20,12},{24,0},{28,4},{32,56},... | collective-permute-start | bytes 110600 | tf_op jit(solution)/shard_map/ppermute | solution.py:223
  90.2 5.0 %collective-permute-start.7 = (f32[72,128]{1,0:T(8,128)S(1)}, f32[72,128]{1,0:T(8,128)S(1)}, u32[]{:S(2)}, u32[]{:S(2)}) collective-permute-start(f32[72,128]{1,0:T(8,128)S(1)} %pad_maximum_fusion), channel_id=1, source_target_pairs={{0,20},{4,16},{8,28},{12,24},{16,4},{20,0},{24,12},{28,8},{32,52},... | collective-permute-start | bytes 110600 | tf_op jit(solution)/shard_map/ppermute | solution.py:223
  90.2 6.0 %collective-permute-start.6 = (f32[72,128]{1,0:T(8,128)S(1)}, f32[72,128]{1,0:T(8,128)S(1)}, u32[]{:S(2)}, u32[]{:S(2)}) collective-permute-start(f32[72,128]{1,0:T(8,128)S(1)} %pad_maximum_fusion), channel_id=1, source_target_pairs={{0,16},{4,20},{8,24},{12,28},{16,0},{20,4},{24,8},{28,12},{32,48},... | collective-permute-start | bytes 110600 | tf_op jit(solution)/shard_map/ppermute | solution.py:223
  91.8 6.8 %collective-permute-start.5 = (f32[72,128]{1,0:T(8,128)S(1)}, f32[72,128]{1,0:T(8,128)S(1)}, u32[]{:S(2)}, u32[]{:S(2)}) collective-permute-start(f32[72,128]{1,0:T(8,128)S(1)} %pad_maximum_fusion), channel_id=1, source_target_pairs={{0,12},{4,8},{8,4},{12,0},{16,28},{20,24},{24,20},{28,16},{32,44},... | collective-permute-start | bytes 110600 | tf_op jit(solution)/shard_map/ppermute | solution.py:223
  95.0 4.7 %collective-permute-start.4 = (f32[72,128]{1,0:T(8,128)S(1)}, f32[72,128]{1,0:T(8,128)S(1)}, u32[]{:S(2)}, u32[]{:S(2)}) collective-permute-start(f32[72,128]{1,0:T(8,128)S(1)} %pad_maximum_fusion), channel_id=1, source_target_pairs={{0,8},{4,12},{8,0},{12,4},{16,24},{20,28},{24,16},{28,20},{32,40},... | collective-permute-start | bytes 110600 | tf_op jit(solution)/shard_map/ppermute | solution.py:223
  95.2 4.5 %collective-permute-start.9 = (f32[72,128]{1,0:T(8,128)S(1)}, f32[72,128]{1,0:T(8,128)S(1)}, u32[]{:S(2)}, u32[]{:S(2)}) collective-permute-start(f32[72,128]{1,0:T(8,128)S(1)} %pad_maximum_fusion), channel_id=1, source_target_pairs={{0,28},{4,24},{8,20},{12,16},{16,12},{20,8},{24,4},{28,0},{32,60},... | collective-permute-start | bytes 110600 | tf_op jit(solution)/shard_map/ppermute | solution.py:223
  95.2 4.5 %collective-permute-start.3 = (f32[72,128]{1,0:T(8,128)S(1)}, f32[72,128]{1,0:T(8,128)S(1)}, u32[]{:S(2)}, u32[]{:S(2)}) collective-permute-start(f32[72,128]{1,0:T(8,128)S(1)} %pad_maximum_fusion), channel_id=1, source_target_pairs={{0,4},{4,0},{8,12},{12,8},{16,20},{20,16},{24,28},{28,24},{32,36},... | collective-permute-start | bytes 110600 | tf_op jit(solution)/shard_map/ppermute | solution.py:223
  99.7 7.2 %collective-permute-start.12 = (f32[72,128]{1,0:T(8,128)S(1)}, f32[72,128]{1,0:T(8,128)S(1)}, u32[]{:S(2)}, u32[]{:S(2)}) collective-permute-start(f32[72,128]{1,0:T(8,128)S(1)} %add_add_fusion.1), channel_id=1, source_target_pairs={{0,96},{4,100},{8,104},{12,108},{16,112},{20,116},{24,120},{28,124... | collective-permute-start | bytes 110600 | tf_op jit(solution)/shard_map/ppermute | solution.py:223
  103.8 5.0 %collective-permute-start.11 = (f32[72,128]{1,0:T(8,128)S(1)}, f32[72,128]{1,0:T(8,128)S(1)}, u32[]{:S(2)}, u32[]{:S(2)}) collective-permute-start(f32[72,128]{1,0:T(8,128)S(1)} %add_add_fusion.1), channel_id=1, source_target_pairs={{0,64},{4,68},{8,72},{12,76},{16,80},{20,84},{24,88},{28,92},{32,9... | collective-permute-start | bytes 110600 | tf_op jit(solution)/shard_map/ppermute | solution.py:223
  103.8 5.0 %collective-permute-start.10 = (f32[72,128]{1,0:T(8,128)S(1)}, f32[72,128]{1,0:T(8,128)S(1)}, u32[]{:S(2)}, u32[]{:S(2)}) collective-permute-start(f32[72,128]{1,0:T(8,128)S(1)} %add_add_fusion.1), channel_id=1, source_target_pairs={{0,32},{4,36},{8,40},{12,44},{16,48},{20,52},{24,56},{28,60},{32,0... | collective-permute-start | bytes 110600 | tf_op jit(solution)/shard_map/ppermute | solution.py:223
  110.3 18.4 %all-to-all-start.3 = ((s16[4,8,4096]{2,1,0:T(8,128)(2,1)}), s16[4,8,4096]{2,1,0:T(8,128)(2,1)S(1)}, u32[]{:S(2)}, u32[]{:S(2)}) async-start(s16[4,8,4096]{2,1,0:T(8,128)(2,1)} %collect.1), calls=%async_computation.3 | async-start | bytes 524288 | tf_op jit(solution)/shard_map/all_to_all | solution.py:219
  115.6 13.0 %collective-permute-start.13 = (f32[72,128]{1,0:T(8,128)S(1)}, f32[72,128]{1,0:T(8,128)S(1)}, u32[]{:S(2)}, u32[]{:S(2)}) collective-permute-start(f32[72,128]{1,0:T(8,128)S(1)} %add_add_fusion), channel_id=1, source_target_pairs={{0,128},{64,192},{128,0},{192,64},{1,129},{65,193},{129,1},{193,65... | collective-permute-start | bytes 110600 | tf_op jit(solution)/shard_map/ppermute | solution.py:223

commit v9 on v6

--- a/solution.py
+++ b/solution.py
@@ -19,6 +19,7 @@
 LINES = 8
 CELLS = 2048 * 16384
 MIB = 1024 * 1024
+GRAD_LANE, UPDATE_LANE = 32, 36
 
 WHOLE = pl.BlockSpec(memory_space=pltpu.VMEM)
 SMEM = pl.BlockSpec(memory_space=pltpu.SMEM)
@@ -51,8 +52,10 @@
             out_ref[place // SLOTS, :, columns] = in_ref[row, :, pl.ds(j * BLOCK, BLOCK)]
 
 
-def collect_kernel(place_ref, in_ref, out_ref):
+def collect_kernel(place_ref, in_ref, out_ref, sums_ref):
     lane = lax.broadcasted_iota(jnp.int32, (LINES, 128), 1)
+    line = lax.broadcasted_iota(jnp.int32, (LINES, 128), 0)
+    tile = pl.ds(SLOTS * BLOCK, 128)
     for row in range(GROUPS):
         powers = jnp.zeros((LINES, 128), jnp.int32)
         for j in range(PER_SHARD):
@@ -60,18 +63,28 @@
             position, slot = place // SLOTS, lax.rem(place, SLOTS)
             columns = pl.ds(pl.multiple_of(slot * BLOCK, BLOCK), BLOCK)
             out_ref[row, :, pl.ds(j * BLOCK, BLOCK)] = in_ref[position, :, columns]
-            both = in_ref[position, :, pl.ds(SLOTS * BLOCK, 128)].astype(jnp.int32)
-            powers = jnp.where(lane == j, jnp.where(slot == 0, both[:, 0:1], both[:, 64:65]), powers)
+            powers = jnp.where(lane == j + 64 * slot, in_ref[position, :, tile].astype(jnp.int32), powers)
         out_ref[row, :, pl.ds(PER_SHARD * BLOCK, 128)] = powers.astype(jnp.int16)
+    sums = jnp.zeros((LINES, 128), jnp.float32)
+    for first in range(0, OWNERS, LINES):
+        digits = jnp.zeros((LINES, 128), jnp.int32)
+        for k in range(LINES):
+            digits = jnp.where(line == k, in_ref[first + k, :, tile].astype(jnp.int32), digits)
+        digits = digits.astype(jnp.float32)
+        value = pltpu.roll(digits, 127, 1) + pltpu.roll(digits, 126, 1) * (1.0 / 4096.0)
+        here = (lane == GRAD_LANE) | (lane == UPDATE_LANE)
+        sums += jnp.where(here, value * jnp.exp2(jnp.where(here, digits, 0.0)), 0.0)
+    sums_ref[...] = sums
 
 
 def finish_kernel(sums_ref, in_ref, out_ref):
-    grad_total = sums_ref[0:1, 0:1]
-    update_total = sums_ref[1:2, 0:1]
+    totals = jnp.sum(sums_ref[...], axis=0, keepdims=True)
+    grad_total = totals[:, GRAD_LANE : GRAD_LANE + 1]
+    update_total = totals[:, UPDATE_LANE : UPDATE_LANE + 1]
     graft = jnp.sqrt(grad_total / CELLS) * lax.rsqrt(update_total / CELLS + 1e-06)
     for chunk in range(GROUPS):
         powers = in_ref[chunk, :, pl.ds(PER_SHARD * BLOCK, 128)].astype(jnp.int32).astype(jnp.float32)
-        steps = jnp.exp2(powers) * graft
+        steps = jnp.exp2(powers + pltpu.roll(powers, 64, 1)) * graft
         for j in range(PER_SHARD):
             columns = pl.ds(j * BLOCK, BLOCK)
             coded = in_ref[chunk, :, columns].astype(jnp.int32).astype(jnp.float32)
@@ -110,7 +123,7 @@
 
 
 def owner_kernel(me_ref, place_ref, got_ref, left_ref, right_ref, new_left_ref, new_right_ref, coded_ref,
-                 sums_ref, power_ref, prev_ref, new_ref, n_ref, raw_ref, n_parts_ref, q_parts_ref,
+                 power_ref, sums_ref, prev_ref, new_ref, n_ref, raw_ref, n_parts_ref, q_parts_ref,
                  h_parts_ref, r_parts_ref, got_sem, new_sem):
     slot = pl.program_id(0)
 
@@ -132,7 +145,8 @@
     used = place_ref[0] == wanted
     for b in range(1, BLOCKS):
         used = used | (place_ref[b] == wanted)
-    block = got_ref[...]
+    place = pl.ds(pl.multiple_of(slot * BLOCK, BLOCK), BLOCK)
+    block = got_ref[:, place]
     block = jnp.where(used, block, jnp.zeros_like(block))
     turned = block.T
     steps = [(rows, columns, side) for rows, columns in ((ALL, LOW), (HIGH, HIGH)) for side in range(2)]
@@ -191,13 +205,12 @@
         update_sq += jnp.sum(raw * raw, keepdims=True)
     wide = block.astype(jnp.float32)
     grad_sq = jnp.sum(wide * wide, keepdims=True)
-    line = lax.broadcasted_iota(jnp.int32, sums_ref.shape, 0)
-    sums = jnp.where(line == 0, grad_sq, update_sq)
+    lane = lax.broadcasted_iota(jnp.int32, (1, 128), 1)
+    sums = jnp.where(lane < UPDATE_LANE, grad_sq, update_sq)
     raw = raw_ref[...]
     largest = jnp.max(jnp.abs(raw), axis=1, keepdims=True)
     power = jnp.ceil(jnp.log2(jnp.maximum(largest, 1e-30)) + 0.001) - 15.0
     coded = jnp.round(raw * jnp.exp2(-power)).astype(jnp.int32)
-    place = pl.ds(pl.multiple_of(slot * BLOCK, BLOCK), BLOCK)
     for p in range(OWNERS):
         coded_ref[p, :, place] = coded[p * LINES : (p + 1) * LINES].astype(jnp.int16)
 
@@ -208,9 +221,15 @@
 
     @pl.when(slot == SLOTS - 1)
     def _():
-        sums_ref[...] += sums
-        lane = lax.broadcasted_iota(jnp.int32, power_ref.shape, 1)
-        powers = jnp.where(lane < 64, power_ref[...], power).astype(jnp.int32)
+        total = sums_ref[...] + sums
+        exponent = jnp.ceil(jnp.log2(jnp.maximum(total, 1e-30)))
+        mantissa = total * jnp.exp2(12.0 - exponent)
+        upper = jnp.floor(mantissa)
+        lower = jnp.round((mantissa - upper) * 4096.0)
+        start = jnp.where(lane < UPDATE_LANE, GRAD_LANE, UPDATE_LANE)
+        digits = jnp.where(lane == start, exponent - 12.0, jnp.where(lane == start + 1, upper, lower))
+        held = (lane >= GRAD_LANE) & (lane < UPDATE_LANE + 3)
+        powers = jnp.where(held, digits, jnp.where(lane < 64, power_ref[...], power)).astype(jnp.int32)
         for p in range(OWNERS):
             coded_ref[p, :, pl.ds(SLOTS * BLOCK, 128)] = powers[p * LINES : (p + 1) * LINES].astype(jnp.int16)
         for k in range(SLOTS):
@@ -226,14 +245,8 @@
     return sum([lax.ppermute(x, axis, perm) for perm in perms], x)
 
 
-def sum_near(x):
-    x = add_permuted(x, "mp", [[(d, (d + s) % SHARDS) for d in range(SHARDS)] for s in range(1, 4)])
-    x = add_permuted(x, "r", [[(d, d ^ s) for d in range(MEMBERS)] for s in range(1, 8)])
-    return add_permuted(x, ("g", "r"), [[(d, d ^ (8 * s)) for d in range(OWNERS)] for s in range(1, 4)])
-
-
-def sum_far(x):
-    return add_permuted(x, "g", [[(d, d ^ 2) for d in range(GROUPS)]])
+def sum_mp(x):
+    return add_permuted(x, "mp", [[(d, (d + s) % SHARDS) for d in range(SHARDS)] for s in range(1, 4)])
 
 
 def shards(gradient, block_owner, prev_left, prev_right):
@@ -266,24 +279,23 @@
     parts = pltpu.VMEM((2, 2, BLOCK, BLOCK), jnp.bfloat16)
     stat_shape = jax.ShapeDtypeStruct((SLOTS, BLOCK, BLOCK), jnp.float32)
     coded_shape = (OWNERS, LINES, SLOTS * BLOCK + 128)
-    new_left, new_right, coded, sums = pl.pallas_call(
+    new_left, new_right, coded = pl.pallas_call(
         owner_kernel,
         grid=(SLOTS,),
         out_shape=[
             stat_shape,
             stat_shape,
             jax.ShapeDtypeStruct(coded_shape, jnp.int16),
-            jax.ShapeDtypeStruct((8, 128), jnp.float32),
         ],
-        in_specs=[SMEM, SMEM, pl.BlockSpec((BLOCK, BLOCK), lambda k: (0, k)), stat_spec, stat_spec],
+        in_specs=[SMEM, SMEM, WHOLE, stat_spec, stat_spec],
         out_specs=[
             stat_spec,
             stat_spec,
-            pl.BlockSpec(coded_shape, lambda k: (0, 0, 0)),
-            pl.BlockSpec((8, 128), lambda k: (0, 0)),
+            WHOLE,
         ],
         scratch_shapes=[
             pltpu.VMEM((BLOCK, 128), jnp.float32),
+            pltpu.VMEM((1, 128), jnp.float32),
             pltpu.VMEM((2, SLOTS, BLOCK, BLOCK), jnp.float32),
             pltpu.VMEM((2, SLOTS, BLOCK, BLOCK), jnp.float32),
             pltpu.VMEM((2, BLOCK, BLOCK), jnp.float32),
@@ -303,16 +315,17 @@
     )(me, places, got, prev_left[0, 0], prev_right[0, 0])
 
     returned = exchange(coded, ("r", "g"))
-    sums = sum_near(sums)
-    back = pl.pallas_call(
+    back, sums = pl.pallas_call(
         collect_kernel,
-        out_shape=jax.ShapeDtypeStruct((GROUPS, LINES, PER_SHARD * BLOCK + 128), jnp.int16),
+        out_shape=[
+            jax.ShapeDtypeStruct((GROUPS, LINES, PER_SHARD * BLOCK + 128), jnp.int16),
+            jax.ShapeDtypeStruct((LINES, 128), jnp.float32),
+        ],
         in_specs=[SMEM, WHOLE],
-        out_specs=WHOLE,
+        out_specs=[WHOLE, WHOLE],
         compiler_params=params(8),
         name="collect",
     )(places, returned)
-    sums, back = lax.optimization_barrier((sums, back))
     back = exchange(back, "g")
     update_out = pl.pallas_call(
         finish_kernel,
@@ -321,7 +334,7 @@
         out_specs=WHOLE,
         compiler_params=params(8),
         name="finish",
-    )(sum_far(sums), back).reshape(gradient.shape)
+    )(sum_mp(sums), back).reshape(gradient.shape)
     return (update_out, new_left[None, None], new_right[None, None])
 
 

time: 131 us -> 129 us (0.985)
  blocking collectives: 0 us -> 37.4 us
  starting transfers between devices: 49 us -> 24.4 us
  waiting for transfers between devices: 56 us -> 42 us
    all_to_all x0 -> x1, blocking collectives: none -> 37.4 us  [exchange(): return lax.all_to_all(x, axes, split_axis=0, concat_axis=0, tiled=True)]
    ppermute x14 -> x3, starting transfers between devices: 21.8 us -> 4.45 us  [add_permuted(): return sum([lax.ppermute(x, axis, perm) for perm in perms], x)]
    ppermute x14 -> x3, waiting for transfers between devices: 18.7 us -> 3.93 us  [add_permuted(): return sum([lax.ppermute(x, axis, perm) for perm in perms], x)]
    all_to_all x4 -> x3, starting transfers between devices: 27.2 us -> 19.9 us  [exchange(): return lax.all_to_all(x, axes, split_axis=0, concat_axis=0, tiled=True)]
    all_to_all x4 -> x3, waiting for transfers between devices: 37.3 us -> 38 us  [exchange(): return lax.all_to_all(x, axes, split_axis=0, concat_axis=0, tiled=True)]
  transfers between devices with their start and end apart: 18 -> 6, of which waited for: 8 -> 5; matrix products, arithmetic and copies ran while one was open for 0% -> 0% of each run, Pallas kernels for 1% -> 1%
where the time goes in v9:
time: 129 us; the launch traced here: 127 us
  waiting for transfers between devices  42 us (33%)
  blocking collectives  37.4 us (29%)
  starting transfers between devices  24.4 us (19%)
  Pallas kernels  21.5 us (17%)
    all_to_all x3, waiting for transfers between devices, exchange(): return lax.all_to_all(x, axes, split_axis=0, concat_axis=0, tiled=True)  38 us
    all_to_all x1, blocking collectives, exchange(): return lax.all_to_all(x, axes, split_axis=0, concat_axis=0, tiled=True)  37.4 us
    all_to_all x3, starting transfers between devices, exchange(): return lax.all_to_all(x, axes, split_axis=0, concat_axis=0, tiled=True)  19.9 us
    pallas_call x1, Pallas kernels, shards(): pl.pallas_call(owner_kernel, grid=(SLOTS,), out_shape=[stat_shape, stat_s...  15.8 us
    ppermute x3, starting transfers between devices, add_permuted(): return sum([lax.ppermute(x, axis, perm) for perm in perms], x)  4.45 us
    ppermute x3, waiting for transfers between devices, add_permuted(): return sum([lax.ppermute(x, axis, perm) for perm in perms], x)  3.93 us
  transfers between devices with their start and end apart: 6, of which 5 were waited for; matrix products, arithmetic and copies ran while one was open for 0% of the time, Pallas kernels for 1%

profile of v9, /device:TPU:8, one launch (start us, length us, event | category | flops | bytes accessed | tf_op | source)
XLA Modules:
  0.0 126.6 jit_solution(17665102296390124634)
XLA Ops:
  0.6 8.5 %all-to-all-start = ((bf16[4,8,4096]{2,1,0:T(8,128)(2,1)}), bf16[4,8,4096]{2,1,0:T(8,128)(2,1)S(1)}, u32[]{:S(2)}, u32[]{:S(2)}) async-start(bf16[4,8,4096]{2,1,0:T(8,128)(2,1)} %bitcast.11), calls=%async_computation | async-start | bytes 524288 | tf_op jit(solution)/shard_map/all_to_all | solution.py:241
  9.1 0.0 copy-start
  9.1 0.7 copy-done
  9.8 0.0 copy-start.1
  9.8 1.5 %places.1.place_ref = s32[32]{0:T(128)S(1)} custom-call(s32[1]{0:T(128)} %bitcast.shard_ref, s32[4,32]{1,0:T(4,128)S(1)} %copy-done), custom_call_target="tpu_custom_call" | custom-call | flops 1000 | bytes 1000 | tf_op jit(solution)/shard_map/places/pallas_call | solution.py:257
  11.3 8.6 %all-to-all-done.in_ref = bf16[4,8,4096]{2,1,0:T(8,128)(2,1)S(1)} async-done(((bf16[4,8,4096]{2,1,0:T(8,128)(2,1)}), bf16[4,8,4096]{2,1,0:T(8,128)(2,1)S(1)}, u32[]{:S(2)}, u32[]{:S(2)}) %all-to-all-start) | async-done | bytes 262176 | tf_op jit(solution)/shard_map/all_to_all | solution.py:241
  19.8 1.7 %route.1 = bf16[64,8,1024]{2,1,0:T(8,128)(2,1)} custom-call(s32[32]{0:T(128)S(1)} %places.1.place_ref, bf16[4,8,4096]{2,1,0:T(8,128)(2,1)S(1)} %all-to-all-done.in_ref), custom_call_target="tpu_custom_call" | custom-call | tf_op jit(solution)/shard_map/route/pallas_call | solution.py:268
  21.5 6.6 %all-to-all-start.1 = ((bf16[64,8,1024]{2,1,0:T(8,128)(2,1)}), bf16[64,8,1024]{2,1,0:T(8,128)(2,1)S(1)}, u32[]{:S(2)}, u32[]{:S(2)}) async-start(bf16[64,8,1024]{2,1,0:T(8,128)(2,1)} %route.1), calls=%async_computation.1 | async-start | bytes 2097152 | tf_op jit(solution)/shard_map/all_to_all | solution.py:241
  28.2 27.1 %all-to-all-done.1 = bf16[64,8,1024]{2,1,0:T(8,128)(2,1)S(1)} async-done(((bf16[64,8,1024]{2,1,0:T(8,128)(2,1)}), bf16[64,8,1024]{2,1,0:T(8,128)(2,1)S(1)}, u32[]{:S(2)}, u32[]{:S(2)}) %all-to-all-start.1) | async-done | bytes 1048608 | tf_op jit(solution)/shard_map/all_to_all | solution.py:241
  55.2 0.0 copy-done.1
  55.2 15.8 %owner.1 = (f32[2,512,512]{2,1,0:T(8,128)}, f32[2,512,512]{2,1,0:T(8,128)}, s16[64,8,1152]{2,1,0:T(8,128)(2,1)S(1)}) custom-call(s32[1]{0:T(128)} %bitcast.1.me_ref, s32[32]{0:T(128)S(1)} %places.1.place_ref, bf16[512,1024]{1,0:T(8,128)(2,1)S(1)} %bitcast.9, f32[2,512,512]{2,1,0:T(8,128)S(1)} %bitcast.10, f32[2,512,512]{2,1,0:T(8,128)} %bitcast.13), custom_call_target="tpu_custom_call" | custom-call | flops 13421772800 | bytes 12582912 | tf_op jit(solution)/shard_map/owner/pallas_call | solution.py:282
  71.1 37.4 %all_to_all.20.in_ref = s16[64,8,1152]{2,1,0:T(8,128)(2,1)S(1)} all-to-all(s16[64,8,1152]{2,1,0:T(8,128)(2,1)S(1)} %get-tuple-element.8), channel_id=1, replica_groups=mesh['g'=4,'r'=16,'mp'=4] {'r','g'}, dimensions={0} | all-to-all | bytes 2359296 | tf_op jit(solution)/shard_map/all_to_all | solution.py:241
  108.5 1.5 %collect.1 = (s16[4,8,4224]{2,1,0:T(8,128)(2,1)}, f32[8,128]{1,0:T(8,128)S(1)}) custom-call(s32[32]{0:T(128)S(1)} %places.1.place_ref, s16[64,8,1152]{2,1,0:T(8,128)(2,1)S(1)} %all_to_all.20.in_ref), custom_call_target="tpu_custom_call" | custom-call | tf_op jit(solution)/shard_map/collect/pallas_call | solution.py:318
  109.9 4.8 %all-to-all-start.3 = ((s16[4,8,4224]{2,1,0:T(8,128)(2,1)}), s16[4,8,4224]{2,1,0:T(8,128)(2,1)S(1)}, u32[]{:S(2)}, u32[]{:S(2)}) async-start(s16[4,8,4224]{2,1,0:T(8,128)(2,1)} %get-tuple-element.10), calls=%async_computation.3 | async-start | bytes 540672 | tf_op jit(solution)/shard_map/all_to_all | solution.py:241
  114.8 2.8 %collective-permute-start.2 = (f32[8,128]{1,0:T(8,128)S(1)}, f32[8,128]{1,0:T(8,128)S(1)}, u32[]{:S(2)}, u32[]{:S(2)}) collective-permute-start(f32[8,128]{1,0:T(8,128)S(1)} %get-tuple-element.9), channel_id=1, source_target_pairs={{0,3},{1,0},{2,1},{3,2},{4,7},{5,4},{6,5},{7,6},{8,11},{9,8},{10,9... | collective-permute-start | bytes 12296 | tf_op jit(solution)/shard_map/ppermute | solution.py:245
  117.5 0.8 collective-permute-start.1
  118.3 0.9 collective-permute-start
  119.2 0.0 collective-permute-done.2
  119.2 3.4 %collective-permute-done.1 = f32[8,128]{1,0:T(8,128)S(1)} collective-permute-done((f32[8,128]{1,0:T(8,128)S(1)}, f32[8,128]{1,0:T(8,128)S(1)}, u32[]{:S(2)}, u32[]{:S(2)}) %collective-permute-start.1) | collective-permute-done | bytes 4128 | tf_op jit(solution)/shard_map/ppermute | solution.py:245
  122.6 0.5 collective-permute-done
  123.1 2.4 %all-to-all-done.3.in_ref = s16[4,8,4224]{2,1,0:T(8,128)(2,1)S(1)} async-done(((s16[4,8,4224]{2,1,0:T(8,128)(2,1)}), s16[4,8,4224]{2,1,0:T(8,128)(2,1)S(1)}, u32[]{:S(2)}, u32[]{:S(2)}) %all-to-all-start.3) | async-done | bytes 270368 | tf_op jit(solution)/shard_map/all_to_all | solution.py:241
  125.6 1.0 finish.1
  (1 shorter events, 0.0 us)
Async XLA Ops:
  0.6 19.2 %all-to-all-start = ((bf16[4,8,4096]{2,1,0:T(8,128)(2,1)}), bf16[4,8,4096]{2,1,0:T(8,128)(2,1)S(1)}, u32[]{:S(2)}, u32[]{:S(2)}) async-start(bf16[4,8,4096]{2,1,0:T(8,128)(2,1)} %bitcast.11), calls=%async_computation | async-start | bytes 524288 | tf_op jit(solution)/shard_map/all_to_all | solution.py:241
  9.1 0.7 copy-start
  9.8 45.5 %copy-start.1 = (f32[1,1,2,512,512]{4,3,2,1,0:T(8,128)S(1)}, f32[1,1,2,512,512]{4,3,2,1,0:T(8,128)}, u32[]{:S(2)}) copy-start(f32[1,1,2,512,512]{4,3,2,1,0:T(8,128)} %param.6) | copy-start | bytes 6291460
  21.5 33.7 %all-to-all-start.1 = ((bf16[64,8,1024]{2,1,0:T(8,128)(2,1)}), bf16[64,8,1024]{2,1,0:T(8,128)(2,1)S(1)}, u32[]{:S(2)}, u32[]{:S(2)}) async-start(bf16[64,8,1024]{2,1,0:T(8,128)(2,1)} %route.1), calls=%async_computation.1 | async-start | bytes 2097152 | tf_op jit(solution)/shard_map/all_to_all | solution.py:241
  109.9 15.6 %all-to-all-start.3 = ((s16[4,8,4224]{2,1,0:T(8,128)(2,1)}), s16[4,8,4224]{2,1,0:T(8,128)(2,1)S(1)}, u32[]{:S(2)}, u32[]{:S(2)}) async-start(s16[4,8,4224]{2,1,0:T(8,128)(2,1)} %get-tuple-element.10), calls=%async_computation.3 | async-start | bytes 540672 | tf_op jit(solution)/shard_map/all_to_all | solution.py:241
  114.8 4.5 %collective-permute-start.2 = (f32[8,128]{1,0:T(8,128)S(1)}, f32[8,128]{1,0:T(8,128)S(1)}, u32[]{:S(2)}, u32[]{:S(2)}) collective-permute-start(f32[8,128]{1,0:T(8,128)S(1)} %get-tuple-element.9), channel_id=1, source_target_pairs={{0,3},{1,0},{2,1},{3,2},{4,7},{5,4},{6,5},{7,6},{8,11},{9,8},{10,9... | collective-permute-start | bytes 12296 | tf_op jit(solution)/shard_map/ppermute | solution.py:245
  117.5 5.1 %collective-permute-start.1 = (f32[8,128]{1,0:T(8,128)S(1)}, f32[8,128]{1,0:T(8,128)S(1)}, u32[]{:S(2)}, u32[]{:S(2)}) collective-permute-start(f32[8,128]{1,0:T(8,128)S(1)} %get-tuple-element.9), channel_id=1, source_target_pairs={{0,2},{1,3},{2,0},{3,1},{4,6},{5,7},{6,4},{7,5},{8,10},{9,11},{10,... | collective-permute-start | bytes 12296 | tf_op jit(solution)/shard_map/ppermute | solution.py:245
  118.3 4.8 %collective-permute-start = (f32[8,128]{1,0:T(8,128)S(1)}, f32[8,128]{1,0:T(8,128)S(1)}, u32[]{:S(2)}, u32[]{:S(2)}) collective-permute-start(f32[8,128]{1,0:T(8,128)S(1)} %get-tuple-element.9), channel_id=1, source_target_pairs={{0,1},{1,2},{2,3},{3,0},{4,5},{5,6},{6,7},{7,4},{8,9},{9,10},{10,1... | collective-permute-start | bytes 12296 | tf_op jit(solution)/shard_map/ppermute | solution.py:245

commit v10 on v9

--- a/solution.py
+++ b/solution.py
@@ -44,12 +44,21 @@
         place_ref[b] = (lax.rem(owner, MEMBERS) * GROUPS + owner // MEMBERS) * SLOTS + slot
 
 
-def route_kernel(place_ref, in_ref, out_ref):
+def route_kernel(place_ref, in_ref, out_ref, sem):
+    copies = []
     for row in range(GROUPS):
         for j in range(PER_SHARD):
             place = place_ref[row * PER_SHARD + j]
             columns = pl.ds(pl.multiple_of(lax.rem(place, SLOTS) * BLOCK, BLOCK), BLOCK)
-            out_ref[place // SLOTS, :, columns] = in_ref[row, :, pl.ds(j * BLOCK, BLOCK)]
+            copy = pltpu.make_async_copy(
+                in_ref.at[row, :, pl.ds(j * BLOCK, BLOCK)],
+                out_ref.at[place // SLOTS, :, columns],
+                sem.at[row, j],
+            )
+            copy.start()
+            copies.append(copy)
+    for copy in copies:
+        copy.wait()
 
 
 def collect_kernel(place_ref, in_ref, out_ref, sums_ref):
@@ -123,33 +132,25 @@
 
 
 def owner_kernel(me_ref, place_ref, got_ref, left_ref, right_ref, new_left_ref, new_right_ref, coded_ref,
-                 power_ref, sums_ref, prev_ref, new_ref, n_ref, raw_ref, n_parts_ref, q_parts_ref,
-                 h_parts_ref, r_parts_ref, got_sem, new_sem):
-    slot = pl.program_id(0)
-
-    def fetch(side, k):
+                 prev_ref, new_ref, n_ref, raw_ref, n_parts_ref, q_parts_ref, h_parts_ref, r_parts_ref,
+                 staged_ref, got_sem, new_sem, coded_sem):
+    slots = range(SLOTS)
+    both = [(slot, side) for slot in slots for side in range(2)]
+
+    def fetch(slot, side):
         source = (left_ref, right_ref)[side]
-        return pltpu.make_async_copy(source.at[k], prev_ref.at[side, k], got_sem.at[side, k])
-
-    def write(side, k):
+        return pltpu.make_async_copy(source.at[slot], prev_ref.at[slot, side], got_sem.at[slot, side])
+
+    def write(slot, side):
         target = (new_left_ref, new_right_ref)[side]
-        return pltpu.make_async_copy(new_ref.at[side, k], target.at[k], new_sem.at[side, k])
-
-    @pl.when(slot == 0)
-    def _():
-        for k in range(SLOTS):
-            for side in range(2):
-                fetch(side, k).start()
-
-    wanted = me_ref[0] * SLOTS + slot
-    used = place_ref[0] == wanted
-    for b in range(1, BLOCKS):
-        used = used | (place_ref[b] == wanted)
-    place = pl.ds(pl.multiple_of(slot * BLOCK, BLOCK), BLOCK)
-    block = got_ref[:, place]
-    block = jnp.where(used, block, jnp.zeros_like(block))
-    turned = block.T
-    steps = [(rows, columns, side) for rows, columns in ((ALL, LOW), (HIGH, HIGH)) for side in range(2)]
+        return pltpu.make_async_copy(new_ref.at[slot, side], target.at[slot], new_sem.at[slot, side])
+
+    def send(slot):
+        last = BLOCK + 128 if slot == SLOTS - 1 else BLOCK
+        columns = pl.ds(slot * BLOCK, last)
+        return pltpu.make_async_copy(
+            staged_ref.at[:, :, columns], coded_ref.at[:, :, columns], coded_sem.at[slot]
+        )
 
     def eye(rows, columns, value):
         shape = (rows.stop - rows.start, columns.stop - columns.start)
@@ -157,84 +158,106 @@
         across = lax.broadcasted_iota(jnp.int32, shape, 1) + columns.start
         return jnp.where(down == across, jnp.float32(value), jnp.float32(0))
 
-    def pair(ref, side):
-        return ref.at[side, 0], ref.at[side, 1]
-
-    norms = []
-    for side in range(2):
+    def pair(ref, slot, side):
+        return ref.at[slot, side, 0], ref.at[slot, side, 1]
+
+    for slot, side in both:
+        fetch(slot, side).start()
+    blocks, turneds = [], []
+    for slot in slots:
+        wanted = me_ref[0] * SLOTS + slot
+        used = place_ref[0] == wanted
+        for b in range(1, BLOCKS):
+            used = used | (place_ref[b] == wanted)
+        block = got_ref[:, slot * BLOCK : (slot + 1) * BLOCK]
+        block = jnp.where(used, block, jnp.zeros_like(block))
+        blocks.append(block)
+        turneds.append(block.T)
+
+    norms = {}
+    for slot, side in both:
+        block, turned = blocks[slot], turneds[slot]
         gram = dot(block, turned) if side == 0 else dot(turned, block)
-        fetch(side, slot).wait()
-        stat = BETA * prev_ref[side, slot] + gram
-        new_ref[side, slot] = stat
-        write(side, slot).start()
+        fetch(slot, side).wait()
+        stat = BETA * prev_ref[slot, side] + gram
+        new_ref[slot, side] = stat
+        write(slot, side).start()
         damped = stat + eye(ALL, ALL, EPS_DAMP)
         norm = jnp.sqrt(jnp.sum(damped * damped, keepdims=True))
         n = damped * (1.0 / norm)
-        n_ref[side] = n
-        put(pair(n_parts_ref, side), ALL, ALL, n)
-        norms.append(norm)
-    for rows, columns, side in steps:
-        n = n_ref[side, rows, columns]
-        n_parts = pair(n_parts_ref, side)
+        n_ref[slot, side] = n
+        put(pair(n_parts_ref, slot, side), ALL, ALL, n)
+        norms[slot, side] = norm
+
+    steps = [(rows, columns, k, s) for rows, columns in ((ALL, LOW), (HIGH, HIGH)) for k, s in both]
+    for rows, columns, slot, side in steps:
+        n = n_ref[slot, side, rows, columns]
+        n_parts, q_parts = pair(n_parts_ref, slot, side), pair(q_parts_ref, slot, side)
+        h_parts = pair(h_parts_ref, slot, side)
         n2 = dot3(n_parts, n_parts, rows, columns)
-        put(pair(q_parts_ref, side), rows, columns, eye(rows, columns, 1.5625) - 2.5 * n + n2)
-        put(pair(h_parts_ref, side), rows, columns, 1.25 * n - n2)
+        put(q_parts, rows, columns, eye(rows, columns, 1.5625) - 2.5 * n + n2)
+        put(h_parts, rows, columns, 1.25 * n - n2)
         if columns == LOW:
-            mirror(pair(q_parts_ref, side))
-            mirror(pair(h_parts_ref, side))
-    for rows, columns, side in steps:
-        q_parts = pair(q_parts_ref, side)
-        put(pair(r_parts_ref, side), rows, columns, dot3(q_parts, q_parts, rows, columns))
+            mirror(q_parts)
+            mirror(h_parts)
+    for rows, columns, slot, side in steps:
+        q_parts, r_parts = pair(q_parts_ref, slot, side), pair(r_parts_ref, slot, side)
+        put(r_parts, rows, columns, dot3(q_parts, q_parts, rows, columns))
         if columns == LOW:
-            mirror(pair(r_parts_ref, side))
-    for rows, columns, side in steps:
-        product = dot3(pair(h_parts_ref, side), pair(r_parts_ref, side), rows, columns)
-        product = eye(rows, columns, 1.5625) - 1.25 * n_ref[side, rows, columns] - product
-        product = product * lax.rsqrt(jnp.sqrt(0.25 * norms[side]))
-        put(pair(n_parts_ref, side), rows, columns, product)
+            mirror(r_parts)
+    for rows, columns, slot, side in steps:
+        product = dot3(pair(h_parts_ref, slot, side), pair(r_parts_ref, slot, side), rows, columns)
+        product = eye(rows, columns, 1.5625) - 1.25 * n_ref[slot, side, rows, columns] - product
+        product = product * lax.rsqrt(jnp.sqrt(0.25 * norms[slot, side]))
+        put(pair(n_parts_ref, slot, side), rows, columns, product)
         if columns == LOW:
-            mirror(pair(n_parts_ref, side))
-    left_root = jnp.concatenate([n_parts_ref[0, 0], n_parts_ref[0, 1]], axis=1)
+            mirror(pair(n_parts_ref, slot, side))
     for columns in (LOW, HIGH):
-        part = block[:, columns]
-        put(pair(q_parts_ref, 0), ALL, columns, dot(left_root, jnp.concatenate([part, part], axis=0)))
+        for slot in slots:
+            high, low = pair(n_parts_ref, slot, 0)
+            part = blocks[slot][:, columns]
+            half = dot(jnp.concatenate([high[...], low[...]], axis=1), jnp.concatenate([part, part], axis=0))
+            put(pair(q_parts_ref, slot, 0), ALL, columns, half)
+    grad_sq = jnp.zeros((1, 1), jnp.float32)
     update_sq = jnp.zeros((1, 1), jnp.float32)
-    for columns in (LOW, HIGH):
-        raw = dot3(pair(q_parts_ref, 0), pair(n_parts_ref, 1), ALL, columns)
-        raw_ref[:, columns] = raw
-        update_sq += jnp.sum(raw * raw, keepdims=True)
-    wide = block.astype(jnp.float32)
-    grad_sq = jnp.sum(wide * wide, keepdims=True)
+    for slot in slots:
+        for columns in (LOW, HIGH):
+            raw = dot3(pair(q_parts_ref, slot, 0), pair(n_parts_ref, slot, 1), ALL, columns)
+            raw_ref[slot, :, columns] = raw
+            update_sq += jnp.sum(raw * raw, keepdims=True)
+        wide = blocks[slot].astype(jnp.float32)
+        grad_sq += jnp.sum(wide * wide, keepdims=True)
+
+    row_powers = []
+    for slot in slots:
+        raw = raw_ref[slot]
+        largest = jnp.max(jnp.abs(raw), axis=1, keepdims=True)
+        power = jnp.ceil(jnp.log2(jnp.maximum(largest, 1e-30)) + 0.001) - 15.0
+        coded = jnp.round(raw * jnp.exp2(-power)).astype(jnp.int32)
+        for p in range(OWNERS):
+            staged_ref[p, :, pl.ds(slot * BLOCK, BLOCK)] = coded[p * LINES : (p + 1) * LINES].astype(jnp.int16)
+        row_powers.append(power)
+        if slot < SLOTS - 1:
+            send(slot).start()
+
     lane = lax.broadcasted_iota(jnp.int32, (1, 128), 1)
-    sums = jnp.where(lane < UPDATE_LANE, grad_sq, update_sq)
-    raw = raw_ref[...]
-    largest = jnp.max(jnp.abs(raw), axis=1, keepdims=True)
-    power = jnp.ceil(jnp.log2(jnp.maximum(largest, 1e-30)) + 0.001) - 15.0
-    coded = jnp.round(raw * jnp.exp2(-power)).astype(jnp.int32)
+    total = jnp.where(lane < UPDATE_LANE, grad_sq, update_sq)
+    exponent = jnp.ceil(jnp.log2(jnp.maximum(total, 1e-30)))
+    mantissa = total * jnp.exp2(12.0 - exponent)
+    upper = jnp.floor(mantissa)
+    lower = jnp.round((mantissa - upper) * 4096.0)
+    start = jnp.where(lane < UPDATE_LANE, GRAD_LANE, UPDATE_LANE)
+    digits = jnp.where(lane == start, exponent - 12.0, jnp.where(lane == start + 1, upper, lower))
+    held = (lane >= GRAD_LANE) & (lane < UPDATE_LANE + 3)
+    powers = jnp.where(lane < 64, row_powers[0], row_powers[1])
+    powers = jnp.where(held, digits, powers).astype(jnp.int32)
     for p in range(OWNERS):
-        coded_ref[p, :, place] = coded[p * LINES : (p + 1) * LINES].astype(jnp.int16)
-
-    @pl.when(slot == 0)
-    def _():
-        sums_ref[...] = sums
-        power_ref[...] = jnp.broadcast_to(power, power_ref.shape)
-
-    @pl.when(slot == SLOTS - 1)
-    def _():
-        total = sums_ref[...] + sums
-        exponent = jnp.ceil(jnp.log2(jnp.maximum(total, 1e-30)))
-        mantissa = total * jnp.exp2(12.0 - exponent)
-        upper = jnp.floor(mantissa)
-        lower = jnp.round((mantissa - upper) * 4096.0)
-        start = jnp.where(lane < UPDATE_LANE, GRAD_LANE, UPDATE_LANE)
-        digits = jnp.where(lane == start, exponent - 12.0, jnp.where(lane == start + 1, upper, lower))
-        held = (lane >= GRAD_LANE) & (lane < UPDATE_LANE + 3)
-        powers = jnp.where(held, digits, jnp.where(lane < 64, power_ref[...], power)).astype(jnp.int32)
-        for p in range(OWNERS):
-            coded_ref[p, :, pl.ds(SLOTS * BLOCK, 128)] = powers[p * LINES : (p + 1) * LINES].astype(jnp.int16)
-        for k in range(SLOTS):
-            for side in range(2):
-                write(side, k).wait()
+        staged_ref[p, :, pl.ds(SLOTS * BLOCK, 128)] = powers[p * LINES : (p + 1) * LINES].astype(jnp.int16)
+    send(SLOTS - 1).start()
+    for slot, side in both:
+        write(slot, side).wait()
+    for slot in slots:
+        send(slot).wait()
 
 
 def exchange(x, axes):
@@ -269,45 +292,38 @@
         route_kernel,
         out_shape=jax.ShapeDtypeStruct((OWNERS, LINES, SLOTS * BLOCK), jnp.bfloat16),
         in_specs=[SMEM, WHOLE],
-        out_specs=WHOLE,
+        out_specs=pl.BlockSpec(memory_space=pl.ANY),
+        scratch_shapes=[pltpu.SemaphoreType.DMA((GROUPS, PER_SHARD))],
         compiler_params=params(4),
         name="route",
     )(places, pieces)
     got = exchange(routed, ("r", "g")).reshape(BLOCK, SLOTS * BLOCK)
 
     stat_spec = pl.BlockSpec(memory_space=pl.ANY)
-    parts = pltpu.VMEM((2, 2, BLOCK, BLOCK), jnp.bfloat16)
     stat_shape = jax.ShapeDtypeStruct((SLOTS, BLOCK, BLOCK), jnp.float32)
     coded_shape = (OWNERS, LINES, SLOTS * BLOCK + 128)
+    wide = pltpu.VMEM((SLOTS, 2, BLOCK, BLOCK), jnp.float32)
+    parts = pltpu.VMEM((SLOTS, 2, 2, BLOCK, BLOCK), jnp.bfloat16)
     new_left, new_right, coded = pl.pallas_call(
         owner_kernel,
-        grid=(SLOTS,),
-        out_shape=[
-            stat_shape,
-            stat_shape,
-            jax.ShapeDtypeStruct(coded_shape, jnp.int16),
-        ],
+        out_shape=[stat_shape, stat_shape, jax.ShapeDtypeStruct(coded_shape, jnp.int16)],
         in_specs=[SMEM, SMEM, WHOLE, stat_spec, stat_spec],
-        out_specs=[
-            stat_spec,
-            stat_spec,
-            WHOLE,
-        ],
+        out_specs=[stat_spec, stat_spec, stat_spec],
         scratch_shapes=[
-            pltpu.VMEM((BLOCK, 128), jnp.float32),
-            pltpu.VMEM((1, 128), jnp.float32),
-            pltpu.VMEM((2, SLOTS, BLOCK, BLOCK), jnp.float32),
-            pltpu.VMEM((2, SLOTS, BLOCK, BLOCK), jnp.float32),
-            pltpu.VMEM((2, BLOCK, BLOCK), jnp.float32),
-            pltpu.VMEM((BLOCK, BLOCK), jnp.float32),
+            wide,
+            wide,
+            wide,
+            pltpu.VMEM((SLOTS, BLOCK, BLOCK), jnp.float32),
             parts,
             parts,
             parts,
             parts,
-            pltpu.SemaphoreType.DMA((2, SLOTS)),
-            pltpu.SemaphoreType.DMA((2, SLOTS)),
+            pltpu.VMEM(coded_shape, jnp.int16),
+            pltpu.SemaphoreType.DMA((SLOTS, 2)),
+            pltpu.SemaphoreType.DMA((SLOTS, 2)),
+            pltpu.SemaphoreType.DMA((SLOTS,)),
         ],
-        compiler_params=params(48),
+        compiler_params=params(50),
         cost_estimate=pl.CostEstimate(
             flops=50 * 2 * BLOCK**3, bytes_accessed=12 * MIB, transcendentals=0
         ),

time: 129 us -> 129 us (level)
  no operation moved by 1% of the time
where the time goes in v10:
time: 129 us; the launch traced here: 127 us
  waiting for transfers between devices  42 us (33%)
  blocking collectives  37.4 us (29%)
  starting transfers between devices  24.4 us (19%)
  Pallas kernels  21.7 us (17%)
    all_to_all x3, waiting for transfers between devices, exchange(): return lax.all_to_all(x, axes, split_axis=0, concat_axis=0, tiled=True)  38 us
    all_to_all x1, blocking collectives, exchange(): return lax.all_to_all(x, axes, split_axis=0, concat_axis=0, tiled=True)  37.4 us
    all_to_all x3, starting transfers between devices, exchange(): return lax.all_to_all(x, axes, split_axis=0, concat_axis=0, tiled=True)  19.9 us
    pallas_call x1, Pallas kernels, shards(): pl.pallas_call(owner_kernel, out_shape=[stat_shape, stat_shape, jax.Shape...  16 us
    ppermute x3, starting transfers between devices, add_permuted(): return sum([lax.ppermute(x, axis, perm) for perm in perms], x)  4.45 us
    ppermute x3, waiting for transfers between devices, add_permuted(): return sum([lax.ppermute(x, axis, perm) for perm in perms], x)  3.93 us
  transfers between devices with their start and end apart: 6, of which 5 were waited for; matrix products, arithmetic and copies ran while one was open for 0% of the time, Pallas kernels for 1%

profile of v10, /device:TPU:8, one launch (start us, length us, event | category | flops | bytes accessed | tf_op | source)
XLA Modules:
  0.0 126.7 jit_solution(13245054937734275235)
XLA Ops:
  0.6 8.5 %all-to-all-start = ((bf16[4,8,4096]{2,1,0:T(8,128)(2,1)}), bf16[4,8,4096]{2,1,0:T(8,128)(2,1)S(1)}, u32[]{:S(2)}, u32[]{:S(2)}) async-start(bf16[4,8,4096]{2,1,0:T(8,128)(2,1)} %bitcast.10), calls=%async_computation | async-start | bytes 524288 | tf_op jit(solution)/shard_map/all_to_all | solution.py:264
  9.1 0.0 copy-start
  9.1 0.7 copy-done
  9.8 1.5 %places.1.place_ref = s32[32]{0:T(128)S(1)} custom-call(s32[1]{0:T(128)} %bitcast.shard_ref, s32[4,32]{1,0:T(4,128)S(1)} %copy-done), custom_call_target="tpu_custom_call" | custom-call | flops 1000 | bytes 1000 | tf_op jit(solution)/shard_map/places/pallas_call | solution.py:280
  11.3 8.6 %all-to-all-done.in_ref = bf16[4,8,4096]{2,1,0:T(8,128)(2,1)S(1)} async-done(((bf16[4,8,4096]{2,1,0:T(8,128)(2,1)}), bf16[4,8,4096]{2,1,0:T(8,128)(2,1)S(1)}, u32[]{:S(2)}, u32[]{:S(2)}) %all-to-all-start) | async-done | bytes 262176 | tf_op jit(solution)/shard_map/all_to_all | solution.py:264
  19.8 1.7 %route.1 = bf16[64,8,1024]{2,1,0:T(8,128)(2,1)} custom-call(s32[32]{0:T(128)S(1)} %places.1.place_ref, bf16[4,8,4096]{2,1,0:T(8,128)(2,1)S(1)} %all-to-all-done.in_ref), custom_call_target="tpu_custom_call" | custom-call | tf_op jit(solution)/shard_map/route/pallas_call | solution.py:291
  21.5 6.6 %all-to-all-start.1 = ((bf16[64,8,1024]{2,1,0:T(8,128)(2,1)}), bf16[64,8,1024]{2,1,0:T(8,128)(2,1)S(1)}, u32[]{:S(2)}, u32[]{:S(2)}) async-start(bf16[64,8,1024]{2,1,0:T(8,128)(2,1)} %route.1), calls=%async_computation.1 | async-start | bytes 2097152 | tf_op jit(solution)/shard_map/all_to_all | solution.py:264
  28.1 27.1 %all-to-all-done.1 = bf16[64,8,1024]{2,1,0:T(8,128)(2,1)S(1)} async-done(((bf16[64,8,1024]{2,1,0:T(8,128)(2,1)}), bf16[64,8,1024]{2,1,0:T(8,128)(2,1)S(1)}, u32[]{:S(2)}, u32[]{:S(2)}) %all-to-all-start.1) | async-done | bytes 1048608 | tf_op jit(solution)/shard_map/all_to_all | solution.py:264
  55.2 16.0 %owner.1 = (f32[2,512,512]{2,1,0:T(8,128)}, f32[2,512,512]{2,1,0:T(8,128)}, s16[64,8,1152]{2,1,0:T(8,128)(2,1)S(1)}) custom-call(s32[1]{0:T(128)} %bitcast.1.me_ref, s32[32]{0:T(128)S(1)} %places.1.place_ref, bf16[512,1024]{1,0:T(8,128)(2,1)S(1)} %bitcast.9, f32[2,512,512]{2,1,0:T(8,128)} %bitcast.12, f32[2,512,512]{2,1,0:T(8,128)} %bitcast.13), custom_call_target="tpu_custom_call" | custom-call | flops 13421772800 | bytes 12582912 | tf_op jit(solution)/shard_map/owner/pallas_call | solution.py:307
  71.2 37.4 %all_to_all.20.in_ref = s16[64,8,1152]{2,1,0:T(8,128)(2,1)S(1)} all-to-all(s16[64,8,1152]{2,1,0:T(8,128)(2,1)S(1)} %get-tuple-element.8), channel_id=1, replica_groups=mesh['g'=4,'r'=16,'mp'=4] {'r','g'}, dimensions={0} | all-to-all | bytes 2359296 | tf_op jit(solution)/shard_map/all_to_all | solution.py:264
  108.6 1.5 %collect.1 = (s16[4,8,4224]{2,1,0:T(8,128)(2,1)}, f32[8,128]{1,0:T(8,128)S(1)}) custom-call(s32[32]{0:T(128)S(1)} %places.1.place_ref, s16[64,8,1152]{2,1,0:T(8,128)(2,1)S(1)} %all_to_all.20.in_ref), custom_call_target="tpu_custom_call" | custom-call | tf_op jit(solution)/shard_map/collect/pallas_call | solution.py:334
  110.1 4.8 %all-to-all-start.3 = ((s16[4,8,4224]{2,1,0:T(8,128)(2,1)}), s16[4,8,4224]{2,1,0:T(8,128)(2,1)S(1)}, u32[]{:S(2)}, u32[]{:S(2)}) async-start(s16[4,8,4224]{2,1,0:T(8,128)(2,1)} %get-tuple-element.10), calls=%async_computation.3 | async-start | bytes 540672 | tf_op jit(solution)/shard_map/all_to_all | solution.py:264
  114.9 2.8 %collective-permute-start.2 = (f32[8,128]{1,0:T(8,128)S(1)}, f32[8,128]{1,0:T(8,128)S(1)}, u32[]{:S(2)}, u32[]{:S(2)}) collective-permute-start(f32[8,128]{1,0:T(8,128)S(1)} %get-tuple-element.9), channel_id=1, source_target_pairs={{0,3},{1,0},{2,1},{3,2},{4,7},{5,4},{6,5},{7,6},{8,11},{9,8},{10,9... | collective-permute-start | bytes 12296 | tf_op jit(solution)/shard_map/ppermute | solution.py:268
  117.7 0.8 collective-permute-start.1
  118.5 0.9 collective-permute-start
  119.4 0.0 collective-permute-done.2
  119.4 3.4 %collective-permute-done.1 = f32[8,128]{1,0:T(8,128)S(1)} collective-permute-done((f32[8,128]{1,0:T(8,128)S(1)}, f32[8,128]{1,0:T(8,128)S(1)}, u32[]{:S(2)}, u32[]{:S(2)}) %collective-permute-start.1) | collective-permute-done | bytes 4128 | tf_op jit(solution)/shard_map/ppermute | solution.py:268
  122.8 0.5 collective-permute-done
  123.3 2.4 %all-to-all-done.3.in_ref = s16[4,8,4224]{2,1,0:T(8,128)(2,1)S(1)} async-done(((s16[4,8,4224]{2,1,0:T(8,128)(2,1)}), s16[4,8,4224]{2,1,0:T(8,128)(2,1)S(1)}, u32[]{:S(2)}, u32[]{:S(2)}) %all-to-all-start.3) | async-done | bytes 270368 | tf_op jit(solution)/shard_map/all_to_all | solution.py:264
  125.7 1.0 finish.1
  (1 shorter events, 0.0 us)
Async XLA Ops:
  0.6 19.2 %all-to-all-start = ((bf16[4,8,4096]{2,1,0:T(8,128)(2,1)}), bf16[4,8,4096]{2,1,0:T(8,128)(2,1)S(1)}, u32[]{:S(2)}, u32[]{:S(2)}) async-start(bf16[4,8,4096]{2,1,0:T(8,128)(2,1)} %bitcast.10), calls=%async_computation | async-start | bytes 524288 | tf_op jit(solution)/shard_map/all_to_all | solution.py:264
  9.1 0.7 copy-start
  21.5 33.7 %all-to-all-start.1 = ((bf16[64,8,1024]{2,1,0:T(8,128)(2,1)}), bf16[64,8,1024]{2,1,0:T(8,128)(2,1)S(1)}, u32[]{:S(2)}, u32[]{:S(2)}) async-start(bf16[64,8,1024]{2,1,0:T(8,128)(2,1)} %route.1), calls=%async_computation.1 | async-start | bytes 2097152 | tf_op jit(solution)/shard_map/all_to_all | solution.py:264
  110.1 15.6 %all-to-all-start.3 = ((s16[4,8,4224]{2,1,0:T(8,128)(2,1)}), s16[4,8,4224]{2,1,0:T(8,128)(2,1)S(1)}, u32[]{:S(2)}, u32[]{:S(2)}) async-start(s16[4,8,4224]{2,1,0:T(8,128)(2,1)} %get-tuple-element.10), calls=%async_computation.3 | async-start | bytes 540672 | tf_op jit(solution)/shard_map/all_to_all | solution.py:264
  114.9 4.5 %collective-permute-start.2 = (f32[8,128]{1,0:T(8,128)S(1)}, f32[8,128]{1,0:T(8,128)S(1)}, u32[]{:S(2)}, u32[]{:S(2)}) collective-permute-start(f32[8,128]{1,0:T(8,128)S(1)} %get-tuple-element.9), channel_id=1, source_target_pairs={{0,3},{1,0},{2,1},{3,2},{4,7},{5,4},{6,5},{7,6},{8,11},{9,8},{10,9... | collective-permute-start | bytes 12296 | tf_op jit(solution)/shard_map/ppermute | solution.py:268
  117.7 5.1 %collective-permute-start.1 = (f32[8,128]{1,0:T(8,128)S(1)}, f32[8,128]{1,0:T(8,128)S(1)}, u32[]{:S(2)}, u32[]{:S(2)}) collective-permute-start(f32[8,128]{1,0:T(8,128)S(1)} %get-tuple-element.9), channel_id=1, source_target_pairs={{0,2},{1,3},{2,0},{3,1},{4,6},{5,7},{6,4},{7,5},{8,10},{9,11},{10,... | collective-permute-start | bytes 12296 | tf_op jit(solution)/shard_map/ppermute | solution.py:268
  118.5 4.8 %collective-permute-start = (f32[8,128]{1,0:T(8,128)S(1)}, f32[8,128]{1,0:T(8,128)S(1)}, u32[]{:S(2)}, u32[]{:S(2)}) collective-permute-start(f32[8,128]{1,0:T(8,128)S(1)} %get-tuple-element.9), channel_id=1, source_target_pairs={{0,1},{1,2},{2,3},{3,0},{4,5},{5,6},{6,7},{7,4},{8,9},{9,10},{10,1... | collective-permute-start | bytes 12296 | tf_op jit(solution)/shard_map/ppermute | solution.py:268

commit v11 on v10

--- a/solution.py
+++ b/solution.py
@@ -116,10 +116,9 @@
 
 
 def dot3(a, b, rows, columns):
-    return dot(
-        jnp.concatenate([a[0][rows], a[0][rows], a[1][rows]], axis=1),
-        jnp.concatenate([b[0][:, columns], b[1][:, columns], b[0][:, columns]], axis=0),
-    )
+    count = rows.stop - rows.start
+    stacked = dot(jnp.concatenate([a[0][rows], a[1][rows]], axis=0), b[0][:, columns])
+    return stacked[:count] + (stacked[count:] + dot(a[0][rows], b[1][:, columns]))
 
 
 def put(pair, rows, columns, x):
@@ -215,9 +214,8 @@
     for columns in (LOW, HIGH):
         for slot in slots:
             high, low = pair(n_parts_ref, slot, 0)
-            part = blocks[slot][:, columns]
-            half = dot(jnp.concatenate([high[...], low[...]], axis=1), jnp.concatenate([part, part], axis=0))
-            put(pair(q_parts_ref, slot, 0), ALL, columns, half)
+            half = dot(jnp.concatenate([high[...], low[...]], axis=0), blocks[slot][:, columns])
+            put(pair(q_parts_ref, slot, 0), ALL, columns, half[:BLOCK] + half[BLOCK:])
     grad_sq = jnp.zeros((1, 1), jnp.float32)
     update_sq = jnp.zeros((1, 1), jnp.float32)
     for slot in slots:

time: 129 us -> 129 us (level)
  no operation moved by 1% of the time
where the time goes in v11:
time: 129 us; the launch traced here: 126 us
  waiting for transfers between devices  42 us (33%)
  blocking collectives  37.4 us (29%)
  starting transfers between devices  24.4 us (19%)
  Pallas kernels  21.2 us (16%)
    all_to_all x3, waiting for transfers between devices, exchange(): return lax.all_to_all(x, axes, split_axis=0, concat_axis=0, tiled=True)  38 us
    all_to_all x1, blocking collectives, exchange(): return lax.all_to_all(x, axes, split_axis=0, concat_axis=0, tiled=True)  37.4 us
    all_to_all x3, starting transfers between devices, exchange(): return lax.all_to_all(x, axes, split_axis=0, concat_axis=0, tiled=True)  19.9 us
    pallas_call x1, Pallas kernels, shards(): pl.pallas_call(owner_kernel, out_shape=[stat_shape, stat_shape, jax.Shape...  15.5 us
    ppermute x3, starting transfers between devices, add_permuted(): return sum([lax.ppermute(x, axis, perm) for perm in perms], x)  4.45 us
    ppermute x3, waiting for transfers between devices, add_permuted(): return sum([lax.ppermute(x, axis, perm) for perm in perms], x)  3.93 us
  transfers between devices with their start and end apart: 6, of which 5 were waited for; matrix products, arithmetic and copies ran while one was open for 0% of the time, Pallas kernels for 1%

profile of v11, /device:TPU:8, one launch (start us, length us, event | category | flops | bytes accessed | tf_op | source)
XLA Modules:
  0.0 126.2 jit_solution(12835467348001688990)
XLA Ops:
  0.6 8.5 %all-to-all-start = ((bf16[4,8,4096]{2,1,0:T(8,128)(2,1)}), bf16[4,8,4096]{2,1,0:T(8,128)(2,1)S(1)}, u32[]{:S(2)}, u32[]{:S(2)}) async-start(bf16[4,8,4096]{2,1,0:T(8,128)(2,1)} %bitcast.10), calls=%async_computation | async-start | bytes 524288 | tf_op jit(solution)/shard_map/all_to_all | solution.py:262
  9.1 0.0 copy-start
  9.1 0.7 copy-done
  9.8 1.5 %places.1.place_ref = s32[32]{0:T(128)S(1)} custom-call(s32[1]{0:T(128)} %bitcast.shard_ref, s32[4,32]{1,0:T(4,128)S(1)} %copy-done), custom_call_target="tpu_custom_call" | custom-call | flops 1000 | bytes 1000 | tf_op jit(solution)/shard_map/places/pallas_call | solution.py:278
  11.3 8.6 %all-to-all-done.in_ref = bf16[4,8,4096]{2,1,0:T(8,128)(2,1)S(1)} async-done(((bf16[4,8,4096]{2,1,0:T(8,128)(2,1)}), bf16[4,8,4096]{2,1,0:T(8,128)(2,1)S(1)}, u32[]{:S(2)}, u32[]{:S(2)}) %all-to-all-start) | async-done | bytes 262176 | tf_op jit(solution)/shard_map/all_to_all | solution.py:262
  19.8 1.7 %route.1 = bf16[64,8,1024]{2,1,0:T(8,128)(2,1)} custom-call(s32[32]{0:T(128)S(1)} %places.1.place_ref, bf16[4,8,4096]{2,1,0:T(8,128)(2,1)S(1)} %all-to-all-done.in_ref), custom_call_target="tpu_custom_call" | custom-call | tf_op jit(solution)/shard_map/route/pallas_call | solution.py:289
  21.5 6.6 %all-to-all-start.1 = ((bf16[64,8,1024]{2,1,0:T(8,128)(2,1)}), bf16[64,8,1024]{2,1,0:T(8,128)(2,1)S(1)}, u32[]{:S(2)}, u32[]{:S(2)}) async-start(bf16[64,8,1024]{2,1,0:T(8,128)(2,1)} %route.1), calls=%async_computation.1 | async-start | bytes 2097152 | tf_op jit(solution)/shard_map/all_to_all | solution.py:262
  28.1 27.1 %all-to-all-done.1 = bf16[64,8,1024]{2,1,0:T(8,128)(2,1)S(1)} async-done(((bf16[64,8,1024]{2,1,0:T(8,128)(2,1)}), bf16[64,8,1024]{2,1,0:T(8,128)(2,1)S(1)}, u32[]{:S(2)}, u32[]{:S(2)}) %all-to-all-start.1) | async-done | bytes 1048608 | tf_op jit(solution)/shard_map/all_to_all | solution.py:262
  55.2 15.5 %owner.1 = (f32[2,512,512]{2,1,0:T(8,128)}, f32[2,512,512]{2,1,0:T(8,128)}, s16[64,8,1152]{2,1,0:T(8,128)(2,1)S(1)}) custom-call(s32[1]{0:T(128)} %bitcast.1.me_ref, s32[32]{0:T(128)S(1)} %places.1.place_ref, bf16[512,1024]{1,0:T(8,128)(2,1)S(1)} %bitcast.9, f32[2,512,512]{2,1,0:T(8,128)} %bitcast.12, f32[2,512,512]{2,1,0:T(8,128)} %bitcast.13), custom_call_target="tpu_custom_call" | custom-call | flops 13421772800 | bytes 12582912 | tf_op jit(solution)/shard_map/owner/pallas_call | solution.py:305
  70.8 37.4 %all_to_all.20.in_ref = s16[64,8,1152]{2,1,0:T(8,128)(2,1)S(1)} all-to-all(s16[64,8,1152]{2,1,0:T(8,128)(2,1)S(1)} %get-tuple-element.8), channel_id=1, replica_groups=mesh['g'=4,'r'=16,'mp'=4] {'r','g'}, dimensions={0} | all-to-all | bytes 2359296 | tf_op jit(solution)/shard_map/all_to_all | solution.py:262
  108.1 1.5 %collect.1 = (s16[4,8,4224]{2,1,0:T(8,128)(2,1)}, f32[8,128]{1,0:T(8,128)S(1)}) custom-call(s32[32]{0:T(128)S(1)} %places.1.place_ref, s16[64,8,1152]{2,1,0:T(8,128)(2,1)S(1)} %all_to_all.20.in_ref), custom_call_target="tpu_custom_call" | custom-call | tf_op jit(solution)/shard_map/collect/pallas_call | solution.py:332
  109.6 4.8 %all-to-all-start.3 = ((s16[4,8,4224]{2,1,0:T(8,128)(2,1)}), s16[4,8,4224]{2,1,0:T(8,128)(2,1)S(1)}, u32[]{:S(2)}, u32[]{:S(2)}) async-start(s16[4,8,4224]{2,1,0:T(8,128)(2,1)} %get-tuple-element.10), calls=%async_computation.3 | async-start | bytes 540672 | tf_op jit(solution)/shard_map/all_to_all | solution.py:262
  114.4 2.8 %collective-permute-start.2 = (f32[8,128]{1,0:T(8,128)S(1)}, f32[8,128]{1,0:T(8,128)S(1)}, u32[]{:S(2)}, u32[]{:S(2)}) collective-permute-start(f32[8,128]{1,0:T(8,128)S(1)} %get-tuple-element.9), channel_id=1, source_target_pairs={{0,3},{1,0},{2,1},{3,2},{4,7},{5,4},{6,5},{7,6},{8,11},{9,8},{10,9... | collective-permute-start | bytes 12296 | tf_op jit(solution)/shard_map/ppermute | solution.py:266
  117.2 0.8 collective-permute-start.1
  118.0 0.9 collective-permute-start
  118.9 0.0 collective-permute-done.2
  118.9 3.4 %collective-permute-done.1 = f32[8,128]{1,0:T(8,128)S(1)} collective-permute-done((f32[8,128]{1,0:T(8,128)S(1)}, f32[8,128]{1,0:T(8,128)S(1)}, u32[]{:S(2)}, u32[]{:S(2)}) %collective-permute-start.1) | collective-permute-done | bytes 4128 | tf_op jit(solution)/shard_map/ppermute | solution.py:266
  122.3 0.5 collective-permute-done
  122.8 2.4 %all-to-all-done.3.in_ref = s16[4,8,4224]{2,1,0:T(8,128)(2,1)S(1)} async-done(((s16[4,8,4224]{2,1,0:T(8,128)(2,1)}), s16[4,8,4224]{2,1,0:T(8,128)(2,1)S(1)}, u32[]{:S(2)}, u32[]{:S(2)}) %all-to-all-start.3) | async-done | bytes 270368 | tf_op jit(solution)/shard_map/all_to_all | solution.py:262
  125.2 1.0 finish.1
  (1 shorter events, 0.0 us)
Async XLA Ops:
  0.6 19.2 %all-to-all-start = ((bf16[4,8,4096]{2,1,0:T(8,128)(2,1)}), bf16[4,8,4096]{2,1,0:T(8,128)(2,1)S(1)}, u32[]{:S(2)}, u32[]{:S(2)}) async-start(bf16[4,8,4096]{2,1,0:T(8,128)(2,1)} %bitcast.10), calls=%async_computation | async-start | bytes 524288 | tf_op jit(solution)/shard_map/all_to_all | solution.py:262
  9.1 0.7 copy-start
  21.5 33.7 %all-to-all-start.1 = ((bf16[64,8,1024]{2,1,0:T(8,128)(2,1)}), bf16[64,8,1024]{2,1,0:T(8,128)(2,1)S(1)}, u32[]{:S(2)}, u32[]{:S(2)}) async-start(bf16[64,8,1024]{2,1,0:T(8,128)(2,1)} %route.1), calls=%async_computation.1 | async-start | bytes 2097152 | tf_op jit(solution)/shard_map/all_to_all | solution.py:262
  109.6 15.6 %all-to-all-start.3 = ((s16[4,8,4224]{2,1,0:T(8,128)(2,1)}), s16[4,8,4224]{2,1,0:T(8,128)(2,1)S(1)}, u32[]{:S(2)}, u32[]{:S(2)}) async-start(s16[4,8,4224]{2,1,0:T(8,128)(2,1)} %get-tuple-element.10), calls=%async_computation.3 | async-start | bytes 540672 | tf_op jit(solution)/shard_map/all_to_all | solution.py:262
  114.4 4.5 %collective-permute-start.2 = (f32[8,128]{1,0:T(8,128)S(1)}, f32[8,128]{1,0:T(8,128)S(1)}, u32[]{:S(2)}, u32[]{:S(2)}) collective-permute-start(f32[8,128]{1,0:T(8,128)S(1)} %get-tuple-element.9), channel_id=1, source_target_pairs={{0,3},{1,0},{2,1},{3,2},{4,7},{5,4},{6,5},{7,6},{8,11},{9,8},{10,9... | collective-permute-start | bytes 12296 | tf_op jit(solution)/shard_map/ppermute | solution.py:266
  117.2 5.1 %collective-permute-start.1 = (f32[8,128]{1,0:T(8,128)S(1)}, f32[8,128]{1,0:T(8,128)S(1)}, u32[]{:S(2)}, u32[]{:S(2)}) collective-permute-start(f32[8,128]{1,0:T(8,128)S(1)} %get-tuple-element.9), channel_id=1, source_target_pairs={{0,2},{1,3},{2,0},{3,1},{4,6},{5,7},{6,4},{7,5},{8,10},{9,11},{10,... | collective-permute-start | bytes 12296 | tf_op jit(solution)/shard_map/ppermute | solution.py:266
  118.0 4.8 %collective-permute-start = (f32[8,128]{1,0:T(8,128)S(1)}, f32[8,128]{1,0:T(8,128)S(1)}, u32[]{:S(2)}, u32[]{:S(2)}) collective-permute-start(f32[8,128]{1,0:T(8,128)S(1)} %get-tuple-element.9), channel_id=1, source_target_pairs={{0,1},{1,2},{2,3},{3,0},{4,5},{5,6},{6,7},{7,4},{8,9},{9,10},{10,1... | collective-permute-start | bytes 12296 | tf_op jit(solution)/shard_map/ppermute | solution.py:266

commit v12 on v11

--- a/solution.py
+++ b/solution.py
@@ -61,9 +61,8 @@
         copy.wait()
 
 
-def collect_kernel(place_ref, in_ref, out_ref, sums_ref):
+def collect_kernel(place_ref, in_ref, out_ref):
     lane = lax.broadcasted_iota(jnp.int32, (LINES, 128), 1)
-    line = lax.broadcasted_iota(jnp.int32, (LINES, 128), 0)
     tile = pl.ds(SLOTS * BLOCK, 128)
     for row in range(GROUPS):
         powers = jnp.zeros((LINES, 128), jnp.int32)
@@ -74,6 +73,12 @@
             out_ref[row, :, pl.ds(j * BLOCK, BLOCK)] = in_ref[position, :, columns]
             powers = jnp.where(lane == j + 64 * slot, in_ref[position, :, tile].astype(jnp.int32), powers)
         out_ref[row, :, pl.ds(PER_SHARD * BLOCK, 128)] = powers.astype(jnp.int16)
+
+
+def add_kernel(in_ref, sums_ref):
+    lane = lax.broadcasted_iota(jnp.int32, (LINES, 128), 1)
+    line = lax.broadcasted_iota(jnp.int32, (LINES, 128), 0)
+    tile = pl.ds(SLOTS * BLOCK, 128)
     sums = jnp.zeros((LINES, 128), jnp.float32)
     for first in range(0, OWNERS, LINES):
         digits = jnp.zeros((LINES, 128), jnp.int32)
@@ -329,14 +334,20 @@
     )(me, places, got, prev_left[0, 0], prev_right[0, 0])
 
     returned = exchange(coded, ("r", "g"))
-    back, sums = pl.pallas_call(
+    sums = pl.pallas_call(
+        add_kernel,
+        out_shape=jax.ShapeDtypeStruct((LINES, 128), jnp.float32),
+        in_specs=[WHOLE],
+        out_specs=WHOLE,
+        compiler_params=params(8),
+        name="add",
+    )(returned)
+    sums, returned = lax.optimization_barrier((sums, returned))
+    back = pl.pallas_call(
         collect_kernel,
-        out_shape=[
-            jax.ShapeDtypeStruct((GROUPS, LINES, PER_SHARD * BLOCK + 128), jnp.int16),
-            jax.ShapeDtypeStruct((LINES, 128), jnp.float32),
-        ],
+        out_shape=jax.ShapeDtypeStruct((GROUPS, LINES, PER_SHARD * BLOCK + 128), jnp.int16),
         in_specs=[SMEM, WHOLE],
-        out_specs=[WHOLE, WHOLE],
+        out_specs=WHOLE,
         compiler_params=params(8),
         name="collect",
     )(places, returned)

time: 129 us -> 129 us (level)
  no operation moved by 1% of the time
where the time goes in v12:
time: 129 us; the launch traced here: 126 us
  waiting for transfers between devices  42 us (33%)
  blocking collectives  37.4 us (29%)
  starting transfers between devices  24.4 us (19%)
  Pallas kernels  21.3 us (17%)
    all_to_all x3, waiting for transfers between devices, exchange(): return lax.all_to_all(x, axes, split_axis=0, concat_axis=0, tiled=True)  38 us
    all_to_all x1, blocking collectives, exchange(): return lax.all_to_all(x, axes, split_axis=0, concat_axis=0, tiled=True)  37.4 us
    all_to_all x3, starting transfers between devices, exchange(): return lax.all_to_all(x, axes, split_axis=0, concat_axis=0, tiled=True)  19.9 us
    pallas_call x1, Pallas kernels, shards(): pl.pallas_call(owner_kernel, out_shape=[stat_shape, stat_shape, jax.Shape...  15.5 us
    ppermute x3, starting transfers between devices, add_permuted(): return sum([lax.ppermute(x, axis, perm) for perm in perms], x)  4.45 us
    ppermute x3, waiting for transfers between devices, add_permuted(): return sum([lax.ppermute(x, axis, perm) for perm in perms], x)  3.93 us
  transfers between devices with their start and end apart: 6, of which 5 were waited for; matrix products, arithmetic and copies ran while one was open for 0% of the time, Pallas kernels for 1%

profile of v12, /device:TPU:8, one launch (start us, length us, event | category | flops | bytes accessed | tf_op | source)
XLA Modules:
  0.0 126.3 jit_solution(15462156974588201307)
XLA Ops:
  0.6 8.5 %all-to-all-start = ((bf16[4,8,4096]{2,1,0:T(8,128)(2,1)}), bf16[4,8,4096]{2,1,0:T(8,128)(2,1)S(1)}, u32[]{:S(2)}, u32[]{:S(2)}) async-start(bf16[4,8,4096]{2,1,0:T(8,128)(2,1)} %bitcast.10), calls=%async_computation | async-start | bytes 524288 | tf_op jit(solution)/shard_map/all_to_all | solution.py:267
  9.1 0.0 copy-start
  9.1 0.7 copy-done
  9.8 1.5 %places.1.place_ref = s32[32]{0:T(128)S(1)} custom-call(s32[1]{0:T(128)} %bitcast.1.shard_ref, s32[4,32]{1,0:T(4,128)S(1)} %copy-done), custom_call_target="tpu_custom_call" | custom-call | flops 1000 | bytes 1000 | tf_op jit(solution)/shard_map/places/pallas_call | solution.py:283
  11.3 8.6 %all-to-all-done.in_ref = bf16[4,8,4096]{2,1,0:T(8,128)(2,1)S(1)} async-done(((bf16[4,8,4096]{2,1,0:T(8,128)(2,1)}), bf16[4,8,4096]{2,1,0:T(8,128)(2,1)S(1)}, u32[]{:S(2)}, u32[]{:S(2)}) %all-to-all-start) | async-done | bytes 262176 | tf_op jit(solution)/shard_map/all_to_all | solution.py:267
  19.8 1.7 %route.1 = bf16[64,8,1024]{2,1,0:T(8,128)(2,1)} custom-call(s32[32]{0:T(128)S(1)} %places.1.place_ref, bf16[4,8,4096]{2,1,0:T(8,128)(2,1)S(1)} %all-to-all-done.in_ref), custom_call_target="tpu_custom_call" | custom-call | tf_op jit(solution)/shard_map/route/pallas_call | solution.py:294
  21.5 6.6 %all-to-all-start.1 = ((bf16[64,8,1024]{2,1,0:T(8,128)(2,1)}), bf16[64,8,1024]{2,1,0:T(8,128)(2,1)S(1)}, u32[]{:S(2)}, u32[]{:S(2)}) async-start(bf16[64,8,1024]{2,1,0:T(8,128)(2,1)} %route.1), calls=%async_computation.1 | async-start | bytes 2097152 | tf_op jit(solution)/shard_map/all_to_all | solution.py:267
  28.1 27.1 %all-to-all-done.1 = bf16[64,8,1024]{2,1,0:T(8,128)(2,1)S(1)} async-done(((bf16[64,8,1024]{2,1,0:T(8,128)(2,1)}), bf16[64,8,1024]{2,1,0:T(8,128)(2,1)S(1)}, u32[]{:S(2)}, u32[]{:S(2)}) %all-to-all-start.1) | async-done | bytes 1048608 | tf_op jit(solution)/shard_map/all_to_all | solution.py:267
  55.2 15.5 %owner.1 = (f32[2,512,512]{2,1,0:T(8,128)}, f32[2,512,512]{2,1,0:T(8,128)}, s16[64,8,1152]{2,1,0:T(8,128)(2,1)S(1)}) custom-call(s32[1]{0:T(128)} %bitcast.me_ref, s32[32]{0:T(128)S(1)} %places.1.place_ref, bf16[512,1024]{1,0:T(8,128)(2,1)S(1)} %bitcast.9, f32[2,512,512]{2,1,0:T(8,128)} %bitcast.12, f32[2,512,512]{2,1,0:T(8,128)} %bitcast.13), custom_call_target="tpu_custom_call" | custom-call | flops 13421772800 | bytes 12582912 | tf_op jit(solution)/shard_map/owner/pallas_call | solution.py:310
  70.8 37.4 %all_to_all.20.in_ref = s16[64,8,1152]{2,1,0:T(8,128)(2,1)S(1)} all-to-all(s16[64,8,1152]{2,1,0:T(8,128)(2,1)S(1)} %get-tuple-element.8), channel_id=1, replica_groups=mesh['g'=4,'r'=16,'mp'=4] {'r','g'}, dimensions={0} | all-to-all | bytes 2359296 | tf_op jit(solution)/shard_map/all_to_all | solution.py:267
  108.1 0.1 add.20
  108.2 1.5 %collect.1 = s16[4,8,4224]{2,1,0:T(8,128)(2,1)} custom-call(s32[32]{0:T(128)S(1)} %places.1.place_ref, s16[64,8,1152]{2,1,0:T(8,128)(2,1)S(1)} %all_to_all.20.in_ref), custom_call_target="tpu_custom_call" | custom-call | tf_op jit(solution)/shard_map/collect/pallas_call | solution.py:346
  109.7 4.8 %all-to-all-start.3 = ((s16[4,8,4224]{2,1,0:T(8,128)(2,1)}), s16[4,8,4224]{2,1,0:T(8,128)(2,1)S(1)}, u32[]{:S(2)}, u32[]{:S(2)}) async-start(s16[4,8,4224]{2,1,0:T(8,128)(2,1)} %collect.1), calls=%async_computation.3 | async-start | bytes 540672 | tf_op jit(solution)/shard_map/all_to_all | solution.py:267
  114.5 2.8 %collective-permute-start.2 = (f32[8,128]{1,0:T(8,128)S(1)}, f32[8,128]{1,0:T(8,128)S(1)}, u32[]{:S(2)}, u32[]{:S(2)}) collective-permute-start(f32[8,128]{1,0:T(8,128)S(1)} %add.20), channel_id=1, source_target_pairs={{0,3},{1,0},{2,1},{3,2},{4,7},{5,4},{6,5},{7,6},{8,11},{9,8},{10,9... | collective-permute-start | bytes 12296 | tf_op jit(solution)/shard_map/ppermute | solution.py:271
  117.3 0.8 collective-permute-start.1
  118.1 0.9 collective-permute-start
  119.0 0.0 collective-permute-done.2
  119.0 3.4 %collective-permute-done.1 = f32[8,128]{1,0:T(8,128)S(1)} collective-permute-done((f32[8,128]{1,0:T(8,128)S(1)}, f32[8,128]{1,0:T(8,128)S(1)}, u32[]{:S(2)}, u32[]{:S(2)}) %collective-permute-start.1) | collective-permute-done | bytes 4128 | tf_op jit(solution)/shard_map/ppermute | solution.py:271
  122.4 0.5 collective-permute-done
  122.9 2.4 %all-to-all-done.3.in_ref = s16[4,8,4224]{2,1,0:T(8,128)(2,1)S(1)} async-done(((s16[4,8,4224]{2,1,0:T(8,128)(2,1)}), s16[4,8,4224]{2,1,0:T(8,128)(2,1)S(1)}, u32[]{:S(2)}, u32[]{:S(2)}) %all-to-all-start.3) | async-done | bytes 270368 | tf_op jit(solution)/shard_map/all_to_all | solution.py:267
  125.3 1.0 finish.1
  (1 shorter events, 0.0 us)
Async XLA Ops:
  0.6 19.2 %all-to-all-start = ((bf16[4,8,4096]{2,1,0:T(8,128)(2,1)}), bf16[4,8,4096]{2,1,0:T(8,128)(2,1)S(1)}, u32[]{:S(2)}, u32[]{:S(2)}) async-start(bf16[4,8,4096]{2,1,0:T(8,128)(2,1)} %bitcast.10), calls=%async_computation | async-start | bytes 524288 | tf_op jit(solution)/shard_map/all_to_all | solution.py:267
  9.1 0.7 copy-start
  21.5 33.7 %all-to-all-start.1 = ((bf16[64,8,1024]{2,1,0:T(8,128)(2,1)}), bf16[64,8,1024]{2,1,0:T(8,128)(2,1)S(1)}, u32[]{:S(2)}, u32[]{:S(2)}) async-start(bf16[64,8,1024]{2,1,0:T(8,128)(2,1)} %route.1), calls=%async_computation.1 | async-start | bytes 2097152 | tf_op jit(solution)/shard_map/all_to_all | solution.py:267
  109.7 15.6 %all-to-all-start.3 = ((s16[4,8,4224]{2,1,0:T(8,128)(2,1)}), s16[4,8,4224]{2,1,0:T(8,128)(2,1)S(1)}, u32[]{:S(2)}, u32[]{:S(2)}) async-start(s16[4,8,4224]{2,1,0:T(8,128)(2,1)} %collect.1), calls=%async_computation.3 | async-start | bytes 540672 | tf_op jit(solution)/shard_map/all_to_all | solution.py:267
  114.5 4.5 %collective-permute-start.2 = (f32[8,128]{1,0:T(8,128)S(1)}, f32[8,128]{1,0:T(8,128)S(1)}, u32[]{:S(2)}, u32[]{:S(2)}) collective-permute-start(f32[8,128]{1,0:T(8,128)S(1)} %add.20), channel_id=1, source_target_pairs={{0,3},{1,0},{2,1},{3,2},{4,7},{5,4},{6,5},{7,6},{8,11},{9,8},{10,9... | collective-permute-start | bytes 12296 | tf_op jit(solution)/shard_map/ppermute | solution.py:271
  117.3 5.1 %collective-permute-start.1 = (f32[8,128]{1,0:T(8,128)S(1)}, f32[8,128]{1,0:T(8,128)S(1)}, u32[]{:S(2)}, u32[]{:S(2)}) collective-permute-start(f32[8,128]{1,0:T(8,128)S(1)} %add.20), channel_id=1, source_target_pairs={{0,2},{1,3},{2,0},{3,1},{4,6},{5,7},{6,4},{7,5},{8,10},{9,11},{10,... | collective-permute-start | bytes 12296 | tf_op jit(solution)/shard_map/ppermute | solution.py:271
  118.1 4.8 %collective-permute-start = (f32[8,128]{1,0:T(8,128)S(1)}, f32[8,128]{1,0:T(8,128)S(1)}, u32[]{:S(2)}, u32[]{:S(2)}) collective-permute-start(f32[8,128]{1,0:T(8,128)S(1)} %add.20), channel_id=1, source_target_pairs={{0,1},{1,2},{2,3},{3,0},{4,5},{5,6},{6,7},{7,4},{8,9},{9,10},{10,1... | collective-permute-start | bytes 12296 | tf_op jit(solution)/shard_map/ppermute | solution.py:271

commit v13 on v11

--- a/solution.py
+++ b/solution.py
@@ -61,19 +61,21 @@
         copy.wait()
 
 
-def collect_kernel(place_ref, in_ref, out_ref, sums_ref):
+def collect_kernel(group_ref, place_ref, in_ref, *refs):
+    out_refs, sums_ref = refs[:GROUPS], refs[GROUPS]
     lane = lax.broadcasted_iota(jnp.int32, (LINES, 128), 1)
     line = lax.broadcasted_iota(jnp.int32, (LINES, 128), 0)
     tile = pl.ds(SLOTS * BLOCK, 128)
-    for row in range(GROUPS):
+    for shift, out_ref in enumerate(out_refs):
+        row = lax.rem(group_ref[0] + shift, GROUPS)
         powers = jnp.zeros((LINES, 128), jnp.int32)
         for j in range(PER_SHARD):
             place = place_ref[row * PER_SHARD + j]
             position, slot = place // SLOTS, lax.rem(place, SLOTS)
             columns = pl.ds(pl.multiple_of(slot * BLOCK, BLOCK), BLOCK)
-            out_ref[row, :, pl.ds(j * BLOCK, BLOCK)] = in_ref[position, :, columns]
+            out_ref[:, pl.ds(j * BLOCK, BLOCK)] = in_ref[position, :, columns]
             powers = jnp.where(lane == j + 64 * slot, in_ref[position, :, tile].astype(jnp.int32), powers)
-        out_ref[row, :, pl.ds(PER_SHARD * BLOCK, 128)] = powers.astype(jnp.int16)
+        out_ref[:, pl.ds(PER_SHARD * BLOCK, 128)] = powers.astype(jnp.int16)
     sums = jnp.zeros((LINES, 128), jnp.float32)
     for first in range(0, OWNERS, LINES):
         digits = jnp.zeros((LINES, 128), jnp.int32)
@@ -86,17 +88,19 @@
     sums_ref[...] = sums
 
 
-def finish_kernel(sums_ref, in_ref, out_ref):
+def finish_kernel(group_ref, sums_ref, *refs):
+    in_refs, out_ref = refs[:GROUPS], refs[GROUPS]
     totals = jnp.sum(sums_ref[...], axis=0, keepdims=True)
     grad_total = totals[:, GRAD_LANE : GRAD_LANE + 1]
     update_total = totals[:, UPDATE_LANE : UPDATE_LANE + 1]
     graft = jnp.sqrt(grad_total / CELLS) * lax.rsqrt(update_total / CELLS + 1e-06)
-    for chunk in range(GROUPS):
-        powers = in_ref[chunk, :, pl.ds(PER_SHARD * BLOCK, 128)].astype(jnp.int32).astype(jnp.float32)
+    for shift, in_ref in enumerate(in_refs):
+        chunk = lax.rem(group_ref[0] + GROUPS - shift, GROUPS)
+        powers = in_ref[:, pl.ds(PER_SHARD * BLOCK, 128)].astype(jnp.int32).astype(jnp.float32)
         steps = jnp.exp2(powers + pltpu.roll(powers, 64, 1)) * graft
         for j in range(PER_SHARD):
             columns = pl.ds(j * BLOCK, BLOCK)
-            coded = in_ref[chunk, :, columns].astype(jnp.int32).astype(jnp.float32)
+            coded = in_ref[:, columns].astype(jnp.int32).astype(jnp.float32)
             out_ref[chunk, :, columns] = (coded * steps[:, j : j + 1]).astype(jnp.bfloat16)
 
 
@@ -329,26 +333,26 @@
     )(me, places, got, prev_left[0, 0], prev_right[0, 0])
 
     returned = exchange(coded, ("r", "g"))
-    back, sums = pl.pallas_call(
+    group = jnp.reshape(lax.axis_index("g"), (1,)).astype(jnp.int32)
+    *back, sums = pl.pallas_call(
         collect_kernel,
-        out_shape=[
-            jax.ShapeDtypeStruct((GROUPS, LINES, PER_SHARD * BLOCK + 128), jnp.int16),
-            jax.ShapeDtypeStruct((LINES, 128), jnp.float32),
-        ],
-        in_specs=[SMEM, WHOLE],
-        out_specs=[WHOLE, WHOLE],
+        out_shape=[jax.ShapeDtypeStruct((LINES, PER_SHARD * BLOCK + 128), jnp.int16)] * GROUPS
+        + [jax.ShapeDtypeStruct((LINES, 128), jnp.float32)],
+        in_specs=[SMEM, SMEM, WHOLE],
+        out_specs=[WHOLE] * (GROUPS + 1),
         compiler_params=params(8),
         name="collect",
-    )(places, returned)
-    back = exchange(back, "g")
+    )(group, places, returned)
+    for shift in range(1, GROUPS):
+        back[shift] = lax.ppermute(back[shift], "g", [(d, (d + shift) % GROUPS) for d in range(GROUPS)])
     update_out = pl.pallas_call(
         finish_kernel,
         out_shape=jax.ShapeDtypeStruct(spread_shape, jnp.bfloat16),
-        in_specs=[WHOLE, WHOLE],
+        in_specs=[SMEM] + [WHOLE] * (GROUPS + 1),
         out_specs=WHOLE,
         compiler_params=params(8),
         name="finish",
-    )(sum_mp(sums), back).reshape(gradient.shape)
+    )(group, sum_mp(sums), *back).reshape(gradient.shape)
     return (update_out, new_left[None, None], new_right[None, None])
 
 

time: 129 us -> 129 us (level)
  starting transfers between devices: 24.4 us -> 26.9 us
    ppermute x0 -> x3, starting transfers between devices: none -> 7.23 us  [shards(): lax.ppermute(back[shift], 'g', [(d, (d + shift) % GROUPS) for d in range(...]
    ppermute x0 -> x3, waiting for transfers between devices: none -> 5.15 us  [shards(): lax.ppermute(back[shift], 'g', [(d, (d + shift) % GROUPS) for d in range(...]
    all_to_all x3 -> x2, starting transfers between devices: 19.9 us -> 15.1 us  [exchange(): return lax.all_to_all(x, axes, split_axis=0, concat_axis=0, tiled=True)]
    ppermute x3, waiting for transfers between devices: 3.93 us -> 0.01 us  [add_permuted(): return sum([lax.ppermute(x, axis, perm) for perm in perms], x)]
    all_to_all x3 -> x2, waiting for transfers between devices: 38 us -> 35.6 us  [exchange(): return lax.all_to_all(x, axes, split_axis=0, concat_axis=0, tiled=True)]
  transfers between devices with their start and end apart: 6 -> 8, of which waited for: 5 -> 5; matrix products, arithmetic and copies ran while one was open for 0% -> 0% of each run, Pallas kernels for 1% -> 1%
where the time goes in v13:
time: 129 us; the launch traced here: 127 us
  waiting for transfers between devices  40.8 us (32%)
  blocking collectives  37.4 us (29%)
  starting transfers between devices  26.9 us (21%)
  Pallas kernels  20.5 us (16%)
    all_to_all x1, blocking collectives, exchange(): return lax.all_to_all(x, axes, split_axis=0, concat_axis=0, tiled=True)  37.4 us
    all_to_all x2, waiting for transfers between devices, exchange(): return lax.all_to_all(x, axes, split_axis=0, concat_axis=0, tiled=True)  35.6 us
    pallas_call x1, Pallas kernels, shards(): pl.pallas_call(owner_kernel, out_shape=[stat_shape, stat_shape, jax.Shape...  15.5 us
    all_to_all x2, starting transfers between devices, exchange(): return lax.all_to_all(x, axes, split_axis=0, concat_axis=0, tiled=True)  15.1 us
    ppermute x3, starting transfers between devices, shards(): lax.ppermute(back[shift], 'g', [(d, (d + shift) % GROUPS) for d in range(...  7.23 us
    ppermute x3, waiting for transfers between devices, shards(): lax.ppermute(back[shift], 'g', [(d, (d + shift) % GROUPS) for d in range(...  5.15 us
    ppermute x3, starting transfers between devices, add_permuted(): return sum([lax.ppermute(x, axis, perm) for perm in perms], x)  4.54 us
  transfers between devices with their start and end apart: 8, of which 5 were waited for; matrix products, arithmetic and copies ran while one was open for 0% of the time, Pallas kernels for 1%

profile of v13, /device:TPU:8, one launch (start us, length us, event | category | flops | bytes accessed | tf_op | source)
XLA Modules:
  0.0 126.9 jit_solution(1306009965485411084)
XLA Ops:
  0.6 8.5 %all-to-all-start = ((bf16[4,8,4096]{2,1,0:T(8,128)(2,1)}), bf16[4,8,4096]{2,1,0:T(8,128)(2,1)S(1)}, u32[]{:S(2)}, u32[]{:S(2)}) async-start(bf16[4,8,4096]{2,1,0:T(8,128)(2,1)} %bitcast.12), calls=%async_computation | async-start | bytes 524288 | tf_op jit(solution)/shard_map/all_to_all | solution.py:266
  9.1 0.0 copy-start
  9.1 0.7 copy-done
  9.8 1.5 %places.1.place_ref = s32[32]{0:T(128)S(1)} custom-call(s32[1]{0:T(128)} %bitcast.1.shard_ref, s32[4,32]{1,0:T(4,128)S(1)} %copy-done), custom_call_target="tpu_custom_call" | custom-call | flops 1000 | bytes 1000 | tf_op jit(solution)/shard_map/places/pallas_call | solution.py:282
  11.3 8.6 %all-to-all-done.in_ref = bf16[4,8,4096]{2,1,0:T(8,128)(2,1)S(1)} async-done(((bf16[4,8,4096]{2,1,0:T(8,128)(2,1)}), bf16[4,8,4096]{2,1,0:T(8,128)(2,1)S(1)}, u32[]{:S(2)}, u32[]{:S(2)}) %all-to-all-start) | async-done | bytes 262176 | tf_op jit(solution)/shard_map/all_to_all | solution.py:266
  19.8 1.7 %route.1 = bf16[64,8,1024]{2,1,0:T(8,128)(2,1)} custom-call(s32[32]{0:T(128)S(1)} %places.1.place_ref, bf16[4,8,4096]{2,1,0:T(8,128)(2,1)S(1)} %all-to-all-done.in_ref), custom_call_target="tpu_custom_call" | custom-call | tf_op jit(solution)/shard_map/route/pallas_call | solution.py:293
  21.5 6.6 %all-to-all-start.1 = ((bf16[64,8,1024]{2,1,0:T(8,128)(2,1)}), bf16[64,8,1024]{2,1,0:T(8,128)(2,1)S(1)}, u32[]{:S(2)}, u32[]{:S(2)}) async-start(bf16[64,8,1024]{2,1,0:T(8,128)(2,1)} %route.1), calls=%async_computation.1 | async-start | bytes 2097152 | tf_op jit(solution)/shard_map/all_to_all | solution.py:266
  28.1 27.1 %all-to-all-done.1 = bf16[64,8,1024]{2,1,0:T(8,128)(2,1)S(1)} async-done(((bf16[64,8,1024]{2,1,0:T(8,128)(2,1)}), bf16[64,8,1024]{2,1,0:T(8,128)(2,1)S(1)}, u32[]{:S(2)}, u32[]{:S(2)}) %all-to-all-start.1) | async-done | bytes 1048608 | tf_op jit(solution)/shard_map/all_to_all | solution.py:266
  55.2 15.5 %owner.1 = (f32[2,512,512]{2,1,0:T(8,128)}, f32[2,512,512]{2,1,0:T(8,128)}, s16[64,8,1152]{2,1,0:T(8,128)(2,1)S(1)}) custom-call(s32[1]{0:T(128)} %bitcast.2.me_ref, s32[32]{0:T(128)S(1)} %places.1.place_ref, bf16[512,1024]{1,0:T(8,128)(2,1)S(1)} %bitcast.10, f32[2,512,512]{2,1,0:T(8,128)} %bitcast.13, f32[2,512,512]{2,1,0:T(8,128)} %bitcast.14), custom_call_target="tpu_custom_call" | custom-call | flops 13421772800 | bytes 12582912 | tf_op jit(solution)/shard_map/owner/pallas_call | solution.py:309
  70.8 37.4 %all_to_all.15.in_ref = s16[64,8,1152]{2,1,0:T(8,128)(2,1)S(1)} all-to-all(s16[64,8,1152]{2,1,0:T(8,128)(2,1)S(1)} %get-tuple-element.11), channel_id=1, replica_groups=mesh['g'=4,'r'=16,'mp'=4] {'r','g'}, dimensions={0} | all-to-all | bytes 2359296 | tf_op jit(solution)/shard_map/all_to_all | solution.py:266
  108.1 0.8 collect.1
  108.9 2.9 %collective-permute-start.2 = (f32[8,128]{1,0:T(8,128)S(1)}, f32[8,128]{1,0:T(8,128)S(1)}, u32[]{:S(2)}, u32[]{:S(2)}) collective-permute-start(f32[8,128]{1,0:T(8,128)S(1)} %get-tuple-element.12), channel_id=1, source_target_pairs={{0,3},{1,0},{2,1},{3,2},{4,7},{5,4},{6,5},{7,6},{8,11},{9,8},{10,9... | collective-permute-start | bytes 12296 | tf_op jit(solution)/shard_map/ppermute | solution.py:270
  111.8 0.8 collective-permute-start.1
  112.6 0.9 collective-permute-start
  113.5 2.3 %collective-permute-start.3 = (s16[8,4224]{1,0:T(8,128)(2,1)S(1)}, s16[8,4224]{1,0:T(8,128)(2,1)S(1)}, u32[]{:S(2)}, u32[]{:S(2)}) collective-permute-start(s16[8,4224]{1,0:T(8,128)(2,1)S(1)} %get-tuple-element.14), channel_id=1, source_target_pairs={{0,64},{64,128},{128,192},{192,0},{1,65},{65,129},{129,193},{193,1... | collective-permute-start | bytes 202760 | tf_op jit(solution)/shard_map/ppermute | solution.py:347
  115.8 3.6 %collective-permute-start.4 = (s16[8,4224]{1,0:T(8,128)(2,1)S(1)}, s16[8,4224]{1,0:T(8,128)(2,1)S(1)}, u32[]{:S(2)}, u32[]{:S(2)}) collective-permute-start(s16[8,4224]{1,0:T(8,128)(2,1)S(1)} %get-tuple-element.15), channel_id=1, source_target_pairs={{0,128},{64,192},{128,0},{192,64},{1,129},{65,193},{129,1},{193,65... | collective-permute-start | bytes 202760 | tf_op jit(solution)/shard_map/ppermute | solution.py:347
  119.4 0.0 collective-permute-done.2
  119.4 1.3 %collective-permute-start.5 = (s16[8,4224]{1,0:T(8,128)(2,1)S(1)}, s16[8,4224]{1,0:T(8,128)(2,1)S(1)}, u32[]{:S(2)}, u32[]{:S(2)}) collective-permute-start(s16[8,4224]{1,0:T(8,128)(2,1)S(1)} %get-tuple-element.16), channel_id=1, source_target_pairs={{0,192},{64,0},{128,64},{192,128},{1,193},{65,1},{129,65},{193,129... | collective-permute-start | bytes 202760 | tf_op jit(solution)/shard_map/ppermute | solution.py:347
  120.7 0.0 collective-permute-done.1
  120.7 0.0 collective-permute-done
  120.7 0.1 collective-permute-done.3.refs_1_
  120.8 4.6 %collective-permute-done.4.refs_2_ = s16[8,4224]{1,0:T(8,128)(2,1)S(1)} collective-permute-done((s16[8,4224]{1,0:T(8,128)(2,1)S(1)}, s16[8,4224]{1,0:T(8,128)(2,1)S(1)}, u32[]{:S(2)}, u32[]{:S(2)}) %collective-permute-start.4) | collective-permute-done | bytes 67616 | tf_op jit(solution)/shard_map/ppermute | solution.py:347
  125.4 0.4 collective-permute-done.5.refs_3_
  125.9 1.0 finish.1
  (1 shorter events, 0.0 us)
Async XLA Ops:
  0.6 19.2 %all-to-all-start = ((bf16[4,8,4096]{2,1,0:T(8,128)(2,1)}), bf16[4,8,4096]{2,1,0:T(8,128)(2,1)S(1)}, u32[]{:S(2)}, u32[]{:S(2)}) async-start(bf16[4,8,4096]{2,1,0:T(8,128)(2,1)} %bitcast.12), calls=%async_computation | async-start | bytes 524288 | tf_op jit(solution)/shard_map/all_to_all | solution.py:266
  9.1 0.7 copy-start
  21.5 33.7 %all-to-all-start.1 = ((bf16[64,8,1024]{2,1,0:T(8,128)(2,1)}), bf16[64,8,1024]{2,1,0:T(8,128)(2,1)S(1)}, u32[]{:S(2)}, u32[]{:S(2)}) async-start(bf16[64,8,1024]{2,1,0:T(8,128)(2,1)} %route.1), calls=%async_computation.1 | async-start | bytes 2097152 | tf_op jit(solution)/shard_map/all_to_all | solution.py:266
  108.9 10.4 %collective-permute-start.2 = (f32[8,128]{1,0:T(8,128)S(1)}, f32[8,128]{1,0:T(8,128)S(1)}, u32[]{:S(2)}, u32[]{:S(2)}) collective-permute-start(f32[8,128]{1,0:T(8,128)S(1)} %get-tuple-element.12), channel_id=1, source_target_pairs={{0,3},{1,0},{2,1},{3,2},{4,7},{5,4},{6,5},{7,6},{8,11},{9,8},{10,9... | collective-permute-start | bytes 12296 | tf_op jit(solution)/shard_map/ppermute | solution.py:270
  111.8 8.9 %collective-permute-start.1 = (f32[8,128]{1,0:T(8,128)S(1)}, f32[8,128]{1,0:T(8,128)S(1)}, u32[]{:S(2)}, u32[]{:S(2)}) collective-permute-start(f32[8,128]{1,0:T(8,128)S(1)} %get-tuple-element.12), channel_id=1, source_target_pairs={{0,2},{1,3},{2,0},{3,1},{4,6},{5,7},{6,4},{7,5},{8,10},{9,11},{10,... | collective-permute-start | bytes 12296 | tf_op jit(solution)/shard_map/ppermute | solution.py:270
  112.6 8.1 %collective-permute-start = (f32[8,128]{1,0:T(8,128)S(1)}, f32[8,128]{1,0:T(8,128)S(1)}, u32[]{:S(2)}, u32[]{:S(2)}) collective-permute-start(f32[8,128]{1,0:T(8,128)S(1)} %get-tuple-element.12), channel_id=1, source_target_pairs={{0,1},{1,2},{2,3},{3,0},{4,5},{5,6},{6,7},{7,4},{8,9},{9,10},{10,1... | collective-permute-start | bytes 12296 | tf_op jit(solution)/shard_map/ppermute | solution.py:270
  113.5 7.4 %collective-permute-start.3 = (s16[8,4224]{1,0:T(8,128)(2,1)S(1)}, s16[8,4224]{1,0:T(8,128)(2,1)S(1)}, u32[]{:S(2)}, u32[]{:S(2)}) collective-permute-start(s16[8,4224]{1,0:T(8,128)(2,1)S(1)} %get-tuple-element.14), channel_id=1, source_target_pairs={{0,64},{64,128},{128,192},{192,0},{1,65},{65,129},{129,193},{193,1... | collective-permute-start | bytes 202760 | tf_op jit(solution)/shard_map/ppermute | solution.py:347
  115.8 9.7 %collective-permute-start.4 = (s16[8,4224]{1,0:T(8,128)(2,1)S(1)}, s16[8,4224]{1,0:T(8,128)(2,1)S(1)}, u32[]{:S(2)}, u32[]{:S(2)}) collective-permute-start(s16[8,4224]{1,0:T(8,128)(2,1)S(1)} %get-tuple-element.15), channel_id=1, source_target_pairs={{0,128},{64,192},{128,0},{192,64},{1,129},{65,193},{129,1},{193,65... | collective-permute-start | bytes 202760 | tf_op jit(solution)/shard_map/ppermute | solution.py:347
  119.4 6.5 %collective-permute-start.5 = (s16[8,4224]{1,0:T(8,128)(2,1)S(1)}, s16[8,4224]{1,0:T(8,128)(2,1)S(1)}, u32[]{:S(2)}, u32[]{:S(2)}) collective-permute-start(s16[8,4224]{1,0:T(8,128)(2,1)S(1)} %get-tuple-element.16), channel_id=1, source_target_pairs={{0,192},{64,0},{128,64},{192,128},{1,193},{65,1},{129,65},{193,129... | collective-permute-start | bytes 202760 | tf_op jit(solution)/shard_map/ppermute | solution.py:347
